TPU v7x, 32 devices: a whole 2x2x4 slice. The times are simulated.
32 devices in a mesh: fsdp: 2 (over x), ctx: 8 (over z, core), tensor: 2 (over y).
Axes of the slice: x: 2, y: 2, z: 4, core: 2. Of those that a mesh axis runs over, the one named last changes fastest.
Arguments:
- inputs: bfloat16 [2, 8, 1024, 768], P(None, 'fsdp', 'ctx'), may hold values from -6 to 6
- out_grad: bfloat16 [2, 8, 1024, 768], P(None, 'fsdp', 'ctx'), may hold values from -6 to 6
- lengths: int32 [2, 8], P(None, 'fsdp'), may hold values from 256 to 1024, as said below
- routes: int32 [2, 8, 1024], P(None, 'fsdp', 'ctx'), may hold values from 0 to 15
- slots: int32 [2, 8, 1024], P(None, 'fsdp', 'ctx'), may hold values from -1 to 24, as said below
- norm_gains: bfloat16 [2, 768], P(None, ('fsdp', 'ctx')), may hold values from 0.5 to 1.5
- router_matrix: bfloat16 [768, 16], P(('fsdp', 'ctx')), may hold values from -0.109375 to 0.109375
- input_projection: bfloat16 [2, 1536, 768], P(None, ('fsdp', 'ctx', 'tensor')), may hold values from -0.21875 to 0.21875
- inner_projection: bfloat16 [1536, 80], P(('fsdp', 'ctx', 'tensor')), may hold values from -0.15625 to 0.15625
- step_projection: bfloat16 [1536, 48], P(('fsdp', 'ctx', 'tensor')), may hold values from -1.5 to 1.5
- step_bias: bfloat16 [1536], P(('fsdp', 'ctx', 'tensor')), may hold values from -12 to 4
- channel_params: bfloat16 [1536, 22], P(('fsdp', 'ctx', 'tensor')), may hold values from -12 to 4
- output_projection: bfloat16 [1536, 768], P(('fsdp', 'ctx', 'tensor')), may hold values from -1.5 to 1.5
- expert_up: bfloat16 [16, 768, 3072], P(('fsdp', 'ctx'), None, 'tensor'), may hold values from -0.21875 to 0.21875
- expert_down: bfloat16 [16, 3072, 768], P(('fsdp', 'ctx'), 'tensor'), may hold values from -6 to 6
Outputs:
- activations: bfloat16 [2, 8, 1024, 768], P(None, 'fsdp', 'ctx')
- input_grad: float32 [2, 8, 1024, 768], P(None, 'fsdp', 'ctx')
- grad_norm_gains: float32 [2, 768], P(None, ('fsdp', 'ctx'))
- grad_router: float32 [768, 16], P(('fsdp', 'ctx'))
- grad_in_proj: float32 [2, 1536, 768], P(None, ('fsdp', 'ctx', 'tensor'))
- grad_x_proj: float32 [1536, 80], P(('fsdp', 'ctx', 'tensor'))
- grad_dt_proj: float32 [1536, 48], P(('fsdp', 'ctx', 'tensor'))
- grad_step_bias: float32 [1536], P(('fsdp', 'ctx', 'tensor'))
- grad_channel: float32 [1536, 22], P(('fsdp', 'ctx', 'tensor'))
- grad_out_proj: float32 [1536, 768], P(('fsdp', 'ctx', 'tensor'))
- grad_expert_up: float32 [16, 768, 3072], P(('fsdp', 'ctx'), None, 'tensor')
- grad_expert_down: float32 [16, 3072, 768], P(('fsdp', 'ctx'), 'tensor')
Inputs may be any that keep to these rules, and one draw needn't show every extreme that they name: `lengths`: in every micro-batch and every fsdp index, one of its 4 sequences has length 1024. Padded positions have -1. Among the tokens of one micro-batch on one fsdp index and one ctx index, kept tokens with the same route have distinct slots; in every micro-batch some expert gets all 25 slots from every such group.
All inputs are finite; a program needn't handle non-finite values.
Results may differ from a plain program's by a relative error of at most 0.017.
Values may be sent and summed in bfloat16 or wider, within the bound.
A program may use at most 256 MiB of HBM per device.

v0:
```python
import functools

import jax
import jax.numpy as jnp
from jax import lax
from jax.experimental import pallas as pl
from jax.experimental.pallas import tpu as pltpu
from jax.sharding import PartitionSpec as P

N = 16
CONV_TAPS = 4
R = 48
EPS = 1e-05
BLK = 8
LANES = 128
F32 = jnp.float32
BF16 = jnp.bfloat16
OWNERS = ("fsdp", "ctx")


def silu_parts(value):
    sig = jax.nn.sigmoid(value)
    return value * sig, sig * (1.0 + value * (1.0 - sig))


def swapped(value):
    return lax.ppermute(value, "tensor", [(0, 1), (1, 0)])


def tensor_total(value, dtype):
    sent = value.astype(dtype)
    if lax.axis_size("tensor") == 2:
        return sent.astype(F32) + swapped(sent).astype(F32)
    return jnp.sum(lax.all_gather(sent, "tensor").astype(F32), axis=0)


def tensor_share(value):
    peers, here = lax.axis_size("tensor"), lax.axis_index("tensor")
    share = value.shape[-1] // peers
    if peers == 2:
        own = jnp.where(here == 0, value[..., :share], value[..., share:])
        other = jnp.where(here == 0, value[..., share:], value[..., :share])
        return own + swapped(other.astype(BF16)).astype(F32)
    return lax.psum_scatter(value, "tensor", scatter_dimension=value.ndim - 1, tiled=True)


def tensor_columns(value):
    if lax.axis_size("tensor") == 2:
        other = swapped(value)
        first = lax.axis_index("tensor") == 0
        return jnp.concatenate(
            [jnp.where(first, value, other), jnp.where(first, other, value)], -1
        )
    return lax.all_gather(value, "tensor", axis=value.ndim - 1, tiled=True)


def moved(value, by):
    peers = lax.axis_size("ctx")
    pairs = [(i, i + by) for i in range(peers) if 0 <= i + by < peers]
    return lax.ppermute(value, "ctx", pairs)


def carried(state, log_decay, rates, sign):
    def both(parts):
        return jnp.concatenate([parts[0], parts[1][None]], 0)

    def apply(late_log, early):
        return jnp.exp(late_log[None] * rates[:, None, :]) * early

    got = moved(both((state, log_decay)), sign)
    excl = (got[:N], got[N])
    width = 1
    peers = lax.axis_size("ctx")
    while width < peers - 1:
        incl = (state + apply(log_decay, excl[0]), log_decay + excl[1])
        got = moved(both(incl), sign * (width + 1))
        excl = (excl[0] + apply(excl[1], got[:N]), excl[1] + got[N])
        width = 2 * width + 1
    return excl[0]


def spread_matrix():
    rows = lax.broadcasted_iota(jnp.int32, (2 * N, N * LANES), 0) % N
    cols = lax.broadcasted_iota(jnp.int32, (2 * N, N * LANES), 1) // LANES
    return (rows == cols).astype(F32).astype(BF16)


def spread_into(pairs, rows):
    def turn(i, _):
        matrix = spread_matrix()
        at = pl.ds(pl.multiple_of(i * LANES, LANES), LANES)
        for source, target in pairs:
            value = source[at, :]
            high = value.astype(BF16)
            low = (value - high.astype(F32)).astype(BF16)
            target[at, :] = jnp.dot(
                jnp.concatenate([high, low], 1), matrix, preferred_element_type=F32
            )
        return 0

    lax.fori_loop(0, rows // LANES, turn, 0)


def lanes(k):
    return slice(k * LANES, (k + 1) * LANES)


def end_state_kernel(d_ref, u_ref, b_ref, r_ref, end_ref, rb, bb):
    length, seqs, width = d_ref.shape
    parts = width // LANES
    for n in range(N):
        rb[n] = jnp.broadcast_to(r_ref[n : n + 1, :], (seqs, width))

    @pl.when(pl.program_id(0) == 0)
    def _():
        spread_into([(b_ref, bb)], length * seqs)

    def body(t, carry):
        hs, total = carry
        d = d_ref[t]
        du = d * u_ref[t]
        row = pl.ds(pl.multiple_of(t * seqs, seqs), seqs)
        new = []
        for n in range(N):
            bn = bb[row, lanes(n)]
            for k in range(parts):
                a = jnp.exp(d[:, lanes(k)] * rb[n, :, lanes(k)])
                new.append(a * hs[n * parts + k] + du[:, lanes(k)] * bn)
        return tuple(new), total + d

    zero = jnp.zeros((seqs, LANES), F32)
    hs, total = lax.fori_loop(
        0, length, body, ((zero,) * (N * parts), jnp.zeros((seqs, width), F32)), unroll=4
    )
    for n in range(N):
        for k in range(parts):
            end_ref[n, :, lanes(k)] = hs[n * parts + k]
    end_ref[N] = total


def forward_kernel(d_ref, u_ref, b_ref, c_ref, r_ref, h0_ref, y_ref, st_ref, rb, bb, cb):
    length, seqs, width = d_ref.shape
    parts = width // LANES
    for n in range(N):
        rb[n] = jnp.broadcast_to(r_ref[n : n + 1, :], (seqs, width))

    @pl.when(pl.program_id(0) == 0)
    def _():
        spread_into([(b_ref, bb), (c_ref, cb)], length * seqs)

    def block(i, hs):
        for n in range(N):
            for k in range(parts):
                st_ref[i, n, :, lanes(k)] = hs[n * parts + k]

        def body(step, hs):
            t = i * BLK + step
            d = d_ref[t]
            du = d * u_ref[t]
            row = pl.ds(pl.multiple_of(t * seqs, seqs), seqs)
            ys = [jnp.zeros((seqs, LANES), F32) for _ in range(parts)]
            new = []
            for n in range(N):
                bn = bb[row, lanes(n)]
                cn = cb[row, lanes(n)]
                for k in range(parts):
                    a = jnp.exp(d[:, lanes(k)] * rb[n, :, lanes(k)])
                    h = a * hs[n * parts + k] + du[:, lanes(k)] * bn
                    ys[k] = ys[k] + h * cn
                    new.append(h)
            for k in range(parts):
                y_ref[t, :, lanes(k)] = ys[k]
            return tuple(new)

        return lax.fori_loop(0, BLK, body, hs, unroll=4)

    lax.fori_loop(
        0,
        length // BLK,
        block,
        tuple(h0_ref[n, :, lanes(k)] for n in range(N) for k in range(parts)),
    )


def start_grad_kernel(d_ref, dy_ref, c_ref, r_ref, g_ref, rb, cb):
    length, seqs, width = d_ref.shape
    parts = width // LANES
    for n in range(N):
        rb[n] = jnp.broadcast_to(r_ref[n : n + 1, :], (seqs, width))

    @pl.when(pl.program_id(0) == 0)
    def _():
        spread_into([(c_ref, cb)], length * seqs)

    def body(i, gs):
        t = length - 1 - i
        d = d_ref[t]
        dy = dy_ref[t]
        row = pl.ds(pl.multiple_of(t * seqs, seqs), seqs)
        new = []
        for n in range(N):
            cn = cb[row, lanes(n)]
            for k in range(parts):
                a = jnp.exp(d[:, lanes(k)] * rb[n, :, lanes(k)])
                new.append(a * (gs[n * parts + k] + dy[:, lanes(k)] * cn))
        return tuple(new)

    zero = jnp.zeros((seqs, LANES), F32)
    gs = lax.fori_loop(0, length, body, (zero,) * (N * parts), unroll=4)
    for n in range(N):
        for k in range(parts):
            g_ref[n, :, lanes(k)] = gs[n * parts + k]


def backward_kernel(
    d_ref,
    u_ref,
    dy_ref,
    b_ref,
    c_ref,
    r_ref,
    st_ref,
    g0_ref,
    ds_ref,
    du_ref,
    db_ref,
    dc_ref,
    rg_ref,
    rb,
    bb,
    cb,
    hb,
    ab,
    pb,
    pc,
):
    length, seqs, width = d_ref.shape
    parts = width // LANES
    for n in range(N):
        rb[n] = jnp.broadcast_to(r_ref[n : n + 1, :], (seqs, width))

    @pl.when(pl.program_id(0) == 0)
    def _():
        spread_into([(b_ref, bb), (c_ref, cb)], length * seqs)
        db_ref[...] = jnp.zeros_like(db_ref)
        dc_ref[...] = jnp.zeros_like(dc_ref)

    rg_ref[...] = jnp.zeros_like(rg_ref)
    ones = jnp.ones((LANES, LANES), BF16)
    lane = lax.broadcasted_iota(jnp.int32, (N * seqs, length), 1)

    def block(turn, gs):
        i = length // BLK - 1 - turn

        def again(step, hs):
            t = i * BLK + step
            d = d_ref[t]
            du = d * u_ref[t]
            row = pl.ds(pl.multiple_of(t * seqs, seqs), seqs)
            new = []
            for n in range(N):
                bn = bb[row, lanes(n)]
                for k in range(parts):
                    a = jnp.exp(d[:, lanes(k)] * rb[n, :, lanes(k)])
                    h = a * hs[n * parts + k] + du[:, lanes(k)] * bn
                    ab[step, n, :, lanes(k)] = a
                    hb[step + 1, n, :, lanes(k)] = h
                    new.append(h)
            return tuple(new)

        hs = tuple(st_ref[i, n, :, lanes(k)] for n in range(N) for k in range(parts))
        for n in range(N):
            for k in range(parts):
                hb[0, n, :, lanes(k)] = hs[n * parts + k]
        lax.fori_loop(0, BLK, again, hs, unroll=4)

        def back(turn, gs):
            step = BLK - 1 - turn
            t = i * BLK + step
            row = pl.ds(pl.multiple_of(t * seqs, seqs), seqs)
            d = d_ref[t]
            u = u_ref[t]
            dy = dy_ref[t]
            du = d * u
            prods = [jnp.zeros((seqs, LANES), F32) for _ in range(parts)]
            steps = [jnp.zeros((seqs, LANES), F32) for _ in range(parts)]
            new = []
            for n in range(N):
                bn = bb[row, lanes(n)]
                cn = cb[row, lanes(n)]
                b_sum = c_sum = None
                for k in range(parts):
                    g = gs[n * parts + k] + cn * dy[:, lanes(k)]
                    c_term = hb[step + 1, n, :, lanes(k)] * dy[:, lanes(k)]
                    b_term = g * du[:, lanes(k)]
                    c_sum = c_term if k == 0 else c_sum + c_term
                    b_sum = b_term if k == 0 else b_sum + b_term
                    prods[k] = prods[k] + g * bn
                    carried_g = g * ab[step, n, :, lanes(k)]
                    decay_g = carried_g * hb[step, n, :, lanes(k)]
                    steps[k] = steps[k] + decay_g * rb[n, :, lanes(k)]
                    rg_ref[n, :, lanes(k)] = rg_ref[n, :, lanes(k)] + decay_g * d[:, lanes(k)]
                    new.append(carried_g)
                pb[step, n * seqs : (n + 1) * seqs, :] = b_sum
                pc[step, n * seqs : (n + 1) * seqs, :] = c_sum
            for k in range(parts):
                ds_ref[t, :, lanes(k)] = steps[k] + prods[k] * u[:, lanes(k)]
                du_ref[t, :, lanes(k)] = prods[k] * d[:, lanes(k)]
            return tuple(new)

        gs = lax.fori_loop(0, BLK, back, gs, unroll=2)
        b_new = jnp.zeros((N * seqs, length), F32)
        c_new = jnp.zeros((N * seqs, length), F32)
        for step in range(BLK):
            here = lane == i * BLK + step
            b_new = jnp.where(
                here, jnp.dot(pb[step].astype(BF16), ones, preferred_element_type=F32), b_new
            )
            c_new = jnp.where(
                here, jnp.dot(pc[step].astype(BF16), ones, preferred_element_type=F32), c_new
            )
        db_ref[...] += b_new
        dc_ref[...] += c_new
        return gs

    lax.fori_loop(
        0,
        length // BLK,
        block,
        tuple(g0_ref[n, :, lanes(k)] for n in range(N) for k in range(parts)),
    )


def scan_call(kernel, arrays, outs, scratch, width, chans):
    def spec(shape):
        if shape[-1] == chans:
            rank = len(shape)
            return pl.BlockSpec(
                (*shape[:-1], width), lambda j, rank=rank: (0,) * (rank - 1) + (j,)
            )
        return pl.BlockSpec(shape, lambda j, rank=len(shape): (0,) * rank)

    return pl.pallas_call(
        kernel,
        grid=(chans // width,),
        in_specs=[spec(a.shape) for a in arrays],
        out_specs=[spec(s) for s in outs],
        out_shape=[jax.ShapeDtypeStruct(s, F32) for s in outs],
        scratch_shapes=[pltpu.VMEM(s, F32) for s in scratch],
        compiler_params=pltpu.CompilerParams(vmem_limit_bytes=62 << 20),
    )(*arrays)


def per_device(
    inputs,
    out_grad,
    lengths,
    routes,
    slots,
    norm_gains,
    router_matrix,
    input_projection,
    inner_projection,
    step_projection,
    step_bias,
    channel_params,
    output_projection,
    expert_up,
    expert_down,
):
    micros, group, length, width = inputs.shape
    seqs = micros * group
    tokens = length * seqs
    owners = lax.axis_size("fsdp") * lax.axis_size("ctx")
    experts = router_matrix.shape[1]
    capacity = max(2, (25 * group * length + 32 * experts - 1) // (32 * experts))
    slots_each = micros * capacity
    rows = experts * slots_each

    def by_token(value):
        return jnp.moveaxis(value, 2, 0).reshape(tokens, *value.shape[3:])

    def by_sequence(value):
        return jnp.moveaxis(value.reshape(length, micros, group, value.shape[-1]), 0, 2)

    narrow = jnp.concatenate(
        [inner_projection, step_projection, channel_params, step_bias[:, None]], 1
    )
    x_cols = inner_projection.shape[1]
    cuts = [x_cols, x_cols + R, x_cols + R + channel_params.shape[1]]
    routing = jnp.concatenate([router_matrix, norm_gains.T], 1)
    joined = narrow.shape[0] == routing.shape[0]
    if joined:
        narrow = jnp.concatenate([narrow, routing], 1)
    narrow_cols = narrow.shape[1]
    pad = -narrow_cols % LANES
    wide = jnp.concatenate(
        [
            input_projection[0],
            input_projection[1],
            output_projection,
            jnp.pad(narrow, ((0, 0), (0, pad))),
        ],
        1,
    )
    full = lax.all_gather(wide, OWNERS, axis=0, tiled=True)
    w_in, w_gate, w_out = (full[:, i * width : (i + 1) * width] for i in range(3))
    tail = full[:, 3 * width :]
    w_x = tail[:, : cuts[0]]
    w_step = tail[:, cuts[0] : cuts[1]]
    channel_f = tail[:, cuts[1] : cuts[2]].astype(F32)
    bias_f = tail[:, cuts[2]].astype(F32)
    if joined:
        full_routing = tail[:, cuts[2] + 1 : cuts[2] + 1 + routing.shape[1]]
    else:
        full_routing = lax.all_gather(routing, OWNERS, axis=0, tiled=True)
    w_router = full_routing[:, :experts]
    gains = full_routing[:, experts:].T.astype(F32)
    chans = channel_f.shape[0]
    taps = channel_f[:, :CONV_TAPS].T
    conv_bias = channel_f[:, CONV_TAPS]
    skip = channel_f[:, CONV_TAPS + 1]
    rates = -jnp.exp(channel_f[:, CONV_TAPS + 2 :]).T

    position = lax.axis_index("ctx") * length + jnp.arange(length)
    valid = (position[:, None] < lengths.reshape(1, seqs)).astype(F32).reshape(tokens, 1)
    route = by_token(routes)
    slot = by_token(slots)
    kept = slot >= 0
    kept_f = kept.astype(F32)
    micro_of = (jnp.arange(tokens) // group) % micros
    place = jnp.where(kept, route * slots_each + micro_of * capacity + slot, -1)
    pick = (jnp.arange(rows)[:, None] == place[None, :]).astype(BF16)
    grad_tok = by_token(out_grad)
    grad_act = grad_tok.astype(F32) * valid

    def to_experts(value):
        return lax.all_to_all(
            value.reshape(experts, slots_each, value.shape[-1]),
            OWNERS,
            split_axis=0,
            concat_axis=0,
            tiled=True,
        ).reshape(rows, value.shape[-1])

    grad_rows_raw = to_experts(
        jnp.dot(pick, grad_tok, preferred_element_type=F32).astype(BF16)
    )

    x = by_token(inputs).astype(F32)
    scale1 = lax.rsqrt(jnp.mean(x * x, -1, keepdims=True) + EPS)
    xhat1 = x * scale1
    normed1 = (xhat1 * gains[0]).astype(BF16)
    nt = (((1,), (1,)), ((), ()))
    tn = (((0,), (0,)), ((), ()))

    def dot(a, b, dims=(((1,), (0,)), ((), ()))):
        return lax.dot_general(a, b, dims, preferred_element_type=F32)

    inner = dot(normed1, w_in, nt).astype(BF16)
    rim = (CONV_TAPS - 1) * seqs
    before = moved(inner[tokens - rim :], 1)
    gate_z = dot(normed1, w_gate, nt)
    extended = jnp.concatenate([before, inner], 0).astype(F32)
    conv = conv_bias
    for tap in range(CONV_TAPS):
        conv = conv + taps[tap] * extended[tap * seqs : tap * seqs + tokens]
    u_float, conv_slope = silu_parts(conv)
    u = u_float.astype(BF16)
    u_wide = u.astype(F32)
    proj = tensor_total(dot(u, w_x), F32)
    rank = proj[:, :R].astype(BF16)
    b_vals = proj[:, R : R + N]
    c_vals = proj[:, R + N :]
    step_pre = dot(rank, w_step, nt) + bias_f
    delta = jax.nn.softplus(step_pre)
    cube = (length, seqs, chans)
    delta3 = delta.reshape(cube)
    u3 = u_wide.reshape(cube)
    lane_width = 2 * LANES if chans % (2 * LANES) == 0 else LANES
    wide_rates = (N, seqs, lane_width)
    spread = (tokens, N * LANES)
    call = functools.partial(scan_call, width=lane_width, chans=chans)
    [end] = call(
        end_state_kernel,
        [delta3, u3, b_vals, rates],
        [(N + 1, seqs, chans)],
        [wide_rates, spread],
    )
    state_end, log_decay = end[:N], end[N]
    entry = carried(state_end, log_decay, rates, 1)
    y_scan, starts = call(
        forward_kernel,
        [delta3, u3, b_vals, c_vals, rates, entry],
        [cube, (length // BLK, N, seqs, chans)],
        [wide_rates, spread, spread],
    )
    y_vals = y_scan.reshape(tokens, chans) + skip * u_wide
    silu_z, gate_slope = silu_parts(gate_z)
    gated = (y_vals * silu_z).astype(BF16)
    resid = x + tensor_total(dot(gated, w_out), BF16)

    scale2 = lax.rsqrt(jnp.mean(resid * resid, -1, keepdims=True) + EPS)
    xhat2 = resid * scale2
    normed2 = (xhat2 * gains[1]).astype(BF16)
    probs = jax.nn.softmax(dot(normed2, w_router), -1)
    onehot = (route[:, None] == jnp.arange(experts)).astype(F32)
    gate = jnp.sum(probs * onehot, -1, keepdims=True) * kept_f[:, None]
    high = gate.astype(BF16)
    middle = (gate - high.astype(F32)).astype(BF16)
    low = (gate - high.astype(F32) - middle.astype(F32)).astype(BF16)
    sent = jnp.concatenate(
        [normed2, high, middle, low, jnp.zeros((tokens, LANES - 3), BF16)], 1
    )
    arrived = to_experts(dot(pick, sent).astype(BF16))
    x_rows = arrived[:, :width]
    pieces = arrived[:, width : width + 3].astype(F32)
    gate_rows = pieces[:, :1] + pieces[:, 1:2] + pieces[:, 2:3]
    grad_rows = (gate_rows * grad_rows_raw.astype(F32)).astype(BF16)
    up, down = expert_up[0], expert_down[0]
    hidden = dot(x_rows, up)
    act_float, gelu_pull = jax.vjp(lambda v: jax.nn.gelu(v, approximate=True), hidden)
    act = act_float.astype(BF16)
    part_y = dot(act, down)
    d_hidden = gelu_pull(dot(grad_rows, down, nt))[0].astype(BF16)
    part_x = dot(d_hidden, up, nt)
    returned = jnp.concatenate(
        [tensor_share(part_y).astype(BF16), tensor_share(part_x).astype(BF16)], 1
    )
    grad_up = dot(x_rows, d_hidden, tn)
    grad_down = dot(act, grad_rows, tn)
    back = to_experts(returned)
    share = returned.shape[1] // 2
    own = dot(pick, back, tn).astype(BF16)
    expert_y = tensor_columns(own[:, :share]).astype(F32)
    expert_dx = tensor_columns(own[:, share:]).astype(F32)
    activations = (valid * (resid + gate * expert_y)).astype(BF16)
    gate_grad = jnp.sum(grad_act * expert_y, -1, keepdims=True)
    d_logits = (gate_grad * gate * (onehot - probs)).astype(BF16)
    grad_router = dot(normed2, d_logits, tn)
    d_normed2 = expert_dx + dot(d_logits, w_router, nt)
    gain_grad2 = jnp.sum(d_normed2 * xhat2, 0)
    scaled2 = gains[1] * d_normed2
    d_resid = grad_act + scale2 * (scaled2 - xhat2 * jnp.mean(scaled2 * xhat2, -1, keepdims=True))

    d_mixed = d_resid.astype(BF16)
    d_gated = dot(d_mixed, w_out, nt)
    d_y = d_gated * silu_z
    dy3 = d_y.reshape(cube)
    [start_grad] = call(
        start_grad_kernel,
        [delta3, dy3, c_vals, rates],
        [(N, seqs, chans)],
        [wide_rates, spread],
    )
    grad_out = dot(gated, d_mixed, tn)
    d_gate_z = (d_gated * y_vals * gate_slope).astype(BF16)
    grad_end = carried(start_grad, log_decay, rates, -1)
    step_grad, u_grad, b_grad, c_grad, rate_grad = call(
        backward_kernel,
        [delta3, u3, dy3, b_vals, c_vals, rates, starts, grad_end],
        [cube, cube, (N * seqs, length), (N * seqs, length), (N, seqs, chans)],
        [
            wide_rates,
            spread,
            spread,
            (BLK + 1, N, seqs, lane_width),
            (BLK, N, seqs, lane_width),
            (BLK, N * seqs, LANES),
            (BLK, N * seqs, LANES),
        ],
    )

    def per_token(value):
        return jnp.transpose(value.reshape(N, seqs, length), (2, 1, 0)).reshape(tokens, N)

    d_step = (step_grad.reshape(tokens, chans) * jax.nn.sigmoid(step_pre)).astype(BF16)
    rank_grad = dot(d_step, w_step)
    d_proj = tensor_total(
        jnp.concatenate([rank_grad, per_token(b_grad), per_token(c_grad)], -1), BF16
    ).astype(BF16)
    grad_dt = dot(d_step, rank, tn)
    step_bias_grad = jnp.sum(d_step.astype(F32), 0)
    skip_grad = jnp.sum(d_y * u_wide, 0)
    grad_xproj = dot(u, d_proj, tn)
    d_u = d_y * skip + u_grad.reshape(tokens, chans) + dot(d_proj, w_x, nt)
    d_conv = d_u * conv_slope
    after = moved(d_conv[:rim], -1)
    conv_bias_grad = jnp.sum(d_conv, 0)
    tap_grads = [
        jnp.sum(d_conv * extended[tap * seqs : tap * seqs + tokens], 0) for tap in range(CONV_TAPS)
    ]
    extended_grad = jnp.concatenate([d_conv, after], 0)
    d_inner = jnp.zeros((tokens, chans), F32)
    for tap in range(CONV_TAPS):
        at = (CONV_TAPS - 1 - tap) * seqs
        d_inner = d_inner + taps[tap] * extended_grad[at : at + tokens]
    d_inner = d_inner.astype(BF16)
    d_normed1 = tensor_total(dot(d_inner, w_in) + dot(d_gate_z, w_gate), BF16)
    gain_grad1 = jnp.sum(d_normed1 * xhat1, 0)
    scaled1 = gains[0] * d_normed1
    input_grad = d_resid + scale1 * (
        scaled1 - xhat1 * jnp.mean(scaled1 * xhat1, -1, keepdims=True)
    )

    narrow_grads = jnp.concatenate(
        [
            grad_xproj,
            grad_dt,
            jnp.stack(tap_grads, 1),
            conv_bias_grad[:, None],
            skip_grad[:, None],
            (jnp.sum(rate_grad, 1) * rates).T,
            step_bias_grad[:, None],
        ],
        1,
    )
    routing_grads = jnp.concatenate([grad_router, gain_grad1[:, None], gain_grad2[:, None]], 1)
    if joined:
        narrow_grads = jnp.concatenate([narrow_grads, routing_grads], 1)
    wide_grads = jnp.concatenate(
        [
            dot(d_inner, normed1, tn),
            dot(d_gate_z, normed1, tn),
            grad_out,
            jnp.pad(narrow_grads, ((0, 0), (0, pad))),
        ],
        1,
    )

    def owned(value):
        return lax.psum_scatter(
            value.astype(BF16), OWNERS, scatter_dimension=0, tiled=True
        ).astype(F32)

    mine = owned(wide_grads)
    mine_tail = mine[:, 3 * width :]
    if joined:
        mine_routing = mine_tail[:, cuts[2] + 1 : cuts[2] + 1 + routing.shape[1]]
    else:
        mine_routing = owned(routing_grads)
    return (
        by_sequence(activations),
        by_sequence(input_grad),
        mine_routing[:, experts:].T,
        mine_routing[:, :experts],
        jnp.stack([mine[:, :width], mine[:, width : 2 * width]]),
        mine_tail[:, : cuts[0]],
        mine_tail[:, cuts[0] : cuts[1]],
        mine_tail[:, cuts[2]],
        mine_tail[:, cuts[1] : cuts[2]],
        mine[:, 2 * width : 3 * width],
        grad_up[None],
        grad_down[None],
    )


def solution(mesh):
    return jax.shard_map(
        per_device,
        mesh=mesh,
        in_specs=(
            P(None, "fsdp", "ctx", None),
            P(None, "fsdp", "ctx", None),
            P(None, "fsdp"),
            P(None, "fsdp", "ctx"),
            P(None, "fsdp", "ctx"),
            P(None, ("fsdp", "ctx")),
            P(("fsdp", "ctx"), None),
            P(None, ("fsdp", "ctx", "tensor"), None),
            P(("fsdp", "ctx", "tensor"), None),
            P(("fsdp", "ctx", "tensor"), None),
            P(("fsdp", "ctx", "tensor")),
            P(("fsdp", "ctx", "tensor"), None),
            P(("fsdp", "ctx", "tensor"), None),
            P(("fsdp", "ctx"), None, "tensor"),
            P(("fsdp", "ctx"), "tensor", None),
        ),
        out_specs=(
            P(None, "fsdp", "ctx", None),
            P(None, "fsdp", "ctx", None),
            P(None, ("fsdp", "ctx")),
            P(("fsdp", "ctx"), None),
            P(None, ("fsdp", "ctx", "tensor"), None),
            P(("fsdp", "ctx", "tensor"), None),
            P(("fsdp", "ctx", "tensor"), None),
            P(("fsdp", "ctx", "tensor")),
            P(("fsdp", "ctx", "tensor"), None),
            P(("fsdp", "ctx", "tensor"), None),
            P(("fsdp", "ctx"), None, "tensor"),
            P(("fsdp", "ctx"), "tensor", None),
        ),
        check_vma=False,
    )
```

profile of v0, /device:TPU:0, one launch (start us, length us, event | category | flops | bytes accessed | tf_op | source)
XLA Modules:
  0.0 761.8 jit_solution(14202419041575448493)
XLA Ops:
  16.3 3.7 copy.131
  23.2 42.3 %all-gather.2.cloned.1.call-done = bf16[768,2560]{1,0:T(8,128)(2,1)} async-done(((bf16[48,2560]{1,0:T(8,128)(2,1)}), bf16[768,2560]{1,0:T(8,128)(2,1)}) %all-gather.2.cloned.1.call-update) | async-done | bytes 3932176 | tf_op jit(solution)/shard_map/all_gather | solution.py:406
  68.5 3.3 convolution_convert_fusion.1
  75.0 3.7 convert_bitcast_fusion
  83.8 10.3 %collective-permute-done.1 = f32[1024,80]{1,0:T(8,128)S(1)} collective-permute-done((f32[1024,80]{1,0:T(8,128)S(1)}, f32[1024,80]{1,0:T(8,128)S(1)}, u32[]{:S(2)}, u32[]{:S(2)}) %collective-permute-start.1) | collective-permute-done | bytes 327712 | tf_op jit(solution)/shard_map/ppermute | solution.py:27
  97.1 3.5 fusion.23.d_ref
  100.6 16.3 %shard_map.238 = f32[17,8,768]{2,1,0:T(8,128)} custom-call(f32[128,8,768]{2,1,0:T(8,128)} %fusion.23.d_ref, f32[128,8,768]{2,1,0:T(8,128)} %get-tuple-element.113.u_ref, f32[1024,16]{1,0:T(8,128)} %get-tuple-element.132.b_ref, f32[16,768]{1,0:T(8,128)} %fusion.84.r_ref), custom_call_target="tpu_custom_call" | custom-call | tf_op jit(solution)/shard_map/pallas_call | solution.py:343
  123.3 10.3 %collective-permute-start.3 = (f32[17,8,768]{2,1,0:T(8,128)S(1)}, f32[17,8,768]{2,1,0:T(8,128)S(1)}, u32[]{:S(2)}, u32[]{:S(2)}) collective-permute-start(f32[17,8,768]{2,1,0:T(8,128)S(1)} %pad_maximum_fusion.2), channel_id=1, source_target_pairs={{0,4},{2,6},{4,8},{6,10},{8,12},{10,14},{1,5},{3,7},{5,9},{7,11},{... | collective-permute-start | bytes 1253384 | tf_op jit(solution)/shard_map/ppermute | solution.py:60
  133.6 7.3 collective-permute-done.3
  142.9 4.4 collective-permute-start.4
  147.2 6.0 collective-permute-done.4
  154.1 23.2 %shard_map.239 = (f32[128,8,768]{2,1,0:T(8,128)}, f32[16,16,8,768]{3,2,1,0:T(8,128)}) custom-call(f32[128,8,768]{2,1,0:T(8,128)} %fusion.23.d_ref, f32[128,8,768]{2,1,0:T(8,128)} %get-tuple-element.113.u_ref, f32[1024,16]{1,0:T(8,128)} %get-tuple-element.132.b_ref, f32[1024,16]{1,0:T(8,128)} %get-tuple-element.131.c_ref, f32[16,768]{1,0:T(8,128)} %fusion.84.r_ref, ...), custom_call_target="tpu_custom_call" | custom-call | tf_op jit(solution)/shard_map/pallas_call | solution.py:343
  177.4 6.1 multiply_convert_fusion.4
  183.5 4.4 convolution_convert_fusion
  191.1 29.7 %collective-permute-done.5 = bf16[1024,768]{1,0:T(8,128)(2,1)} collective-permute-done((bf16[1024,768]{1,0:T(8,128)(2,1)}, bf16[1024,768]{1,0:T(8,128)(2,1)}, u32[]{:S(2)}, u32[]{:S(2)}) %collective-permute-start.5) | collective-permute-done | bytes 1572896 | tf_op jit(solution)/shard_map/ppermute | solution.py:27
  229.0 3.5 concatenate.64
  232.6 3.6 fusion.41
  238.7 15.9 %all-to-all-start = ((bf16[16,50,896]{2,1,0:T(8,128)(2,1)}), bf16[16,50,896]{2,1,0:T(8,128)(2,1)S(1)}, u32[]{:S(2)}, u32[]{:S(2)}) async-start(bf16[16,50,896]{2,1,0:T(8,128)(2,1)} %reshape.309), calls=%async_computation | async-start | bytes 3211264 | tf_op jit(solution)/shard_map/all_to_all | solution.py:438
  254.7 3.8 copy.146
  258.4 3.8 reshape.311
  266.4 24.1 %all-to-all-done = bf16[16,50,896]{2,1,0:T(8,128)(2,1)S(1)} async-done(((bf16[16,50,896]{2,1,0:T(8,128)(2,1)}), bf16[16,50,896]{2,1,0:T(8,128)(2,1)S(1)}, u32[]{:S(2)}, u32[]{:S(2)}) %all-to-all-start) | async-done | bytes 1433632 | tf_op jit(solution)/shard_map/all_to_all | solution.py:438
  290.5 5.5 all-to-all-start.1
  299.3 28.0 %all-to-all-done.1 = bf16[16,50,768]{2,1,0:T(8,128)(2,1)S(1)} async-done(((bf16[16,50,768]{2,1,0:T(8,128)(2,1)}), bf16[16,50,768]{2,1,0:T(8,128)(2,1)S(1)}, u32[]{:S(2)}, u32[]{:S(2)}) %all-to-all-start.1) | async-done | bytes 1228832 | tf_op jit(solution)/shard_map/all_to_all | solution.py:438
  328.7 4.2 fusion.38
  336.1 4.6 fusion.7
  345.1 12.4 %collective-permute-done.6 = bf16[800,384]{1,0:T(8,128)(2,1)S(1)} collective-permute-done((bf16[800,384]{1,0:T(8,128)(2,1)S(1)}, bf16[800,384]{1,0:T(8,128)(2,1)S(1)}, u32[]{:S(2)}, u32[]{:S(2)}) %collective-permute-start.6) | collective-permute-done | bytes 614432 | tf_op jit(solution)/shard_map/ppermute | solution.py:27
  357.8 12.7 %collective-permute-done.7 = bf16[800,384]{1,0:T(8,128)(2,1)S(1)} collective-permute-done((bf16[800,384]{1,0:T(8,128)(2,1)S(1)}, bf16[800,384]{1,0:T(8,128)(2,1)S(1)}, u32[]{:S(2)}, u32[]{:S(2)}) %collective-permute-start.7) | collective-permute-done | bytes 614432 | tf_op jit(solution)/shard_map/ppermute | solution.py:27
  371.3 37.1 %all_to_all.15 = bf16[16,50,768]{2,1,0:T(8,128)(2,1)S(1)} all-to-all(bf16[16,50,768]{2,1,0:T(8,128)(2,1)S(1)} %reshape.313), channel_id=1, replica_groups=mesh['fsdp'=2,'ctx'=8,'tensor'=2] {'fsdp','ctx'}, dimensions={0} | all-to-all | bytes 2457600 | tf_op jit(solution)/shard_map/all_to_all | solution.py:438
  409.5 3.5 fusion.40
  414.7 18.7 %collective-permute-done.9 = bf16[1024,384]{1,0:T(8,128)(2,1)S(1)} collective-permute-done((bf16[1024,384]{1,0:T(8,128)(2,1)S(1)}, bf16[1024,384]{1,0:T(8,128)(2,1)S(1)}, u32[]{:S(2)}, u32[]{:S(2)}) %collective-permute-start.9) | collective-permute-done | bytes 786464 | tf_op jit(solution)/shard_map/ppermute | solution.py:27
  436.7 17.5 %collective-permute-done.8 = bf16[1024,384]{1,0:T(8,128)(2,1)S(1)} collective-permute-done((bf16[1024,384]{1,0:T(8,128)(2,1)S(1)}, bf16[1024,384]{1,0:T(8,128)(2,1)S(1)}, u32[]{:S(2)}, u32[]{:S(2)}) %collective-permute-start.8) | collective-permute-done | bytes 786464 | tf_op jit(solution)/shard_map/ppermute | solution.py:27
  470.3 5.5 fusion.22
  475.8 16.3 %shard_map.240 = f32[16,8,768]{2,1,0:T(8,128)} custom-call(f32[128,8,768]{2,1,0:T(8,128)} %fusion.23.d_ref, f32[128,8,768]{2,1,0:T(8,128)} %bitcast.121, f32[1024,16]{1,0:T(8,128)} %get-tuple-element.131.c_ref, f32[16,768]{1,0:T(8,128)} %fusion.84.r_ref), custom_call_target="tpu_custom_call" | custom-call | tf_op jit(solution)/shard_map/pallas_call | solution.py:343
  500.0 14.5 %collective-permute-done.11 = f32[17,8,768]{2,1,0:T(8,128)S(1)} collective-permute-done((f32[17,8,768]{2,1,0:T(8,128)S(1)}, f32[17,8,768]{2,1,0:T(8,128)S(1)}, u32[]{:S(2)}, u32[]{:S(2)}) %collective-permute-start.11) | collective-permute-done | bytes 417824 | tf_op jit(solution)/shard_map/ppermute | solution.py:60
  516.9 22.5 %collective-permute-done.12 = f32[17,8,768]{2,1,0:T(8,128)S(1)} collective-permute-done((f32[17,8,768]{2,1,0:T(8,128)S(1)}, f32[17,8,768]{2,1,0:T(8,128)S(1)}, u32[]{:S(2)}, u32[]{:S(2)}) %collective-permute-start.12) | collective-permute-done | bytes 417824 | tf_op jit(solution)/shard_map/ppermute | solution.py:60
  540.3 58.4 %shard_map.241 = (f32[128,8,768]{2,1,0:T(8,128)}, f32[128,8,768]{2,1,0:T(8,128)}, f32[128,128]{1,0:T(8,128)}, f32[128,128]{1,0:T(8,128)}, f32[16,8,768]{2,1,0:T(8,128)}) custom-call(f32[128,8,768]{2,1,0:T(8,128)} %fusion.23.d_ref, f32[128,8,768]{2,1,0:T(8,128)} %get-tuple-element.113.u_ref, f32[128,8,768]{2,1,0:T(8,128)} %bitcast.122, ...), custom_call_target="tpu_custom_call" | custom-call | tf_op jit(solution)/shard_map/pallas_call | solution.py:343
  598.7 3.7 fusion.98
  606.3 5.5 convolution_convert_fusion.2
  611.9 3.5 fusion.27
  642.4 18.8 %collective-permute-done.15 = bf16[1024,768]{1,0:T(8,128)(2,1)} collective-permute-done((bf16[1024,768]{1,0:T(8,128)(2,1)}, bf16[1024,768]{1,0:T(8,128)(2,1)}, u32[]{:S(2)}, u32[]{:S(2)}) %collective-permute-start.15) | collective-permute-done | bytes 1572896 | tf_op jit(solution)/shard_map/ppermute | solution.py:27
  664.8 4.7 concatenate.76
  669.5 3.5 fusion.8
  673.0 6.3 copy.162
  682.4 7.2 convolution_bitcast_fusion.1
  689.6 8.5 %convolution_bitcast_fusion = f32[1,1536,768]{2,1,0:T(8,128)} fusion(f32[800,768]{1,0:T(8,128)S(1)} %copy-done.27, f32[800]{0:T(1024)S(1)} %copy-done.53, f32[800,1536]{1,0:T(8,128)} %copy-done.67), kind=kOutput, calls=%fused_computation.21 | convolution fusion | flops 1899724800 | bytes 12094592 | tf_op jit(solution)/shard_map/dot_general | solution.py:458
  698.0 3.9 reshape.315
  704.9 4.9 multiply_add_fusion
  715.6 31.9 %reduce-scatter.4.cloned.1.call-done = bf16[48,2560]{1,0:T(8,128)(2,1)} async-done(((bf16[768,2560]{1,0:T(8,128)(2,1)}), bf16[48,2560]{1,0:T(8,128)(2,1)}) %reduce-scatter.4.cloned.1.call-update) | async-done | bytes 245776
  (316 shorter events, 152.9 us)
Async XLA Ops:
  7.2 8.8 %copy-start.23 = (bf16[2,4,128,768]{3,2,1,0:T(8,128)(2,1)S(1)}, bf16[2,4,128,768]{3,2,1,0:T(8,128)(2,1)}, u32[]{:S(2)}) copy-start(bf16[2,4,128,768]{3,2,1,0:T(8,128)(2,1)} %param.15) | copy-start | bytes 4718596
  7.2 58.3 %all-gather.2.cloned.1.call-start = ((), (), s32[]{:S(2)}) async-start(), calls=%async_computation.4 | async-start | bytes 4177920 | tf_op jit(solution)/shard_map/all_gather | solution.py:406
  16.0 52.1 %copy-start.40 = (f32[1024]{0:T(1024)}, f32[1024]{0:T(1024)S(1)}, u32[]{:S(2)}) copy-start(f32[1024]{0:T(1024)S(1)} %rsqrt.20) | copy-start | bytes 12292
  23.2 45.3 %copy-start.2 = (f32[1024,768]{1,0:T(8,128)}, f32[1024,768]{1,0:T(8,128)S(1)}, u32[]{:S(2)}) copy-start(f32[1024,768]{1,0:T(8,128)S(1)} %reshape.325) | copy-start | bytes 9437188
  66.6 16.6 %copy-start.35 = (f32[768,22]{0,1:T(8,128)}, f32[768,22]{0,1:T(8,128)S(1)}, u32[]{:S(2)}) copy-start(f32[768,22]{0,1:T(8,128)S(1)} %convert_element_type.279) | copy-start | bytes 202756
  66.6 110.8 %copy-start.59 = (f32[768]{0:T(1024)}, f32[768]{0:T(1024)S(1)}, u32[]{:S(2)}) copy-start(f32[768]{0:T(1024)S(1)} %get-tuple-element.97) | copy-start | bytes 9220
  71.8 3.0 collective-permute-start
  78.7 98.6 %copy-start.10 = (bf16[1024,768]{1,0:T(8,128)(2,1)}, bf16[1024,768]{1,0:T(8,128)(2,1)S(1)}, u32[]{:S(2)}) copy-start(bf16[1024,768]{1,0:T(8,128)(2,1)S(1)} %get-tuple-element.114) | copy-start | bytes 4718596
  80.5 13.6 %collective-permute-start.1 = (f32[1024,80]{1,0:T(8,128)S(1)}, f32[1024,80]{1,0:T(8,128)S(1)}, u32[]{:S(2)}, u32[]{:S(2)}) collective-permute-start(f32[1024,80]{1,0:T(8,128)S(1)} %fusion.78), channel_id=1, source_target_pairs={{0,1},{1,0},{2,3},{3,2},{4,5},{5,4},{6,7},{7,6},{8,9},{9,8},{10,11... | collective-permute-start | bytes 983048 | tf_op jit(solution)/shard_map/ppermute | solution.py:27
  83.2 13.9 %copy-start.50 = (f32[768]{0:T(1024)}, f32[768]{0:T(1024)S(1)}, u32[]{:S(2)}) copy-start(f32[768]{0:T(1024)S(1)} %convert_reduce_fusion) | copy-start | bytes 9220
  100.6 21.6 %copy-start.24 = (f32[16,768]{1,0:T(8,128)S(1)}, f32[16,768]{1,0:T(8,128)}, u32[]{:S(2)}) copy-start(f32[16,768]{1,0:T(8,128)} %fusion.84.r_ref) | copy-start | bytes 147460
  116.9 4.5 collective-permute-start.2
  123.3 17.6 %collective-permute-start.3 = (f32[17,8,768]{2,1,0:T(8,128)S(1)}, f32[17,8,768]{2,1,0:T(8,128)S(1)}, u32[]{:S(2)}, u32[]{:S(2)}) collective-permute-start(f32[17,8,768]{2,1,0:T(8,128)S(1)} %pad_maximum_fusion.2), channel_id=1, source_target_pairs={{0,4},{2,6},{4,8},{6,10},{8,12},{10,14},{1,5},{3,7},{5,9},{7,11},{... | collective-permute-start | bytes 1253384 | tf_op jit(solution)/shard_map/ppermute | solution.py:60
  142.9 10.3 %collective-permute-start.4 = (f32[17,8,768]{2,1,0:T(8,128)S(1)}, f32[17,8,768]{2,1,0:T(8,128)S(1)}, u32[]{:S(2)}, u32[]{:S(2)}) collective-permute-start(f32[17,8,768]{2,1,0:T(8,128)S(1)} %pad_maximum_fusion.3), channel_id=1, source_target_pairs={{0,8},{2,10},{4,12},{6,14},{1,9},{3,11},{5,13},{7,15},{16,24},{18,... | collective-permute-start | bytes 1253384 | tf_op jit(solution)/shard_map/ppermute | solution.py:60
  183.5 37.3 %copy-start.3 = (f32[1024,768]{1,0:T(8,128)S(1)}, f32[1024,768]{1,0:T(8,128)}, u32[]{:S(2)}) copy-start(f32[1024,768]{1,0:T(8,128)} %copy-done.2) | copy-start | bytes 9437188
  187.9 32.8 %collective-permute-start.5 = (bf16[1024,768]{1,0:T(8,128)(2,1)}, bf16[1024,768]{1,0:T(8,128)(2,1)}, u32[]{:S(2)}, u32[]{:S(2)}) collective-permute-start(bf16[1024,768]{1,0:T(8,128)(2,1)} %convolution_convert_fusion), channel_id=1, source_target_pairs={{0,1},{1,0},{2,3},{3,2},{4,5},{5,4},{6,7},{7,6},{8,9},{9,8},{10,11... | collective-permute-start | bytes 4718600 | tf_op jit(solution)/shard_map/ppermute | solution.py:27
  190.5 32.9 %copy-start.48 = (s32[1024]{0:T(1024)}, s32[1024]{0:T(1024)S(1)}, u32[]{:S(2)}) copy-start(s32[1024]{0:T(1024)S(1)} %reshape.308) | copy-start | bytes 12292
  223.7 8.9 %copy-start.8 = (bf16[1024,768]{1,0:T(8,128)(2,1)}, bf16[1024,768]{1,0:T(8,128)(2,1)S(1)}, u32[]{:S(2)}) copy-start(bf16[1024,768]{1,0:T(8,128)(2,1)S(1)} %multiply_convert_fusion.3) | copy-start | bytes 4718596
  238.7 51.8 %all-to-all-start = ((bf16[16,50,896]{2,1,0:T(8,128)(2,1)}), bf16[16,50,896]{2,1,0:T(8,128)(2,1)S(1)}, u32[]{:S(2)}, u32[]{:S(2)}) async-start(bf16[16,50,896]{2,1,0:T(8,128)(2,1)} %reshape.309), calls=%async_computation | async-start | bytes 3211264 | tf_op jit(solution)/shard_map/all_to_all | solution.py:438
  254.7 7.5 copy-start.61
  290.5 36.7 %all-to-all-start.1 = ((bf16[16,50,768]{2,1,0:T(8,128)(2,1)}), bf16[16,50,768]{2,1,0:T(8,128)(2,1)S(1)}, u32[]{:S(2)}, u32[]{:S(2)}) async-start(bf16[16,50,768]{2,1,0:T(8,128)(2,1)} %reshape.312), calls=%async_computation.1 | async-start | bytes 2752512 | tf_op jit(solution)/shard_map/all_to_all | solution.py:438
  296.0 451.5 %reduce-scatter.4.cloned.1.call-start = ((), (), s32[]{:S(2)}) async-start(), calls=%async_computation.5 | async-start | bytes 4177920
  299.2 33.8 %copy-start.52 = (f32[800]{0:T(1024)}, f32[800]{0:T(1024)S(1)}, u32[]{:S(2)}) copy-start(f32[800]{0:T(1024)S(1)} %fusion.62) | copy-start | bytes 9604
  340.8 16.8 %collective-permute-start.6 = (bf16[800,384]{1,0:T(8,128)(2,1)S(1)}, bf16[800,384]{1,0:T(8,128)(2,1)S(1)}, u32[]{:S(2)}, u32[]{:S(2)}) collective-permute-start(bf16[800,384]{1,0:T(8,128)(2,1)S(1)} %select_convert_fusion.1), channel_id=1, source_target_pairs={{0,1},{1,0},{2,3},{3,2},{4,5},{5,4},{6,7},{7,6},{8,9},{9,8},{10,11... | collective-permute-start | bytes 1843208 | tf_op jit(solution)/shard_map/ppermute | solution.py:27
  344.5 26.0 %collective-permute-start.7 = (bf16[800,384]{1,0:T(8,128)(2,1)S(1)}, bf16[800,384]{1,0:T(8,128)(2,1)S(1)}, u32[]{:S(2)}, u32[]{:S(2)}) collective-permute-start(bf16[800,384]{1,0:T(8,128)(2,1)S(1)} %select_convert_fusion), channel_id=1, source_target_pairs={{0,1},{1,0},{2,3},{3,2},{4,5},{5,4},{6,7},{7,6},{8,9},{9,8},{10,11... | collective-permute-start | bytes 1843208 | tf_op jit(solution)/shard_map/ppermute | solution.py:27
  413.1 23.2 %copy-start.62 = (s32[2,4]{1,0:T(2,128)S(1)}, s32[2,4]{1,0:T(2,128)}, u32[]{:S(2)}) copy-start(s32[2,4]{1,0:T(2,128)} %param.17) | copy-start | bytes 100
  413.2 20.3 %collective-permute-start.9 = (bf16[1024,384]{1,0:T(8,128)(2,1)S(1)}, bf16[1024,384]{1,0:T(8,128)(2,1)S(1)}, u32[]{:S(2)}, u32[]{:S(2)}) collective-permute-start(bf16[1024,384]{1,0:T(8,128)(2,1)S(1)} %slice.338), channel_id=1, source_target_pairs={{0,1},{1,0},{2,3},{3,2},{4,5},{5,4},{6,7},{7,6},{8,9},{9,8},{10,11... | collective-permute-start | bytes 2359304 | tf_op jit(solution)/shard_map/ppermute | solution.py:27
  434.8 19.4 %collective-permute-start.8 = (bf16[1024,384]{1,0:T(8,128)(2,1)S(1)}, bf16[1024,384]{1,0:T(8,128)(2,1)S(1)}, u32[]{:S(2)}, u32[]{:S(2)}) collective-permute-start(bf16[1024,384]{1,0:T(8,128)(2,1)S(1)} %get-tuple-element.124), channel_id=1, source_target_pairs={{0,1},{1,0},{2,3},{3,2},{4,5},{5,4},{6,7},{7,6},{8,9},{9,8},{10,11... | collective-permute-start | bytes 2359304 | tf_op jit(solution)/shard_map/ppermute | solution.py:27
  475.8 21.8 %copy-start.25 = (f32[16,768]{1,0:T(8,128)S(1)}, f32[16,768]{1,0:T(8,128)}, u32[]{:S(2)}) copy-start(f32[16,768]{1,0:T(8,128)} %fusion.84.r_ref) | copy-start | bytes 147460
  492.1 23.1 %copy-start.21 = (f32[16,8,768]{2,1,0:T(8,128)S(1)}, f32[16,8,768]{2,1,0:T(8,128)}, u32[]{:S(2)}) copy-start(f32[16,8,768]{2,1,0:T(8,128)} %shard_map.240) | copy-start | bytes 1179652
  493.2 3.7 collective-permute-start.10
  498.7 15.8 %collective-permute-start.11 = (f32[17,8,768]{2,1,0:T(8,128)S(1)}, f32[17,8,768]{2,1,0:T(8,128)S(1)}, u32[]{:S(2)}, u32[]{:S(2)}) collective-permute-start(f32[17,8,768]{2,1,0:T(8,128)S(1)} %pad_maximum_fusion.5), channel_id=1, source_target_pairs={{4,0},{6,2},{8,4},{10,6},{12,8},{14,10},{5,1},{7,3},{9,5},{11,7},{... | collective-permute-start | bytes 1253384 | tf_op jit(solution)/shard_map/ppermute | solution.py:60
  515.4 24.0 %collective-permute-start.12 = (f32[17,8,768]{2,1,0:T(8,128)S(1)}, f32[17,8,768]{2,1,0:T(8,128)S(1)}, u32[]{:S(2)}, u32[]{:S(2)}) collective-permute-start(f32[17,8,768]{2,1,0:T(8,128)S(1)} %pad_maximum_fusion.6), channel_id=1, source_target_pairs={{8,0},{10,2},{12,4},{14,6},{9,1},{11,3},{13,5},{15,7},{24,16},{26,... | collective-permute-start | bytes 1253384 | tf_op jit(solution)/shard_map/ppermute | solution.py:60
  540.3 58.4 %copy-start.51 = (f32[768]{0:T(1024)S(1)}, f32[768]{0:T(1024)}, u32[]{:S(2)}) copy-start(f32[768]{0:T(1024)} %copy-done.50) | copy-start | bytes 9220
  604.8 7.0 collective-permute-start.13
  615.4 3.2 collective-permute-start.14
  624.7 36.5 %collective-permute-start.15 = (bf16[1024,768]{1,0:T(8,128)(2,1)}, bf16[1024,768]{1,0:T(8,128)(2,1)}, u32[]{:S(2)}, u32[]{:S(2)}) collective-permute-start(bf16[1024,768]{1,0:T(8,128)(2,1)} %add_convert_fusion), channel_id=1, source_target_pairs={{0,1},{1,0},{2,3},{3,2},{4,5},{5,4},{6,7},{7,6},{8,9},{9,8},{10,11... | collective-permute-start | bytes 4718600 | tf_op jit(solution)/shard_map/ppermute | solution.py:27
  627.0 7.2 copy-start.12
  629.5 8.6 %copy-start.57 = (bf16[768]{0:T(1024)(128)(2,1)S(1)}, bf16[768]{0:T(1024)(128)(2,1)}, u32[]{:S(2)}) copy-start(bf16[768]{0:T(1024)(128)(2,1)} %get-tuple-element.88) | copy-start | bytes 4612
  629.5 9.2 %copy-start.56 = (bf16[768]{0:T(1024)(128)(2,1)S(1)}, bf16[768]{0:T(1024)(128)(2,1)}, u32[]{:S(2)}) copy-start(bf16[768]{0:T(1024)(128)(2,1)} %get-tuple-element.89) | copy-start | bytes 4612
  629.5 9.7 %copy-start.55 = (bf16[768]{0:T(1024)(128)(2,1)S(1)}, bf16[768]{0:T(1024)(128)(2,1)}, u32[]{:S(2)}) copy-start(bf16[768]{0:T(1024)(128)(2,1)} %get-tuple-element.94) | copy-start | bytes 4612
  631.2 8.6 %copy-start.29 = (bf16[1024,768]{1,0:T(8,128)(2,1)S(1)}, bf16[1024,768]{1,0:T(8,128)(2,1)}, u32[]{:S(2)}) copy-start(bf16[1024,768]{1,0:T(8,128)(2,1)} %copy-done.28) | copy-start | bytes 4718596
  631.2 8.6 %copy-start.32 = (bf16[1024,768]{1,0:T(8,128)(2,1)S(1)}, bf16[1024,768]{1,0:T(8,128)(2,1)}, u32[]{:S(2)}) copy-start(bf16[1024,768]{1,0:T(8,128)(2,1)} %copy-done.30) | copy-start | bytes 4718596
  639.9 21.3 %copy-start.4 = (f32[1024,768]{1,0:T(8,128)S(1)}, f32[1024,768]{1,0:T(8,128)}, u32[]{:S(2)}) copy-start(f32[1024,768]{1,0:T(8,128)} %copy-done.2) | copy-start | bytes 9437188
  639.9 21.3 %copy-start.39 = (f32[768]{0:T(1024)S(1)}, f32[768]{0:T(1024)}, u32[]{:S(2)}) copy-start(f32[768]{0:T(1024)} %copy-done.38) | copy-start | bytes 9220
  639.9 21.3 %copy-start.41 = (f32[1024]{0:T(1024)S(1)}, f32[1024]{0:T(1024)}, u32[]{:S(2)}) copy-start(f32[1024]{0:T(1024)} %copy-done.40) | copy-start | bytes 12292
  682.3 7.2 copy-start.27
  682.4 7.2 copy-start.53
  (43 other events, 173.8 us)
Sparse Core Ops, SparseCore 0:
  13.9 51.4 all-gather.1
  679.5 67.9 reduce-scatter.3
where the time goes:
time: 773 us; the launch traced here: 762 us
  waiting for transfers between devices  302 us (39%)
  Pallas kernels  114 us (15%)
  matrix products  91.2 us (12%)
  local copies, waits for them, and re-layouts  85.4 us (11%)
  other arithmetic  58.6 us (8%)
  starting transfers between devices  57.8 us (7%)
  blocking collectives  37.1 us (5%)
  between operations  15.8 us (2%)
    ppermute x8, waiting for transfers between devices, swapped(): return lax.ppermute(value, 'tensor', [(0, 1), (1, 0)])  120 us
    pallas_call x4, Pallas kernels, scan_call(): pl.pallas_call(kernel, grid=(chans // width,), in_specs=[spec(a.shape) fo...  114 us
    dot_general x26, matrix products, dot(): return lax.dot_general(a, b, dims, preferred_element_type=F32)  88.3 us
    ppermute x8, waiting for transfers between devices, moved(): return lax.ppermute(value, 'ctx', pairs)  55.2 us
    all_to_all x2, waiting for transfers between devices, to_experts(): lax.all_to_all(value.reshape(experts, slots_each, value.shape[-1]), OWNER...  52.1 us
    all_gather x1, waiting for transfers between devices, per_device(): full = lax.all_gather(wide, OWNERS, axis=0, tiled=True)  42.3 us
    all_to_all x1, blocking collectives, to_experts(): lax.all_to_all(value.reshape(experts, slots_each, value.shape[-1]), OWNER...  37.1 us
    unnamed x3, waiting for transfers between devices  31.9 us
  transfers between devices with their start and end apart: 20, of which 19 were waited for; matrix products, arithmetic and copies ran while one was open for 12% of the time, Pallas kernels for 0%

commit v1 on v0

v1 whole, which is shorter than its diff:
```python
import functools

import jax
import jax.numpy as jnp
from jax import lax
from jax.experimental import pallas as pl
from jax.experimental.pallas import tpu as pltpu
from jax.sharding import PartitionSpec as P

N = 16
CONV_TAPS = 4
R = 48
EPS = 1e-05
BLK = 8
LANES = 128
F32 = jnp.float32
BF16 = jnp.bfloat16
OWNERS = ("fsdp", "ctx")


def silu_parts(value):
    sig = jax.nn.sigmoid(value)
    return value * sig, sig * (1.0 + value * (1.0 - sig))


def swapped(value):
    return lax.ppermute(value, "tensor", [(0, 1), (1, 0)])


def tensor_total(value, dtype):
    sent = value.astype(dtype)
    if lax.axis_size("tensor") == 2:
        return sent.astype(F32) + swapped(sent).astype(F32)
    return jnp.sum(lax.all_gather(sent, "tensor").astype(F32), axis=0)


def tensor_share(value):
    peers, here = lax.axis_size("tensor"), lax.axis_index("tensor")
    share = value.shape[-1] // peers
    if peers == 2:
        own = jnp.where(here == 0, value[..., :share], value[..., share:])
        other = jnp.where(here == 0, value[..., share:], value[..., :share])
        return own + swapped(other.astype(BF16)).astype(F32)
    return lax.psum_scatter(value, "tensor", scatter_dimension=value.ndim - 1, tiled=True)


def tensor_columns(value):
    if lax.axis_size("tensor") == 2:
        other = swapped(value)
        first = lax.axis_index("tensor") == 0
        return jnp.concatenate(
            [jnp.where(first, value, other), jnp.where(first, other, value)], -1
        )
    return lax.all_gather(value, "tensor", axis=value.ndim - 1, tiled=True)


def halved(value, beside=()):
    beside = list(beside)
    sizes = [lax.axis_size(axis) for axis in OWNERS]
    bits = [(axis, 1 << k) for axis, size in zip(OWNERS, sizes) for k in reversed(range(size.bit_length() - 1))]
    rows = value.shape[0] >> len(bits)
    for place in reversed(range(len(bits))):
        axis, bit = bits[place]
        view = value.reshape(1 << place, 2, rows, value.shape[-1])
        high = (lax.axis_index(axis) & bit) != 0
        own = jnp.where(high, view[:, 1], view[:, 0])
        other = jnp.where(high, view[:, 0], view[:, 1]).astype(BF16)
        got = lax.ppermute(other, axis, [(i, i ^ bit) for i in range(lax.axis_size(axis))])
        value = own.astype(F32) + got.astype(F32)
        turn = len(bits) - 1 - place
        if turn < len(beside):
            value, beside[turn] = lax.optimization_barrier((value, beside[turn]))
    return value.reshape(rows, value.shape[-1]), beside


def moved(value, by):
    peers = lax.axis_size("ctx")
    pairs = [(i, i + by) for i in range(peers) if 0 <= i + by < peers]
    return lax.ppermute(value, "ctx", pairs)


def carried(state, log_decay, rates, sign):
    def sent(parts):
        high = parts[1].astype(BF16)
        low = (parts[1] - high.astype(F32)).astype(BF16)
        both = jnp.concatenate([parts[0].astype(BF16), high[None], low[None]], 0)
        got = moved(both, sign * (width + 1)).astype(F32)
        return got[:N], got[N] + got[N + 1]

    def apply(late_log, early):
        return jnp.exp(late_log[None] * rates[:, None, :]) * early

    width = 0
    excl = sent((state, log_decay))
    width = 1
    peers = lax.axis_size("ctx")
    while width < peers - 1:
        incl = (state + apply(log_decay, excl[0]), log_decay + excl[1])
        got = sent(incl)
        excl = (excl[0] + apply(excl[1], got[0]), excl[1] + got[1])
        width = 2 * width + 1
    return excl[0]


def spread_matrix():
    rows = lax.broadcasted_iota(jnp.int32, (2 * N, N * LANES), 0) % N
    cols = lax.broadcasted_iota(jnp.int32, (2 * N, N * LANES), 1) // LANES
    return (rows == cols).astype(F32).astype(BF16)


def spread_into(pairs, rows):
    def turn(i, _):
        matrix = spread_matrix()
        at = pl.ds(pl.multiple_of(i * LANES, LANES), LANES)
        for source, target in pairs:
            value = source[at, :]
            high = value.astype(BF16)
            low = (value - high.astype(F32)).astype(BF16)
            target[at, :] = jnp.dot(
                jnp.concatenate([high, low], 1), matrix, preferred_element_type=F32
            )
        return 0

    lax.fori_loop(0, rows // LANES, turn, 0)


def lanes(k):
    return slice(k * LANES, (k + 1) * LANES)


def end_state_kernel(d_ref, u_ref, b_ref, r_ref, end_ref, rb, bb):
    rows, width = d_ref.shape
    seqs = rb.shape[1]
    length = rows // seqs
    parts = width // LANES
    for n in range(N):
        rb[n] = jnp.broadcast_to(r_ref[n : n + 1, :], (seqs, width))

    @pl.when(pl.program_id(0) == 0)
    def _():
        spread_into([(b_ref, bb)], rows)

    def body(t, carry):
        hs, total = carry
        row = pl.ds(pl.multiple_of(t * seqs, seqs), seqs)
        d = d_ref[row, :]
        du = d * u_ref[row, :]
        new = []
        for n in range(N):
            bn = bb[row, lanes(n)]
            for k in range(parts):
                a = jnp.exp(d[:, lanes(k)] * rb[n, :, lanes(k)])
                new.append(a * hs[n * parts + k] + du[:, lanes(k)] * bn)
        return tuple(new), total + d

    zero = jnp.zeros((seqs, LANES), F32)
    hs, total = lax.fori_loop(
        0, length, body, ((zero,) * (N * parts), jnp.zeros((seqs, width), F32)), unroll=4
    )
    for n in range(N):
        for k in range(parts):
            end_ref[n, :, lanes(k)] = hs[n * parts + k]
    end_ref[N] = total


def forward_kernel(
    d_ref,
    u_ref,
    z_ref,
    b_ref,
    c_ref,
    r_ref,
    skip_ref,
    w_ref,
    h0_ref,
    y_ref,
    gated_ref,
    mixed_ref,
    st_ref,
    h1_ref,
    rb,
    bb,
    cb,
    total,
):
    rows, width = d_ref.shape
    seqs = rb.shape[1]
    length = rows // seqs
    parts = width // LANES
    for n in range(N):
        rb[n] = jnp.broadcast_to(r_ref[n : n + 1, :], (seqs, width))

    @pl.when(pl.program_id(0) == 0)
    def _():
        spread_into([(b_ref, bb), (c_ref, cb)], rows)
        total[...] = jnp.zeros_like(total)

    def block(i, hs):
        for n in range(N):
            for k in range(parts):
                st_ref[i, n, :, lanes(k)] = hs[n * parts + k]

        def body(step, hs):
            t = i * BLK + step
            row = pl.ds(pl.multiple_of(t * seqs, seqs), seqs)
            d = d_ref[row, :]
            u = u_ref[row, :]
            du = d * u
            ys = [u[:, lanes(k)] * skip_ref[:, lanes(k)] for k in range(parts)]
            new = []
            for n in range(N):
                bn = bb[row, lanes(n)]
                cn = cb[row, lanes(n)]
                for k in range(parts):
                    a = jnp.exp(d[:, lanes(k)] * rb[n, :, lanes(k)])
                    h = a * hs[n * parts + k] + du[:, lanes(k)] * bn
                    ys[k] = ys[k] + h * cn
                    new.append(h)
            for k in range(parts):
                y_ref[row, lanes(k)] = ys[k]
            return tuple(new)

        return lax.fori_loop(0, BLK, body, hs, unroll=4)

    hs = lax.fori_loop(
        0,
        length // BLK,
        block,
        tuple(h0_ref[n, :, lanes(k)] for n in range(N) for k in range(parts)),
    )
    for n in range(N):
        for k in range(parts):
            h1_ref[n, :, lanes(k)] = hs[n * parts + k]
    z = z_ref[...]
    gated = (y_ref[...] * (z * jax.nn.sigmoid(z))).astype(BF16)
    gated_ref[...] = gated
    total[...] += jnp.dot(gated, w_ref[...], preferred_element_type=F32)
    mixed_ref[...] = total[...].astype(BF16)


def start_grad_kernel(d_ref, dy_ref, c_ref, r_ref, g_ref, rb, cb):
    rows, width = d_ref.shape
    seqs = rb.shape[1]
    length = rows // seqs
    parts = width // LANES
    for n in range(N):
        rb[n] = jnp.broadcast_to(r_ref[n : n + 1, :], (seqs, width))

    @pl.when(pl.program_id(0) == 0)
    def _():
        spread_into([(c_ref, cb)], rows)

    def body(i, gs):
        t = length - 1 - i
        row = pl.ds(pl.multiple_of(t * seqs, seqs), seqs)
        d = d_ref[row, :]
        dy = dy_ref[row, :]
        new = []
        for n in range(N):
            cn = cb[row, lanes(n)]
            for k in range(parts):
                a = jnp.exp(d[:, lanes(k)] * rb[n, :, lanes(k)])
                new.append(a * (gs[n * parts + k] + dy[:, lanes(k)] * cn))
        return tuple(new)

    zero = jnp.zeros((seqs, LANES), F32)
    gs = lax.fori_loop(0, length, body, (zero,) * (N * parts), unroll=4)
    for n in range(N):
        for k in range(parts):
            g_ref[n, :, lanes(k)] = gs[n * parts + k]


def backward_kernel(
    d_ref,
    u_ref,
    dy_ref,
    sig_ref,
    b_ref,
    c_ref,
    r_ref,
    skip_ref,
    w_ref,
    st_ref,
    g0_ref,
    dstep_ref,
    du_ref,
    dproj_ref,
    rg_ref,
    bias_ref,
    skipg_ref,
    rb,
    bb,
    cb,
    hb,
    ab,
    pb,
    pc,
    dsb,
    total,
    columns,
):
    rows, width = d_ref.shape
    seqs = rb.shape[1]
    length = rows // seqs
    parts = width // LANES
    group = pl.program_id(0)
    for n in range(N):
        rb[n] = jnp.broadcast_to(r_ref[n : n + 1, :], (seqs, width))

    @pl.when(group == 0)
    def _():
        spread_into([(b_ref, bb), (c_ref, cb)], rows)
        total[...] = jnp.zeros_like(total)
        source = lax.broadcasted_iota(jnp.int32, columns.shape, 0) // LANES
        target = lax.broadcasted_iota(jnp.int32, columns.shape, 1)
        columns[...] = (source + R == target).astype(F32).astype(BF16)

    rg_ref[...] = jnp.zeros_like(rg_ref)
    bias_ref[...] = jnp.zeros_like(bias_ref)
    skipg_ref[...] = jnp.zeros_like(skipg_ref)

    def block(turn, gs):
        i = length // BLK - 1 - turn

        def again(step, hs):
            t = i * BLK + step
            row = pl.ds(pl.multiple_of(t * seqs, seqs), seqs)
            d = d_ref[row, :]
            du = d * u_ref[row, :]
            new = []
            for n in range(N):
                bn = bb[row, lanes(n)]
                for k in range(parts):
                    a = jnp.exp(d[:, lanes(k)] * rb[n, :, lanes(k)])
                    h = a * hs[n * parts + k] + du[:, lanes(k)] * bn
                    ab[step, n, :, lanes(k)] = a
                    hb[step + 1, n, :, lanes(k)] = h
                    new.append(h)
            return tuple(new)

        hs = tuple(st_ref[i, n, :, lanes(k)] for n in range(N) for k in range(parts))
        for n in range(N):
            for k in range(parts):
                hb[0, n, :, lanes(k)] = hs[n * parts + k]
        lax.fori_loop(0, BLK, again, hs, unroll=4)

        def back(turn, gs):
            step = BLK - 1 - turn
            t = i * BLK + step
            row = pl.ds(pl.multiple_of(t * seqs, seqs), seqs)
            here = pl.ds(pl.multiple_of(step * seqs, seqs), seqs)
            d = d_ref[row, :]
            u = u_ref[row, :]
            dy = dy_ref[row, :]
            du = d * u
            prods = [jnp.zeros((seqs, LANES), F32) for _ in range(parts)]
            steps = [jnp.zeros((seqs, LANES), F32) for _ in range(parts)]
            new = []
            for n in range(N):
                bn = bb[row, lanes(n)]
                cn = cb[row, lanes(n)]
                b_sum = c_sum = None
                for k in range(parts):
                    g = gs[n * parts + k] + cn * dy[:, lanes(k)]
                    c_term = hb[step + 1, n, :, lanes(k)] * dy[:, lanes(k)]
                    b_term = g * du[:, lanes(k)]
                    c_sum = c_term if k == 0 else c_sum + c_term
                    b_sum = b_term if k == 0 else b_sum + b_term
                    prods[k] = prods[k] + g * bn
                    carried_g = g * ab[step, n, :, lanes(k)]
                    decay_g = carried_g * hb[step, n, :, lanes(k)]
                    steps[k] = steps[k] + decay_g * rb[n, :, lanes(k)]
                    rg_ref[n, :, lanes(k)] = rg_ref[n, :, lanes(k)] + decay_g * d[:, lanes(k)]
                    new.append(carried_g)
                pb[here, lanes(n)] = b_sum
                pc[here, lanes(n)] = c_sum
            skipg_ref[...] += dy * u
            for k in range(parts):
                dsb[here, lanes(k)] = steps[k] + prods[k] * u[:, lanes(k)]
                du_ref[row, lanes(k)] = (
                    prods[k] * d[:, lanes(k)] + dy[:, lanes(k)] * skip_ref[:, lanes(k)]
                )
            return tuple(new)

        gs = lax.fori_loop(0, BLK, back, gs, unroll=2)
        at = pl.ds(pl.multiple_of(i * BLK * seqs, BLK * seqs), BLK * seqs)
        d_step = (dsb[...] * sig_ref[at, :]).astype(BF16)
        dstep_ref[at, :] = d_step
        bias_ref[...] += jnp.sum(d_step.astype(F32).reshape(BLK, seqs, width), 0)
        total[at, :] += (
            jnp.dot(d_step, w_ref[...], preferred_element_type=F32)
            + jnp.dot(pb[...].astype(BF16), columns[: N * LANES], preferred_element_type=F32)
            + jnp.dot(pc[...].astype(BF16), columns[N * LANES :], preferred_element_type=F32)
        )
        return gs

    lax.fori_loop(
        0,
        length // BLK,
        block,
        tuple(g0_ref[n, :, lanes(k)] for n in range(N) for k in range(parts)),
    )

    @pl.when(group == pl.num_programs(0) - 1)
    def _():
        dproj_ref[...] = total[...].astype(BF16)


TN = (((0,), (0,)), ((), ()))
NT = (((1,), (1,)), ((), ()))
NN = (((1,), (0,)), ((), ()))


def dot(a, b, dims=NN):
    return lax.dot_general(a, b, dims, preferred_element_type=F32)


def normalized(x):
    return x * lax.rsqrt(jnp.mean(x * x, -1, keepdims=True) + EPS)


def inner_grad_kernel(
    seqs,
    du_ref,
    dproj_ref,
    conv_ref,
    ext_ref,
    normed_ref,
    x_ref,
    u_ref,
    rank_ref,
    dstep_ref,
    dgate_ref,
    w_in_ref,
    w_gate_ref,
    w_x_ref,
    taps_ref,
    after_ref,
    late_ref,
    early_ref,
    gin_ref,
    gx_ref,
    gdt_ref,
    chan_ref,
    gain_ref,
    dconv,
):
    rows, chans = du_ref.shape
    rim = (CONV_TAPS - 1) * seqs
    turn = pl.program_id(0)
    first = pl.multiple_of((pl.num_programs(0) - 1 - turn) * rows, rows)

    @pl.when(turn == 0)
    def _():
        for ref in (gin_ref, gx_ref, gdt_ref, chan_ref, gain_ref):
            ref[...] = jnp.zeros_like(ref)
        dconv[rows:, :] = after_ref[...]

    @pl.when(turn > 0)
    def _():
        dconv[rows:, :] = dconv[:rim, :]

    def by_seq(value):
        return jnp.sum(value.reshape(rows // seqs, seqs, value.shape[-1]), 0)

    d_proj = dproj_ref[...]
    conv = conv_ref[...]
    sig = jax.nn.sigmoid(conv)
    d_conv = (du_ref[...] + dot(d_proj, w_x_ref[...], NT)) * (sig * (1.0 + conv * (1.0 - sig)))
    dconv[:rows, :] = d_conv
    d_inner = jnp.zeros_like(d_conv)
    for tap in range(CONV_TAPS):
        at = (CONV_TAPS - 1 - tap) * seqs
        d_inner = d_inner + taps_ref[tap : tap + 1, :] * dconv[at : at + rows, :]
        ext = ext_ref[pl.ds(pl.multiple_of(first + tap * seqs, seqs), rows), :]
        chan_ref[tap * seqs : (tap + 1) * seqs, :] += by_seq(d_conv * ext)
    chan_ref[CONV_TAPS * seqs :, :] += by_seq(d_conv)
    d_inner = d_inner.astype(BF16)
    part = dot(d_inner, w_in_ref[...]) + dot(dgate_ref[...], w_gate_ref[...])
    half = pl.num_programs(0) // 2

    @pl.when(turn < half)
    def _():
        late_ref[...] = part.astype(BF16)

    @pl.when(turn >= half)
    def _():
        early_ref[...] = part.astype(BF16)

    gain_ref[...] += by_seq(part * normalized(x_ref[...].astype(F32)))
    gin_ref[...] += dot(d_inner, normed_ref[...], TN)
    gx_ref[...] += dot(u_ref[...], d_proj, TN)
    gdt_ref[...] += dot(dstep_ref[...], rank_ref[...], TN)


def output_kernel(shape, peers, *refs):
    micros, group = shape
    early, late, refs = refs[:peers], refs[peers : 2 * peers], refs[2 * peers :]
    x_ref, dres_ref, act_in_ref, gain_ref, grad_ref, act_ref, grad_tok, act_tok = refs
    x = x_ref[...].astype(F32)
    scale = lax.rsqrt(jnp.mean(x * x, -1, keepdims=True) + EPS)
    xhat = x * scale
    is_early = pl.program_id(0) < pl.num_programs(0) // 2
    d_normed = jnp.zeros_like(x)
    for first, second in zip(early, late):
        d_normed = d_normed + jnp.where(is_early, first[...], second[...]).astype(F32)
    scaled = gain_ref[...] * d_normed
    mean = jnp.mean(scaled * xhat, -1, keepdims=True)
    grad = dres_ref[...].astype(F32) + scale * (scaled - xhat * mean)
    seqs = micros * group
    rows, width = x.shape
    count = rows // seqs
    act = act_in_ref[...].astype(F32)
    for k in range(width // LANES):
        grad_tok[k] = grad[:, lanes(k)]
        act_tok[k] = act[:, lanes(k)]
    for m in range(micros):
        for g in range(group):
            at = pl.ds(m * group + g, count, stride=seqs)
            for k in range(width // LANES):
                grad_ref[m, g, :, lanes(k)] = grad_tok[k, at, :]
                act_ref[m, g, :, lanes(k)] = act_tok[k, at, :].astype(BF16)


def scan_call(kernel, arrays, outs, scratch, width, chans, chunk=0, cost=None):
    def spec(shape, kind):
        def place(j, rank=len(shape)):
            at = [0] * rank
            if "t" in kind:
                at[0] = chunk
            if "c" in kind:
                at[-1] = j
            if "r" in kind:
                at[0] = j
            return tuple(at)

        return pl.BlockSpec(shape, place)

    return pl.pallas_call(
        kernel,
        grid=(chans // width,),
        in_specs=[spec(shape, kind) for _, shape, kind in arrays],
        out_specs=[spec(shape, kind) for _, shape, kind in outs],
        out_shape=[a for a, _, _ in outs],
        scratch_shapes=[
            s if not isinstance(s, tuple) else pltpu.VMEM(s, F32) for s in scratch
        ],
        compiler_params=pltpu.CompilerParams(vmem_limit_bytes=62 << 20),
        cost_estimate=cost,
    )(*[a for a, _, _ in arrays])


def per_device(
    inputs,
    out_grad,
    lengths,
    routes,
    slots,
    norm_gains,
    router_matrix,
    input_projection,
    inner_projection,
    step_projection,
    step_bias,
    channel_params,
    output_projection,
    expert_up,
    expert_down,
):
    micros, group, length, width = inputs.shape
    seqs = micros * group
    tokens = length * seqs
    owners = lax.axis_size("fsdp") * lax.axis_size("ctx")
    experts = router_matrix.shape[1]
    capacity = max(2, (25 * group * length + 32 * experts - 1) // (32 * experts))
    slots_each = micros * capacity
    rows = experts * slots_each

    def by_token(value):
        return jnp.moveaxis(value, 2, 0).reshape(tokens, *value.shape[3:])

    narrow = jnp.concatenate(
        [inner_projection, step_projection, channel_params, step_bias[:, None]], 1
    )
    x_cols = inner_projection.shape[1]
    cuts = [x_cols, x_cols + R, x_cols + R + channel_params.shape[1]]
    routing = jnp.concatenate([router_matrix, norm_gains.T], 1)
    joined = narrow.shape[0] == routing.shape[0]
    if joined:
        narrow = jnp.concatenate([narrow, routing], 1)
    narrow_cols = narrow.shape[1]
    pad = -narrow_cols % LANES
    first = jnp.concatenate([input_projection[0], jnp.pad(narrow, ((0, 0), (0, pad)))], 1)
    later = jnp.concatenate([input_projection[1], output_projection], 1)
    full = lax.all_gather(first, OWNERS, axis=0, tiled=True)
    later_full = lax.all_gather(later, OWNERS, axis=0, tiled=True)

    position = lax.axis_index("ctx") * length + jnp.arange(length)
    valid = (position[:, None] < lengths.reshape(1, seqs)).astype(F32).reshape(tokens, 1)
    route = by_token(routes)
    slot = by_token(slots)
    kept = slot >= 0
    kept_f = kept.astype(F32)
    micro_of = (jnp.arange(tokens) // group) % micros
    place = jnp.where(kept, route * slots_each + micro_of * capacity + slot, -1)
    pick = (
        jnp.arange(rows).reshape(experts, slots_each, 1) == place[None, None, :]
    ).astype(BF16)
    grad_tok = by_token(out_grad)
    grad_act = grad_tok.astype(F32) * valid

    def packed(value):
        return jnp.einsum("est,td->esd", pick, value, preferred_element_type=F32).astype(BF16)

    def unpacked(value):
        flat = value.reshape(rows, value.shape[-1])
        return lax.optimization_barrier(dot(pick.reshape(rows, tokens), flat, TN))

    def swap_owners(value):
        return lax.all_to_all(value, OWNERS, split_axis=0, concat_axis=0, tiled=True)

    grad_packed = packed(grad_tok)

    w_in = full[:, :width]
    tail = full[:, width:]
    w_gate, w_out = later_full[:, :width], later_full[:, width:]
    w_x = tail[:, : cuts[0]]
    w_step = tail[:, cuts[0] : cuts[1]]
    channel_f = tail[:, cuts[1] : cuts[2]].astype(F32)
    bias_f = tail[:, cuts[2]].astype(F32)
    if joined:
        full_routing = tail[:, cuts[2] + 1 : cuts[2] + 1 + routing.shape[1]]
    else:
        full_routing = lax.all_gather(routing, OWNERS, axis=0, tiled=True)
    w_router = full_routing[:, :experts]
    gains = full_routing[:, experts:].T.astype(F32)
    chans = channel_f.shape[0]
    taps = channel_f[:, :CONV_TAPS].T
    conv_bias = channel_f[:, CONV_TAPS]
    skip = channel_f[:, CONV_TAPS + 1]
    rates = -jnp.exp(channel_f[:, CONV_TAPS + 2 :]).T

    x_tok = lax.optimization_barrier(by_token(inputs))
    x = x_tok.astype(F32)
    normed1 = (normalized(x) * gains[0]).astype(BF16)
    inner = dot(normed1, w_in, NT).astype(BF16)
    rim = (CONV_TAPS - 1) * seqs
    before = moved(inner[tokens - rim :], 1)
    gate_z = dot(normed1, w_gate, NT)
    extended = jnp.concatenate([before, inner], 0).astype(F32)
    conv = conv_bias
    for tap in range(CONV_TAPS):
        conv = conv + taps[tap] * extended[tap * seqs : tap * seqs + tokens]
    u = jax.nn.silu(conv).astype(BF16)
    u_wide = u.astype(F32)
    proj = tensor_total(dot(u, w_x), BF16)
    rank = proj[:, :R].astype(BF16)
    b_vals = proj[:, R : R + N]
    c_vals = proj[:, R + N :]
    step_pre = dot(rank, w_step, NT) + bias_f
    delta = jax.nn.softplus(step_pre)
    lane_width = 2 * LANES if chans % (2 * LANES) == 0 else LANES
    wide_rates = (N, seqs, lane_width)
    state_block = (N, seqs, lane_width)
    call = functools.partial(scan_call, width=lane_width, chans=chans)

    def both_in(value, steps=length):
        return (value, (steps * seqs, lane_width), "tc")

    def by_chan(value):
        return (value, (*value.shape[:-1], lane_width), "c")

    def by_rows(value, steps=length):
        return (value, (steps * seqs, value.shape[1]), "t")

    def cost(steps, ops):
        elements = steps * seqs * chans * N
        return pl.CostEstimate(flops=300 * ops * elements, bytes_accessed=elements, transcendentals=0)

    def out(shape, dtype=F32):
        return jax.ShapeDtypeStruct(shape, dtype)

    [end] = call(
        end_state_kernel,
        [both_in(delta), both_in(u_wide), by_rows(b_vals), by_chan(rates)],
        [by_chan(out((N + 1, seqs, chans)))],
        [wide_rates, (tokens, N * LANES)],
        cost=cost(length, 6),
    )
    state_end, log_decay = end[:N], end[N]
    state = carried(state_end, log_decay, rates, 1)
    state, grad_packed = lax.optimization_barrier((state, grad_packed))
    grad_rows_raw = swap_owners(grad_packed)
    pieces = 4 if length % (4 * BLK) == 0 else 1
    steps = length // pieces
    y_parts, gated_parts, mixed_parts, start_parts = [], [], [], []
    for piece in range(pieces):
        if piece > 1:
            state, mixed_parts[piece - 2] = lax.optimization_barrier(
                (state, mixed_parts[piece - 2])
            )
        if piece == pieces - 1:
            state, grad_rows_raw = lax.optimization_barrier((state, grad_rows_raw))
        y_part, gated_part, mixed_part, start_part, state = call(
            forward_kernel,
            [
                both_in(delta, steps),
                both_in(u_wide, steps),
                (gate_z, (steps * seqs, lane_width), "tc"),
                by_rows(b_vals, steps),
                by_rows(c_vals, steps),
                by_chan(rates),
                by_chan(skip[None]),
                (w_out, (lane_width, width), "r"),
                by_chan(state),
            ],
            [
                by_chan(out((steps * seqs, chans))),
                by_chan(out((steps * seqs, chans), BF16)),
                (out((steps * seqs, width), BF16), (steps * seqs, width), ""),
                by_chan(out((steps // BLK, N, seqs, chans))),
                by_chan(out((N, seqs, chans))),
            ],
            [wide_rates, (steps * seqs, N * LANES), (steps * seqs, N * LANES), (steps * seqs, width)],
            chunk=piece,
            cost=cost(steps, 10),
        )
        y_parts.append(y_part)
        gated_parts.append(gated_part)
        mixed_parts.append(tensor_total(mixed_part, BF16))
        start_parts.append(start_part)
    y_vals = jnp.concatenate(y_parts, 0)
    gated = jnp.concatenate(gated_parts, 0)
    starts = jnp.concatenate(start_parts, 0)
    silu_z, gate_slope = silu_parts(gate_z)
    resid = x + jnp.concatenate(mixed_parts, 0)

    scale2 = lax.rsqrt(jnp.mean(resid * resid, -1, keepdims=True) + EPS)
    xhat2 = resid * scale2
    normed2 = (xhat2 * gains[1]).astype(BF16)
    probs = jax.nn.softmax(dot(normed2, w_router), -1)
    onehot = (route[:, None] == jnp.arange(experts)).astype(F32)
    gate = jnp.sum(probs * onehot, -1, keepdims=True) * kept_f[:, None]
    peers, here = lax.axis_size("tensor"), lax.axis_index("tensor")
    share = width // peers

    def half(value):
        cut = value[..., :share]
        for peer in range(1, peers):
            cut = jnp.where(here == peer, value[..., peer * share : (peer + 1) * share], cut)
        return cut

    x_rows = tensor_columns(swap_owners(packed(half(normed2))))
    gate_rows = swap_owners(
        jnp.sum(jnp.where(pick > 0, gate[:, 0], 0.0), -1)[:, None, :]
    )
    grad_rows = (jnp.swapaxes(gate_rows, 1, 2) * grad_rows_raw.astype(F32)).astype(BF16)
    up, down = expert_up[0], expert_down[0]

    def product(a, b, terms):
        return jnp.einsum(terms, a, b, preferred_element_type=F32)

    hidden = product(x_rows, up, "srd,df->srf")
    act_float, gelu_pull = jax.vjp(lambda v: jax.nn.gelu(v, approximate=True), hidden)
    act = act_float.astype(BF16)
    back_y = swap_owners(tensor_share(product(act, down, "srf,fd->srd")).astype(BF16))
    d_hidden = gelu_pull(product(grad_rows, down, "srd,fd->srf"))[0].astype(BF16)
    back_x = swap_owners(tensor_share(product(d_hidden, up, "srf,df->srd")).astype(BF16))
    grad_up = product(x_rows, d_hidden, "srd,srf->df")
    grad_down = product(act, grad_rows, "srf,srd->fd")
    expert_y = unpacked(back_y)
    expert_dx = unpacked(back_x)
    x_half = half(xhat2)
    gain_half = half(gains[1])
    grad_half = half(grad_act)
    router_half = half(w_router.T)
    sums = jnp.stack(
        [jnp.sum(grad_half * expert_y, -1), jnp.sum(gain_half * expert_dx * x_half, -1)]
    )
    sums = tensor_total(sums, F32)
    gate_grad = sums[0][:, None]
    d_logits = (gate_grad * gate * (onehot - probs)).astype(BF16)
    grad_router = dot(normed2, d_logits, TN)
    by_router = dot((xhat2 * gains[1]).astype(BF16), w_router)
    mean_term = (
        sums[1][:, None] + jnp.sum(d_logits.astype(F32) * by_router, -1, keepdims=True)
    ) / width
    d_normed2 = expert_dx + dot(d_logits, router_half)
    gain_grad2 = tensor_columns(jnp.sum(d_normed2 * x_half, 0, keepdims=True))[0]
    d_resid_half = grad_half + scale2 * (gain_half * d_normed2 - x_half * mean_term)
    act_half = (valid * (half(resid) + gate * expert_y)).astype(BF16)

    d_mixed = tensor_columns(d_resid_half.astype(BF16))
    d_mixed, act_half = lax.optimization_barrier((d_mixed, act_half))
    activations = tensor_columns(act_half)
    d_gated = dot(d_mixed, w_out, NT)
    d_y = d_gated * silu_z
    [start_grad] = call(
        start_grad_kernel,
        [both_in(delta), both_in(d_y), by_rows(c_vals), by_chan(rates)],
        [by_chan(out((N, seqs, chans)))],
        [wide_rates, (tokens, N * LANES)],
        cost=cost(length, 6),
    )
    d_gate_z = (d_gated * y_vals * gate_slope).astype(BF16)

    def owned(value):
        return lax.psum_scatter(
            value.astype(BF16), OWNERS, scatter_dimension=0, tiled=True
        ).astype(F32)

    mine_early = owned(
        jnp.concatenate([dot(d_gate_z, normed1, TN), dot(gated, d_mixed, TN)], 1)
    )
    grad_end = carried(start_grad, log_decay, rates, -1)
    w_step_wide = jnp.pad(w_step, ((0, 0), (0, LANES - R)))
    d_step, du_part, d_proj_part, rate_grad, bias_sums, skip_sums = call(
        backward_kernel,
        [
            both_in(delta),
            both_in(u_wide),
            both_in(d_y),
            (jax.nn.sigmoid(step_pre), (tokens, lane_width), "tc"),
            by_rows(b_vals),
            by_rows(c_vals),
            by_chan(rates),
            by_chan(skip[None]),
            (w_step_wide, (lane_width, LANES), "r"),
            by_chan(starts),
            by_chan(grad_end),
        ],
        [
            by_chan(out((tokens, chans), BF16)),
            by_chan(out((tokens, chans))),
            (out((tokens, LANES), BF16), (tokens, LANES), ""),
            by_chan(out((N, seqs, chans))),
            by_chan(out((seqs, chans))),
            by_chan(out((seqs, chans))),
        ],
        [
            wide_rates,
            (tokens, N * LANES),
            (tokens, N * LANES),
            (BLK + 1, N, seqs, lane_width),
            (BLK, N, seqs, lane_width),
            (BLK * seqs, N * LANES),
            (BLK * seqs, N * LANES),
            (BLK * seqs, lane_width),
            (tokens, LANES),
            pltpu.VMEM((2 * N * LANES, LANES), BF16),
        ],
        cost=cost(length, 24),
    )
    d_step, mine_early, activations = lax.optimization_barrier((d_step, mine_early, activations))
    d_proj = tensor_total(d_proj_part, BF16).astype(BF16)
    step_bias_grad = jnp.sum(bias_sums, 0)
    skip_grad = jnp.sum(skip_sums, 0)
    w_x_wide = jnp.pad(w_x, ((0, 0), (0, LANES - x_cols)))
    rim_u = du_part[:rim] + dot(d_proj[:rim], w_x_wide, NT)
    after = moved(rim_u * silu_parts(conv[:rim])[1], -1)
    steps = length // 4
    block = steps * seqs
    turns = length // steps

    def from_end(value):
        return value, pl.BlockSpec((block, value.shape[1]), lambda i: (turns - 1 - i, 0))

    def whole(value):
        return value, pl.BlockSpec(value.shape, lambda i: (0, 0))

    arrays = [
        from_end(du_part),
        from_end(d_proj),
        from_end(conv),
        whole(extended),
        from_end(normed1),
        from_end(x_tok),
        from_end(u),
        from_end(rank),
        from_end(d_step),
        from_end(d_gate_z),
        whole(w_in),
        whole(w_gate),
        whole(w_x_wide),
        whole(taps),
        whole(after),
    ]
    results = [
        (
            out((tokens // 2, width), BF16),
            pl.BlockSpec((block, width), lambda i: (jnp.maximum(turns // 2 - 1 - i, 0), 0)),
        ),
        (
            out((tokens // 2, width), BF16),
            pl.BlockSpec(
                (block, width), lambda i: (jnp.minimum(turns - 1 - i, turns // 2 - 1), 0)
            ),
        ),
        whole(out((chans, width))),
        whole(out((chans, LANES))),
        whole(out((chans, R))),
        whole(out(((CONV_TAPS + 1) * seqs, chans))),
        whole(out((seqs, width))),
    ]
    late_part, early_part, grad_in, grad_xproj, grad_dt, conv_sums, gain_sums = pl.pallas_call(
        functools.partial(inner_grad_kernel, seqs),
        grid=(turns,),
        in_specs=[spec for _, spec in arrays],
        out_specs=[spec for _, spec in results],
        out_shape=[value for value, _ in results],
        scratch_shapes=[pltpu.VMEM((block + rim, chans), F32)],
        compiler_params=pltpu.CompilerParams(vmem_limit_bytes=62 << 20),
    )(*[value for value, _ in arrays])
    grad_xproj = grad_xproj[:, :x_cols]
    conv_sums = jnp.sum(conv_sums.reshape(CONV_TAPS + 1, seqs, chans), 1)
    gain_grad1 = jnp.sum(gain_sums, 0)

    narrow_grads = jnp.concatenate(
        [
            grad_xproj,
            grad_dt,
            conv_sums.T,
            skip_grad[:, None],
            (jnp.sum(rate_grad, 1) * rates).T,
            step_bias_grad[:, None],
        ],
        1,
    )
    routing_grads = jnp.concatenate([grad_router, gain_grad1[:, None], gain_grad2[:, None]], 1)
    if joined:
        narrow_grads = jnp.concatenate([narrow_grads, routing_grads], 1)
    wide_grads = jnp.concatenate(
        [grad_in, jnp.pad(narrow_grads, ((0, 0), (0, pad)))], 1
    )

    halves = [late_part, early_part]
    if peers == 2:
        exchanged = [swapped(part) for part in halves]
    else:
        exchanged = [lax.all_gather(part, "tensor") for part in halves]
    mine, exchanged = halved(wide_grads, exchanged)
    normed_parts = []
    for own, others in zip(halves, exchanged):
        if peers == 2:
            normed_parts.append([own, others])
        else:
            normed_parts.append([others[k] for k in range(peers)])
    late_parts, early_parts = normed_parts

    def rows_of(value):
        return value, pl.BlockSpec((block, value.shape[1]), lambda i: (i, 0))

    def early_rows(value):
        return value, pl.BlockSpec((block, width), lambda i: (jnp.minimum(i, turns // 2 - 1), 0))

    def late_rows(value):
        return value, pl.BlockSpec((block, width), lambda i: (jnp.maximum(i - turns // 2, 0), 0))

    arrays = (
        [early_rows(part) for part in early_parts]
        + [late_rows(part) for part in late_parts]
        + [rows_of(x_tok), rows_of(d_mixed), rows_of(activations), whole(gains[:1])]
    )
    out_spec = pl.BlockSpec((micros, group, steps, width), lambda i: (0, 0, i, 0))
    input_grad, activations = pl.pallas_call(
        functools.partial(output_kernel, (micros, group), peers),
        grid=(turns,),
        in_specs=[spec for _, spec in arrays],
        out_specs=[out_spec, out_spec],
        out_shape=[out(inputs.shape), out(inputs.shape, BF16)],
        scratch_shapes=[pltpu.VMEM((width // LANES, block, LANES), F32)] * 2,
        compiler_params=pltpu.CompilerParams(vmem_limit_bytes=62 << 20),
    )(*[value for value, _ in arrays])
    mine_tail = mine[:, width:]
    if joined:
        mine_routing = mine_tail[:, cuts[2] + 1 : cuts[2] + 1 + routing.shape[1]]
    else:
        mine_routing, _ = halved(routing_grads)
    gains_out = jnp.stack(
        [tensor_total(mine_routing[None, :, experts], F32)[0], mine_routing[:, experts + 1]]
    )
    return (
        activations,
        input_grad,
        gains_out,
        mine_routing[:, :experts],
        jnp.stack([mine[:, :width], mine_early[:, :width]]),
        mine_tail[:, : cuts[0]],
        mine_tail[:, cuts[0] : cuts[1]],
        mine_tail[:, cuts[2]],
        mine_tail[:, cuts[1] : cuts[2]],
        mine_early[:, width:],
        grad_up[None],
        grad_down[None],
    )


def solution(mesh):
    return jax.shard_map(
        per_device,
        mesh=mesh,
        in_specs=(
            P(None, "fsdp", "ctx", None),
            P(None, "fsdp", "ctx", None),
            P(None, "fsdp"),
            P(None, "fsdp", "ctx"),
            P(None, "fsdp", "ctx"),
            P(None, ("fsdp", "ctx")),
            P(("fsdp", "ctx"), None),
            P(None, ("fsdp", "ctx", "tensor"), None),
            P(("fsdp", "ctx", "tensor"), None),
            P(("fsdp", "ctx", "tensor"), None),
            P(("fsdp", "ctx", "tensor")),
            P(("fsdp", "ctx", "tensor"), None),
            P(("fsdp", "ctx", "tensor"), None),
            P(("fsdp", "ctx"), None, "tensor"),
            P(("fsdp", "ctx"), "tensor", None),
        ),
        out_specs=(
            P(None, "fsdp", "ctx", None),
            P(None, "fsdp", "ctx", None),
            P(None, ("fsdp", "ctx")),
            P(("fsdp", "ctx"), None),
            P(None, ("fsdp", "ctx", "tensor"), None),
            P(("fsdp", "ctx", "tensor"), None),
            P(("fsdp", "ctx", "tensor"), None),
            P(("fsdp", "ctx", "tensor")),
            P(("fsdp", "ctx", "tensor"), None),
            P(("fsdp", "ctx", "tensor"), None),
            P(("fsdp", "ctx"), None, "tensor"),
            P(("fsdp", "ctx"), "tensor", None),
        ),
        check_vma=False,
    )
```

time: 773 us -> 616 us (0.80)
  waiting for transfers between devices: 302 us -> 189 us
  Pallas kernels: 114 us -> 152 us
  blocking collectives: 37.1 us -> 0 us
  local copies, waits for them, and re-layouts: 85.4 us -> 52.6 us
  matrix products: 91.2 us -> 69.3 us
  starting transfers between devices: 57.8 us -> 73.2 us
    dot_general x26 -> x13, matrix products: 88.3 us -> 33.8 us  [dot(): return lax.dot_general(a, b, dims, preferred_element_type=F32)]
    pallas_call x4 -> x9, Pallas kernels: 114 us -> 152 us  [the longest x7 129 us: scan_call(): pl.pallas_call(kernel, grid=(chans // width,), in_specs=[spec(shape, kind...]
    all_to_all x1 -> x0, blocking collectives: 37.1 us -> none  [to_experts(): lax.all_to_all(value.reshape(experts, slots_each, value.shape[-1]), OWNER...]
    dot_general x1 -> x8, matrix products: 2.96 us -> 35.5 us  [the longest x6 30.7 us: product(): return jnp.einsum(terms, a, b, preferred_element_type=F32)]
    unnamed x3 -> x4, waiting for transfers between devices: 31.9 us -> 0.05 us
    ppermute x8, waiting for transfers between devices: 55.2 us -> 23.6 us  [moved(): return lax.ppermute(value, 'ctx', pairs)]
    all_to_all x2 -> x5, waiting for transfers between devices: 52.1 us -> 26.8 us  [swap_owners(): lax.all_to_all(value, OWNERS, split_axis=0, concat_axis=0, tiled=True)]
    ppermute x8 -> x16, waiting for transfers between devices: 120 us -> 95.2 us  [swapped(): return lax.ppermute(value, 'tensor', [(0, 1), (1, 0)])]
  transfers between devices with their start and end apart: 20 -> 36, of which waited for: 19 -> 22; matrix products, arithmetic and copies ran while one was open for 12% -> 20% of each run, Pallas kernels for 0% -> 20%
where the time goes in v1:
time: 616 us; the launch traced here: 606 us
  waiting for transfers between devices  189 us (31%)
  Pallas kernels  152 us (25%)
  starting transfers between devices  73.2 us (12%)
  matrix products  69.3 us (11%)
  other arithmetic  54.7 us (9%)
  local copies, waits for them, and re-layouts  52.6 us (9%)
  between operations  15.3 us (2%)
    pallas_call x7, Pallas kernels, scan_call(): pl.pallas_call(kernel, grid=(chans // width,), in_specs=[spec(shape, kind...  129 us
    ppermute x16, waiting for transfers between devices, swapped(): return lax.ppermute(value, 'tensor', [(0, 1), (1, 0)])  95.2 us
    all_gather x1, waiting for transfers between devices, per_device(): full = lax.all_gather(first, OWNERS, axis=0, tiled=True)  34 us
    dot_general x13, matrix products, dot(): return lax.dot_general(a, b, dims, preferred_element_type=F32)  33.8 us
    dot_general x6, matrix products, product(): return jnp.einsum(terms, a, b, preferred_element_type=F32)  30.7 us
    all_to_all x5, starting transfers between devices, swap_owners(): lax.all_to_all(value, OWNERS, split_axis=0, concat_axis=0, tiled=True)  29.5 us
    all_to_all x5, waiting for transfers between devices, swap_owners(): lax.all_to_all(value, OWNERS, split_axis=0, concat_axis=0, tiled=True)  26.8 us
    ppermute x8, waiting for transfers between devices, moved(): return lax.ppermute(value, 'ctx', pairs)  23.6 us
  transfers between devices with their start and end apart: 36, of which 22 were waited for; matrix products, arithmetic and copies ran while one was open for 20% of the time, Pallas kernels for 20%

profile of v1, /device:TPU:0, one launch (start us, length us, event | category | flops | bytes accessed | tf_op | source)
XLA Modules:
  0.0 606.3 jit_solution(16179446026012602435)
XLA Ops:
  14.4 3.8 copy.230
  21.3 34.0 %all-gather.3.cloned.1.call-done = bf16[768,1024]{1,0:T(8,128)(2,1)} async-done(((bf16[48,1024]{1,0:T(8,128)(2,1)}), bf16[768,1024]{1,0:T(8,128)(2,1)}) %all-gather.3.cloned.1.call-update) | async-done | bytes 1572880 | tf_op jit(solution)/shard_map/all_gather | solution.py:595
  64.4 3.7 fusion.130
  71.0 6.4 %collective-permute-done.1 = bf16[1024,80]{1,0:T(8,128)(2,1)S(1)} collective-permute-done((bf16[1024,80]{1,0:T(8,128)(2,1)S(1)}, bf16[1024,80]{1,0:T(8,128)(2,1)S(1)}, u32[]{:S(2)}, u32[]{:S(2)}) %collective-permute-start.1) | collective-permute-done | bytes 163872 | tf_op jit(solution)/shard_map/ppermute | solution.py:27
  78.8 5.1 add_divide_fusion
  83.9 16.5 %shard_map.238 = f32[17,8,768]{2,1,0:T(8,128)} custom-call(f32[1024,768]{1,0:T(8,128)} %get-tuple-element.233.d_ref, f32[1024,768]{1,0:T(8,128)} %get-tuple-element.227.u_ref, f32[1024,16]{1,0:T(8,128)} %get-tuple-element.249.b_ref, f32[16,768]{1,0:T(8,128)} %fusion.95.r_ref), custom_call_target="tpu_custom_call" | custom-call | flops 22649241600 | bytes 12582912 | tf_op jit(solution)/shard_map/pallas_call | solution.py:539
  104.2 3.8 copy.233
  108.1 3.8 reshape.283
  112.8 3.0 collective-permute-start.3
  115.8 4.4 collective-permute-done.3
  120.5 6.8 %collective-permute-start.4 = (bf16[18,8,768]{2,1,0:T(8,128)(2,1)S(1)}, bf16[18,8,768]{2,1,0:T(8,128)(2,1)S(1)}, u32[]{:S(2)}, u32[]{:S(2)}) collective-permute-start(bf16[18,8,768]{2,1,0:T(8,128)(2,1)S(1)} %pad_maximum_fusion.11), channel_id=1, source_target_pairs={{0,8},{2,10},{4,12},{6,14},{1,9},{3,11},{5,13},{7,15},{16,24},{18,... | collective-permute-start | bytes 663560 | tf_op jit(solution)/shard_map/ppermute | solution.py:79
  132.8 9.4 %all-to-all-start = ((bf16[16,50,768]{2,1,0:T(8,128)(2,1)}), bf16[16,50,768]{2,1,0:T(8,128)(2,1)}, u32[]{:S(2)}, u32[]{:S(2)}) async-start(bf16[16,50,768]{2,1,0:T(8,128)(2,1)} %fusion.42), calls=%async_computation | async-start | bytes 2752512 | tf_op jit(solution)/shard_map/all_to_all | solution.py:620
  142.3 5.0 fusion.121.z_ref
  148.8 8.4 %shard_map.239 = (f32[256,768]{1,0:T(8,128)}, bf16[256,768]{1,0:T(8,128)(2,1)}, bf16[256,768]{1,0:T(8,128)(2,1)}, f32[4,16,8,768]{3,2,1,0:T(8,128)}, f32[16,8,768]{2,1,0:T(8,128)}) custom-call(f32[1024,768]{1,0:T(8,128)} %get-tuple-element.233.d_ref, f32[1024,768]{1,0:T(8,128)} %get-tuple-element.227.u_ref, f32[1024,768]{1,0:T(8,128)} %fusion.121.z_ref, ...), custom_call_target="tpu_custom_call" | custom-call | flops 9437184000 | bytes 3145728 | tf_op jit(solution)/shard_map/pallas_call | solution.py:539
  158.8 8.4 %shard_map.240 = (f32[256,768]{1,0:T(8,128)}, bf16[256,768]{1,0:T(8,128)(2,1)}, bf16[256,768]{1,0:T(8,128)(2,1)}, f32[4,16,8,768]{3,2,1,0:T(8,128)}, f32[16,8,768]{2,1,0:T(8,128)}) custom-call(f32[1024,768]{1,0:T(8,128)} %get-tuple-element.233.d_ref, f32[1024,768]{1,0:T(8,128)} %get-tuple-element.227.u_ref, f32[1024,768]{1,0:T(8,128)} %fusion.121.z_ref, ...), custom_call_target="tpu_custom_call" | custom-call | flops 9437184000 | bytes 3145728 | tf_op jit(solution)/shard_map/pallas_call | solution.py:539
  171.1 7.4 %collective-permute-done.6 = bf16[256,768]{1,0:T(8,128)(2,1)S(1)} collective-permute-done((bf16[256,768]{1,0:T(8,128)(2,1)}, bf16[256,768]{1,0:T(8,128)(2,1)S(1)}, u32[]{:S(2)}, u32[]{:S(2)}) %collective-permute-start.6) | collective-permute-done | bytes 393248 | tf_op jit(solution)/shard_map/ppermute | solution.py:27
  180.6 8.4 %shard_map.241 = (f32[256,768]{1,0:T(8,128)}, bf16[256,768]{1,0:T(8,128)(2,1)}, bf16[256,768]{1,0:T(8,128)(2,1)}, f32[4,16,8,768]{3,2,1,0:T(8,128)}, f32[16,8,768]{2,1,0:T(8,128)}) custom-call(f32[1024,768]{1,0:T(8,128)} %get-tuple-element.233.d_ref, f32[1024,768]{1,0:T(8,128)} %get-tuple-element.227.u_ref, f32[1024,768]{1,0:T(8,128)} %fusion.121.z_ref, ...), custom_call_target="tpu_custom_call" | custom-call | flops 9437184000 | bytes 3145728 | tf_op jit(solution)/shard_map/pallas_call | solution.py:539
  189.6 8.4 %shard_map.242 = (f32[256,768]{1,0:T(8,128)}, bf16[256,768]{1,0:T(8,128)(2,1)}, bf16[256,768]{1,0:T(8,128)(2,1)}, f32[4,16,8,768]{3,2,1,0:T(8,128)}, f32[16,8,768]{2,1,0:T(8,128)}) custom-call(f32[1024,768]{1,0:T(8,128)} %get-tuple-element.233.d_ref, f32[1024,768]{1,0:T(8,128)} %get-tuple-element.227.u_ref, f32[1024,768]{1,0:T(8,128)} %fusion.121.z_ref, ...), custom_call_target="tpu_custom_call" | custom-call | flops 9437184000 | bytes 3145728 | tf_op jit(solution)/shard_map/pallas_call | solution.py:539
  200.8 7.4 %collective-permute-done.8 = bf16[256,768]{1,0:T(8,128)(2,1)S(1)} collective-permute-done((bf16[256,768]{1,0:T(8,128)(2,1)}, bf16[256,768]{1,0:T(8,128)(2,1)S(1)}, u32[]{:S(2)}, u32[]{:S(2)}) %collective-permute-start.8) | collective-permute-done | bytes 393248 | tf_op jit(solution)/shard_map/ppermute | solution.py:27
  214.5 5.5 all-to-all-start.2
  221.6 15.8 %all-to-all-done.2 = bf16[16,50,384]{2,1,0:T(8,128)(2,1)S(1)} async-done(((bf16[16,50,384]{2,1,0:T(8,128)(2,1)}), bf16[16,50,384]{2,1,0:T(8,128)(2,1)S(1)}, u32[]{:S(2)}, u32[]{:S(2)}) %all-to-all-start.2) | async-done | bytes 614432 | tf_op jit(solution)/shard_map/all_to_all | solution.py:620
  240.5 4.5 all-to-all-start.1
  245.0 9.1 %collective-permute-done.9 = bf16[16,50,384]{2,0,1:T(8,128)(2,1)S(1)} collective-permute-done((bf16[16,50,384]{2,0,1:T(8,128)(2,1)S(1)}, bf16[16,50,384]{2,0,1:T(8,128)(2,1)S(1)}, u32[]{:S(2)}, u32[]{:S(2)}) %collective-permute-start.9) | collective-permute-done | bytes 614432 | tf_op jit(solution)/shard_map/ppermute | solution.py:27
  255.4 6.4 %multiply_convert_fusion = (bf16[16,50,1536]{2,1,0:T(8,128)(2,1)}, f32[16,50,1536]{2,1,0:T(8,128)}) fusion(bf16[1,768,1536]{2,1,0:T(8,128)(2,1)S(1)} %copy-done.52, bf16[16,50,768]{2,0,1:T(8,128)(2,1)S(1)} %pad_maximum_fusion.4), kind=kOutput, calls=%fused_computation.20 | convolution fusion | flops 1898496000 | bytes 10960896 | tf_op jit(solution)/shard_map/srd,df->srf/dot_general | solution.py:761
  261.9 7.6 %fusion.14 = bf16[16,50,1536]{2,1,0:T(8,128)(2,1)S(1)} fusion(f32[16,50,1536]{2,1,0:T(8,128)} %get-tuple-element.263, bf16[1,1536,768]{2,1,0:T(8,128)(2,1)S(1)} %copy-done.54, bf16[16,50,768]{2,1,0:T(8,128)(2,1)} %all-to-all-done, f32[16,50]{1,0:T(8,128)S(1)} %bitcast.189), kind=kOutput, calls=%fused_computation.19 | convolution fusion | flops 1913856000 | bytes 10964096 | tf_op jit(solution)/shard_map/srd,fd->srf/dot_general | solution.py:761
  273.5 3.7 fusion.24
  277.2 10.5 %collective-permute-done.10 = bf16[16,50,384]{2,0,1:T(8,128)(2,1)S(1)} collective-permute-done((bf16[16,50,384]{2,0,1:T(8,128)(2,1)S(1)}, bf16[16,50,384]{2,0,1:T(8,128)(2,1)S(1)}, u32[]{:S(2)}, u32[]{:S(2)}) %collective-permute-start.10) | collective-permute-done | bytes 614432 | tf_op jit(solution)/shard_map/ppermute | solution.py:27
  288.9 4.3 all-to-all-start.3
  297.8 14.3 %collective-permute-done.11 = bf16[16,50,384]{2,0,1:T(8,128)(2,1)} collective-permute-done((bf16[16,50,384]{2,0,1:T(8,128)(2,1)}, bf16[16,50,384]{2,0,1:T(8,128)(2,1)}, u32[]{:S(2)}, u32[]{:S(2)}) %collective-permute-start.11) | collective-permute-done | bytes 614432 | tf_op jit(solution)/shard_map/ppermute | solution.py:27
  315.2 5.9 all-to-all-start.4
  323.8 3.8 fusion.59
  327.5 11.0 %all-to-all-done.4 = bf16[16,50,384]{2,1,0:T(8,128)(2,1)} async-done(((bf16[16,50,384]{2,1,0:T(8,128)(2,1)}), bf16[16,50,384]{2,1,0:T(8,128)(2,1)}, u32[]{:S(2)}, u32[]{:S(2)}) %all-to-all-start.4) | async-done | bytes 614432 | tf_op jit(solution)/shard_map/all_to_all | solution.py:620
  357.4 13.4 %collective-permute-done.20 = f32[1,384]{1,0:T(1,128)S(1)} collective-permute-done((f32[1,384]{1,0:T(1,128)S(1)}, f32[1,384]{1,0:T(1,128)S(1)}, u32[]{:S(2)}, u32[]{:S(2)}) %collective-permute-start.20) | collective-permute-done | bytes 1568 | tf_op jit(solution)/shard_map/ppermute | solution.py:27
  375.0 5.6 fusion.23
  380.7 16.3 %shard_map.243 = f32[16,8,768]{2,1,0:T(8,128)} custom-call(f32[1024,768]{1,0:T(8,128)} %get-tuple-element.233.d_ref, f32[1024,768]{1,0:T(8,128)} %get-tuple-element.231.dy_ref, f32[1024,16]{1,0:T(8,128)} %get-tuple-element.248.c_ref, f32[16,768]{1,0:T(8,128)} %fusion.95.r_ref), custom_call_target="tpu_custom_call" | custom-call | flops 22649241600 | bytes 12582912 | tf_op jit(solution)/shard_map/pallas_call | solution.py:539
  399.4 2.9 fusion.56
  406.2 6.2 %collective-permute-done.15 = bf16[18,8,768]{2,1,0:T(8,128)(2,1)S(1)} collective-permute-done((bf16[18,8,768]{2,1,0:T(8,128)(2,1)S(1)}, bf16[18,8,768]{2,1,0:T(8,128)(2,1)S(1)}, u32[]{:S(2)}, u32[]{:S(2)}) %collective-permute-start.15) | collective-permute-done | bytes 221216 | tf_op jit(solution)/shard_map/ppermute | solution.py:79
  419.6 10.4 %collective-permute-done.16 = bf16[18,8,768]{2,1,0:T(8,128)(2,1)} collective-permute-done((bf16[18,8,768]{2,1,0:T(8,128)(2,1)}, bf16[18,8,768]{2,1,0:T(8,128)(2,1)}, u32[]{:S(2)}, u32[]{:S(2)}) %collective-permute-start.16) | collective-permute-done | bytes 221216 | tf_op jit(solution)/shard_map/ppermute | solution.py:79
  431.8 63.0 %shard_map.244 = (bf16[1024,768]{1,0:T(8,128)(2,1)}, f32[1024,768]{1,0:T(8,128)}, bf16[1024,128]{1,0:T(8,128)(2,1)}, f32[16,8,768]{2,1,0:T(8,128)}, f32[8,768]{1,0:T(8,128)}, /*index=5*/f32[8,768]{1,0:T(8,128)}) custom-call(f32[1024,768]{1,0:T(8,128)} %get-tuple-element.233.d_ref, f32[1024,768]{1,0:T(8,128)} %get-tuple-element.227.u_ref, ...), custom_call_target="tpu_custom_call" | custom-call | flops 90596966400 | bytes 12582912 | tf_op jit(solution)/shard_map/pallas_call | solution.py:539
  510.1 15.5 %shard_map.245 = (bf16[512,768]{1,0:T(8,128)(2,1)}, bf16[512,768]{1,0:T(8,128)(2,1)}, f32[768,768]{1,0:T(8,128)}, f32[768,128]{1,0:T(8,128)}, f32[768,48]{1,0:T(...) custom-call(f32[1024,768]{1,0:T(8,128)} %get-tuple-element.83.du_ref, bf16[1024,128]{1,0:T(8,128)(2,1)} %copy-done.39, ...), custom_call_target="tpu_custom_call" | custom-call | tf_op jit(solution)/shard_map/pallas_call | solution.py:905
  527.7 3.5 concatenate.83
  539.8 16.6 %collective-permute-done.22.refs_3_ = bf16[512,768]{1,0:T(8,128)(2,1)} collective-permute-done((bf16[512,768]{1,0:T(8,128)(2,1)}, bf16[512,768]{1,0:T(8,128)(2,1)}, u32[]{:S(2)}, u32[]{:S(2)}) %collective-permute-start.22) | collective-permute-done | bytes 786464 | tf_op jit(solution)/shard_map/ppermute | solution.py:27
  556.9 4.5 convolution_bitcast_fusion.1
  561.4 4.4 collective-permute-done.23
  565.9 6.3 %collective-permute-done.24.refs_1_ = bf16[512,768]{1,0:T(8,128)(2,1)S(1)} collective-permute-done((bf16[512,768]{1,0:T(8,128)(2,1)}, bf16[512,768]{1,0:T(8,128)(2,1)S(1)}, u32[]{:S(2)}, u32[]{:S(2)}) %collective-permute-start.24) | collective-permute-done | bytes 786464 | tf_op jit(solution)/shard_map/ppermute | solution.py:27
  572.3 6.2 %convolution_bitcast_fusion = f32[1,1536,768]{2,1,0:T(8,128)} fusion(bf16[16,50,1536]{2,1,0:T(8,128)(2,1)S(1)} %copy-done.60, bf16[16,50,768]{2,1,0:T(8,128)(2,1)} %all-to-all-done, f32[16,50]{1,0:T(8,128)S(1)} %bitcast.190), kind=kOutput, calls=%fused_computation.24 | convolution fusion | flops 1889280000 | bytes 8408192 | tf_op jit(solution)/shard_map/srf,srd->fd/dot_general | solution.py:761
  578.5 4.8 collective-permute-done.25
  586.0 7.2 %shard_map.246 = (f32[2,4,128,768]{3,2,1,0:T(8,128)}, bf16[2,4,128,768]{3,2,1,0:T(8,128)(2,1)}) custom-call(bf16[512,768]{1,0:T(8,128)(2,1)} %get-tuple-element.96.refs_0_, bf16[512,768]{1,0:T(8,128)(2,1)} %copy-done.40, bf16[512,768]{1,0:T(8,128)(2,1)} %get-tuple-element.105.refs_2_, bf16[512,768]{1,0:T(8,128)(2,1)} %collective-permute-done.22.refs_3_, ...), custom_call_target="tpu_custom_call" | custom-call | tf_op jit(solution)/shard_map/pallas_call | solution.py:965
  (333 shorter events, 147.8 us)
Async XLA Ops:
  7.2 48.1 %all-gather.3.cloned.1.call-start = ((), (), s32[]{:S(2)}) async-start(), calls=%async_computation.6 | async-start | bytes 1671168 | tf_op jit(solution)/shard_map/all_gather | solution.py:595
  12.7 129.5 %all-gather.5.cloned.1.call-start = ((), (), s32[]{:S(2)}) async-start(), calls=%async_computation.7 | async-start | bytes 2506752 | tf_op jit(solution)/shard_map/all_gather | solution.py:596
  20.9 188.4 %copy-start.1 = (bf16[1024,768]{1,0:T(8,128)(2,1)}, bf16[1024,768]{1,0:T(8,128)(2,1)S(1)}, u32[]{:S(2)}) copy-start(bf16[1024,768]{1,0:T(8,128)(2,1)S(1)} %reshape.268.x_ref.refs_4_) | copy-start | bytes 4718596
  56.4 13.8 %copy-start.43 = (f32[768,22]{0,1:T(8,128)}, f32[768,22]{0,1:T(8,128)S(1)}, u32[]{:S(2)}) copy-start(f32[768,22]{0,1:T(8,128)S(1)} %convert_element_type.314) | copy-start | bytes 202756
  61.1 3.0 collective-permute-start
  68.6 8.8 %collective-permute-start.1 = (bf16[1024,80]{1,0:T(8,128)(2,1)S(1)}, bf16[1024,80]{1,0:T(8,128)(2,1)S(1)}, u32[]{:S(2)}, u32[]{:S(2)}) collective-permute-start(bf16[1024,80]{1,0:T(8,128)(2,1)S(1)} %convolution_convert_fusion.2), channel_id=1, source_target_pairs={{0,1},{1,0},{2,3},{3,2},{4,5},{5,4},{6,7},{7,6},{8,9},{9,8},{10,11... | collective-permute-start | bytes 491528 | tf_op jit(solution)/shard_map/ppermute | solution.py:27
  102.3 10.2 %collective-permute-start.2 = (bf16[18,8,768]{2,1,0:T(8,128)(2,1)S(1)}, bf16[18,8,768]{2,1,0:T(8,128)(2,1)S(1)}, u32[]{:S(2)}, u32[]{:S(2)}) collective-permute-start(bf16[18,8,768]{2,1,0:T(8,128)(2,1)S(1)} %pad_maximum_fusion.6), channel_id=1, source_target_pairs={{0,2},{2,4},{4,6},{6,8},{8,10},{10,12},{12,14},{1,3},{3,5},{5,7},{... | collective-permute-start | bytes 663560 | tf_op jit(solution)/shard_map/ppermute | solution.py:79
  112.6 14.8 %copy-start.37 = (bf16[1024,768,1]{1,0,2:T(8,128)(2,1)S(1)}, bf16[1024,768,1]{1,0,2:T(8,128)(2,1)}, u32[]{:S(2)}) copy-start(bf16[1024,768,1]{1,0,2:T(8,128)(2,1)} %reshape.283) | copy-start | bytes 4718596
  112.8 7.5 %collective-permute-start.3 = (bf16[18,8,768]{2,1,0:T(8,128)(2,1)S(1)}, bf16[18,8,768]{2,1,0:T(8,128)(2,1)S(1)}, u32[]{:S(2)}, u32[]{:S(2)}) collective-permute-start(bf16[18,8,768]{2,1,0:T(8,128)(2,1)S(1)} %pad_maximum_fusion.10), channel_id=1, source_target_pairs={{0,4},{2,6},{4,8},{6,10},{8,12},{10,14},{1,5},{3,7},{5,9},{7,11},{... | collective-permute-start | bytes 663560 | tf_op jit(solution)/shard_map/ppermute | solution.py:79
  120.5 11.4 %collective-permute-start.4 = (bf16[18,8,768]{2,1,0:T(8,128)(2,1)S(1)}, bf16[18,8,768]{2,1,0:T(8,128)(2,1)S(1)}, u32[]{:S(2)}, u32[]{:S(2)}) collective-permute-start(bf16[18,8,768]{2,1,0:T(8,128)(2,1)S(1)} %pad_maximum_fusion.11), channel_id=1, source_target_pairs={{0,8},{2,10},{4,12},{6,14},{1,9},{3,11},{5,13},{7,15},{16,24},{18,... | collective-permute-start | bytes 663560 | tf_op jit(solution)/shard_map/ppermute | solution.py:79
  132.8 56.7 %all-to-all-start = ((bf16[16,50,768]{2,1,0:T(8,128)(2,1)}), bf16[16,50,768]{2,1,0:T(8,128)(2,1)}, u32[]{:S(2)}, u32[]{:S(2)}) async-start(bf16[16,50,768]{2,1,0:T(8,128)(2,1)} %fusion.42), calls=%async_computation | async-start | bytes 2752512 | tf_op jit(solution)/shard_map/all_to_all | solution.py:620
  157.3 11.8 %collective-permute-start.5 = (bf16[256,768]{1,0:T(8,128)(2,1)}, bf16[256,768]{1,0:T(8,128)(2,1)}, u32[]{:S(2)}, u32[]{:S(2)}) collective-permute-start(bf16[256,768]{1,0:T(8,128)(2,1)} %get-tuple-element.66), channel_id=1, source_target_pairs={{0,1},{1,0},{2,3},{3,2},{4,5},{5,4},{6,7},{7,6},{8,9},{9,8},{10,11... | collective-permute-start | bytes 1179656 | tf_op jit(solution)/shard_map/ppermute | solution.py:27
  167.2 11.4 %collective-permute-start.6 = (bf16[256,768]{1,0:T(8,128)(2,1)}, bf16[256,768]{1,0:T(8,128)(2,1)S(1)}, u32[]{:S(2)}, u32[]{:S(2)}) collective-permute-start(bf16[256,768]{1,0:T(8,128)(2,1)} %get-tuple-element.70), channel_id=1, source_target_pairs={{0,1},{1,0},{2,3},{3,2},{4,5},{5,4},{6,7},{7,6},{8,9},{9,8},{10,11... | collective-permute-start | bytes 1179656 | tf_op jit(solution)/shard_map/ppermute | solution.py:27
  188.9 10.6 %collective-permute-start.7 = (bf16[256,768]{1,0:T(8,128)(2,1)}, bf16[256,768]{1,0:T(8,128)(2,1)}, u32[]{:S(2)}, u32[]{:S(2)}) collective-permute-start(bf16[256,768]{1,0:T(8,128)(2,1)} %get-tuple-element.72), channel_id=1, source_target_pairs={{0,1},{1,0},{2,3},{3,2},{4,5},{5,4},{6,7},{7,6},{8,9},{9,8},{10,11... | collective-permute-start | bytes 1179656 | tf_op jit(solution)/shard_map/ppermute | solution.py:27
  198.0 10.2 %collective-permute-start.8 = (bf16[256,768]{1,0:T(8,128)(2,1)}, bf16[256,768]{1,0:T(8,128)(2,1)S(1)}, u32[]{:S(2)}, u32[]{:S(2)}) collective-permute-start(bf16[256,768]{1,0:T(8,128)(2,1)} %get-tuple-element.76), channel_id=1, source_target_pairs={{0,1},{1,0},{2,3},{3,2},{4,5},{5,4},{6,7},{7,6},{8,9},{9,8},{10,11... | collective-permute-start | bytes 1179656 | tf_op jit(solution)/shard_map/ppermute | solution.py:27
  214.5 22.9 %all-to-all-start.2 = ((bf16[16,50,384]{2,1,0:T(8,128)(2,1)}), bf16[16,50,384]{2,1,0:T(8,128)(2,1)S(1)}, u32[]{:S(2)}, u32[]{:S(2)}) async-start(bf16[16,50,384]{2,1,0:T(8,128)(2,1)} %fusion.66), calls=%async_computation.2 | async-start | bytes 1376256 | tf_op jit(solution)/shard_map/all_to_all | solution.py:620
  237.5 16.6 %collective-permute-start.9 = (bf16[16,50,384]{2,0,1:T(8,128)(2,1)S(1)}, bf16[16,50,384]{2,0,1:T(8,128)(2,1)S(1)}, u32[]{:S(2)}, u32[]{:S(2)}) collective-permute-start(bf16[16,50,384]{2,0,1:T(8,128)(2,1)S(1)} %copy.237), channel_id=1, source_target_pairs={{0,1},{1,0},{2,3},{3,2},{4,5},{5,4},{6,7},{7,6},{8,9},{9,8},{10,11... | collective-permute-start | bytes 1843208 | tf_op jit(solution)/shard_map/ppermute | solution.py:27
  240.5 21.3 %all-to-all-start.1 = ((f32[16,1,50]{2,1,0:T(1,128)}), f32[16,1,50]{2,1,0:T(1,128)S(1)}, u32[]{:S(2)}, u32[]{:S(2)}) async-start(f32[16,1,50]{2,1,0:T(1,128)} %bitcast.15), calls=%async_computation.1 | async-start | bytes 16384 | tf_op jit(solution)/shard_map/all_to_all | solution.py:620
  272.0 15.7 %collective-permute-start.10 = (bf16[16,50,384]{2,0,1:T(8,128)(2,1)S(1)}, bf16[16,50,384]{2,0,1:T(8,128)(2,1)S(1)}, u32[]{:S(2)}, u32[]{:S(2)}) collective-permute-start(bf16[16,50,384]{2,0,1:T(8,128)(2,1)S(1)} %select_convert_fusion.2), channel_id=1, source_target_pairs={{0,1},{1,0},{2,3},{3,2},{4,5},{5,4},{6,7},{7,6},{8,9},{9,8},{10,11... | collective-permute-start | bytes 1843208 | tf_op jit(solution)/shard_map/ppermute | solution.py:27
  288.9 26.3 %all-to-all-start.3 = ((bf16[16,50,384]{2,1,0:T(8,128)(2,1)}), bf16[16,50,384]{2,1,0:T(8,128)(2,1)}, u32[]{:S(2)}, u32[]{:S(2)}) async-start(bf16[16,50,384]{2,1,0:T(8,128)(2,1)} %copy.242), calls=%async_computation.3 | async-start | bytes 1376256 | tf_op jit(solution)/shard_map/all_to_all | solution.py:620
  295.8 16.3 %collective-permute-start.11 = (bf16[16,50,384]{2,0,1:T(8,128)(2,1)}, bf16[16,50,384]{2,0,1:T(8,128)(2,1)}, u32[]{:S(2)}, u32[]{:S(2)}) collective-permute-start(bf16[16,50,384]{2,0,1:T(8,128)(2,1)} %select_convert_fusion.1), channel_id=1, source_target_pairs={{0,1},{1,0},{2,3},{3,2},{4,5},{5,4},{6,7},{7,6},{8,9},{9,8},{10,11... | collective-permute-start | bytes 1843208 | tf_op jit(solution)/shard_map/ppermute | solution.py:27
  315.2 23.3 %all-to-all-start.4 = ((bf16[16,50,384]{2,1,0:T(8,128)(2,1)}), bf16[16,50,384]{2,1,0:T(8,128)(2,1)}, u32[]{:S(2)}, u32[]{:S(2)}) async-start(bf16[16,50,384]{2,1,0:T(8,128)(2,1)} %copy.245), calls=%async_computation.4 | async-start | bytes 1376256 | tf_op jit(solution)/shard_map/all_to_all | solution.py:620
  321.1 186.3 %reduce-scatter.4.cloned.1.call-start = ((), (), s32[]{:S(2)}) async-start(), calls=%async_computation.8 | async-start | bytes 2506752
  327.5 13.8 %copy-start.3 = (f32[1024,768]{1,0:T(8,128)S(1)}, f32[1024,768]{1,0:T(8,128)}, u32[]{:S(2)}) copy-start(f32[1024,768]{1,0:T(8,128)} %copy-done.2) | copy-start | bytes 9437188
  344.3 5.3 collective-permute-start.12
  350.7 21.0 %collective-permute-start.13 = (bf16[1024,384]{1,0:T(8,128)(2,1)S(1)}, bf16[1024,384]{1,0:T(8,128)(2,1)S(1)}, u32[]{:S(2)}, u32[]{:S(2)}) collective-permute-start(bf16[1024,384]{1,0:T(8,128)(2,1)S(1)} %get-tuple-element.235), channel_id=1, source_target_pairs={{0,1},{1,0},{2,3},{3,2},{4,5},{5,4},{6,7},{7,6},{8,9},{9,8},{10,11... | collective-permute-start | bytes 2359304 | tf_op jit(solution)/shard_map/ppermute | solution.py:27
  355.0 15.8 %collective-permute-start.20 = (f32[1,384]{1,0:T(1,128)S(1)}, f32[1,384]{1,0:T(1,128)S(1)}, u32[]{:S(2)}, u32[]{:S(2)}) collective-permute-start(f32[1,384]{1,0:T(1,128)S(1)} %broadcast_in_dim.33), channel_id=1, source_target_pairs={{0,1},{1,0},{2,3},{3,2},{4,5},{5,4},{6,7},{7,6},{8,9},{9,8},{10,11... | collective-permute-start | bytes 4616 | tf_op jit(solution)/shard_map/ppermute | solution.py:27
  372.0 27.3 %copy-start.12 = (bf16[1024,768]{1,0:T(8,128)(2,1)}, bf16[1024,768]{1,0:T(8,128)(2,1)S(1)}, u32[]{:S(2)}) copy-start(bf16[1024,768]{1,0:T(8,128)(2,1)S(1)} %pad_maximum_fusion.2.refs_5_) | copy-start | bytes 4718596
  398.0 4.3 collective-permute-start.14
  403.3 9.1 %collective-permute-start.15 = (bf16[18,8,768]{2,1,0:T(8,128)(2,1)S(1)}, bf16[18,8,768]{2,1,0:T(8,128)(2,1)S(1)}, u32[]{:S(2)}, u32[]{:S(2)}) collective-permute-start(bf16[18,8,768]{2,1,0:T(8,128)(2,1)S(1)} %pad_maximum_fusion.12), channel_id=1, source_target_pairs={{4,0},{6,2},{8,4},{10,6},{12,8},{14,10},{5,1},{7,3},{9,5},{11,7},{... | collective-permute-start | bytes 663560 | tf_op jit(solution)/shard_map/ppermute | solution.py:79
  414.1 15.9 %collective-permute-start.16 = (bf16[18,8,768]{2,1,0:T(8,128)(2,1)}, bf16[18,8,768]{2,1,0:T(8,128)(2,1)}, u32[]{:S(2)}, u32[]{:S(2)}) collective-permute-start(bf16[18,8,768]{2,1,0:T(8,128)(2,1)} %pad_maximum_fusion.13), channel_id=1, source_target_pairs={{8,0},{10,2},{12,4},{14,6},{9,1},{11,3},{13,5},{15,7},{24,16},{26,... | collective-permute-start | bytes 663560 | tf_op jit(solution)/shard_map/ppermute | solution.py:79
  418.0 81.6 %collective-permute-start.18 = (bf16[1024,384]{1,0:T(8,128)(2,1)}, bf16[1024,384]{1,0:T(8,128)(2,1)}, u32[]{:S(2)}, u32[]{:S(2)}) collective-permute-start(bf16[1024,384]{1,0:T(8,128)(2,1)} %get-tuple-element.94), channel_id=1, source_target_pairs={{0,1},{1,0},{2,3},{3,2},{4,5},{5,4},{6,7},{7,6},{8,9},{9,8},{10,11... | collective-permute-start | bytes 2359304 | tf_op jit(solution)/shard_map/ppermute | solution.py:27
  431.8 66.6 %copy-start.44 = (f32[768,22]{0,1:T(8,128)S(1)}, f32[768,22]{0,1:T(8,128)}, u32[]{:S(2)}) copy-start(f32[768,22]{0,1:T(8,128)} %copy-done.43) | copy-start | bytes 202756
  431.8 67.8 %copy-start.22 = (bf16[1024,384]{1,0:T(8,128)(2,1)S(1)}, bf16[1024,384]{1,0:T(8,128)(2,1)}, u32[]{:S(2)}) copy-start(bf16[1024,384]{1,0:T(8,128)(2,1)} %get-tuple-element.94) | copy-start | bytes 2359300
  494.8 8.6 %collective-permute-start.17 = (bf16[1024,128]{1,0:T(8,128)(2,1)}, bf16[1024,128]{1,0:T(8,128)(2,1)S(1)}, u32[]{:S(2)}, u32[]{:S(2)}) collective-permute-start(bf16[1024,128]{1,0:T(8,128)(2,1)} %get-tuple-element.84), channel_id=1, source_target_pairs={{0,1},{1,0},{2,3},{3,2},{4,5},{5,4},{6,7},{7,6},{8,9},{9,8},{10,11... | collective-permute-start | bytes 786440 | tf_op jit(solution)/shard_map/ppermute | solution.py:27
  504.8 4.7 collective-permute-start.19
  510.1 17.5 %copy-start.38 = (f32[768,1]{1,0:T(8,128)S(1)}, f32[768,1]{1,0:T(8,128)}, u32[]{:S(2)}) copy-start(f32[768,1]{1,0:T(8,128)} %copy.252) | copy-start | bytes 9220
  534.6 3.4 collective-permute-start.21
  535.7 20.7 %collective-permute-start.22 = (bf16[512,768]{1,0:T(8,128)(2,1)}, bf16[512,768]{1,0:T(8,128)(2,1)}, u32[]{:S(2)}, u32[]{:S(2)}) collective-permute-start(bf16[512,768]{1,0:T(8,128)(2,1)} %get-tuple-element.105.refs_2_), channel_id=1, source_target_pairs={{0,1},{1,0},{2,3},{3,2},{4,5},{5,4},{6,7},{7,6},{8,9},{9,8},{10,11... | collective-permute-start | bytes 2359304 | tf_op jit(solution)/shard_map/ppermute | solution.py:27
  537.2 19.6 %copy-start.25 = (bf16[16,50,384]{2,0,1:T(8,128)(2,1)S(1)}, bf16[16,50,384]{2,0,1:T(8,128)(2,1)}, u32[]{:S(2)}) copy-start(bf16[16,50,384]{2,0,1:T(8,128)(2,1)} %copy-done.24) | copy-start | bytes 1843204
  537.2 19.6 %copy-start.27 = (bf16[16,50,384]{2,0,1:T(8,128)(2,1)S(1)}, bf16[16,50,384]{2,0,1:T(8,128)(2,1)}, u32[]{:S(2)}) copy-start(bf16[16,50,384]{2,0,1:T(8,128)(2,1)} %copy-done.26) | copy-start | bytes 1843204
  537.2 19.6 %copy-start.58 = (bf16[16,50,1536]{2,1,0:T(8,128)(2,1)S(1)}, bf16[16,50,1536]{2,1,0:T(8,128)(2,1)}, u32[]{:S(2)}) copy-start(bf16[16,50,1536]{2,1,0:T(8,128)(2,1)} %copy-done.57) | copy-start | bytes 7372804
  537.2 35.0 %collective-permute-start.24 = (bf16[512,768]{1,0:T(8,128)(2,1)}, bf16[512,768]{1,0:T(8,128)(2,1)S(1)}, u32[]{:S(2)}, u32[]{:S(2)}) collective-permute-start(bf16[512,768]{1,0:T(8,128)(2,1)} %get-tuple-element.96.refs_0_), channel_id=1, source_target_pairs={{0,1},{1,0},{2,3},{3,2},{4,5},{5,4},{6,7},{7,6},{8,9},{9,8},{10,11... | collective-permute-start | bytes 2359304 | tf_op jit(solution)/shard_map/ppermute | solution.py:27
  556.5 9.3 %collective-permute-start.23 = (bf16[4,48,1024]{2,1,0:T(8,128)(2,1)S(1)}, bf16[4,48,1024]{2,1,0:T(8,128)(2,1)S(1)}, u32[]{:S(2)}, u32[]{:S(2)}) collective-permute-start(bf16[4,48,1024]{2,1,0:T(8,128)(2,1)S(1)} %fusion.77), channel_id=1, source_target_pairs={{0,4},{2,6},{4,0},{6,2},{8,12},{10,14},{12,8},{14,10},{1,5},{3,7},... | collective-permute-start | bytes 1179656 | tf_op jit(solution)/shard_map/ppermute | solution.py:68
  572.2 12.8 %copy-start.21 = (f32[48,1536]{0,1:T(8,128)S(1)}, f32[48,1536]{0,1:T(8,128)}, u32[]{:S(2)}) copy-start(f32[48,1536]{0,1:T(8,128)} %convert_element_type.387) | copy-start | bytes 884740
  572.2 11.1 %collective-permute-start.25 = (bf16[2,48,1024]{2,1,0:T(8,128)(2,1)S(1)}, bf16[2,48,1024]{2,1,0:T(8,128)(2,1)S(1)}, u32[]{:S(2)}, u32[]{:S(2)}) collective-permute-start(bf16[2,48,1024]{2,1,0:T(8,128)(2,1)S(1)} %fusion.83), channel_id=1, source_target_pairs={{0,8},{2,10},{4,12},{6,14},{8,0},{10,2},{12,4},{14,6},{1,9},{3,11}... | collective-permute-start | bytes 589832 | tf_op jit(solution)/shard_map/ppermute | solution.py:68
  583.5 9.8 %collective-permute-start.26 = (bf16[1,48,1024]{2,1,0:T(8,128)(2,1)S(1)}, bf16[1,48,1024]{2,1,0:T(8,128)(2,1)S(1)}, u32[]{:S(2)}, u32[]{:S(2)}) collective-permute-start(bf16[1,48,1024]{2,1,0:T(8,128)(2,1)S(1)} %fusion.89), channel_id=1, source_target_pairs={{0,16},{16,0},{1,17},{17,1},{2,18},{18,2},{3,19},{19,3},{4,20},{20... | collective-permute-start | bytes 294920 | tf_op jit(solution)/shard_map/ppermute | solution.py:68
  595.4 3.6 collective-permute-start.27
  (50 other events, 246.7 us)
Sparse Core Ops, SparseCore 0:
  12.9 42.3 all-gather.2
  58.2 41.1 all-gather.4
  418.1 67.5 reduce-scatter.3

commit v2 on v1

--- a/solution.py
+++ b/solution.py
@@ -32,16 +32,6 @@
     if lax.axis_size("tensor") == 2:
         return sent.astype(F32) + swapped(sent).astype(F32)
     return jnp.sum(lax.all_gather(sent, "tensor").astype(F32), axis=0)
-
-
-def tensor_share(value):
-    peers, here = lax.axis_size("tensor"), lax.axis_index("tensor")
-    share = value.shape[-1] // peers
-    if peers == 2:
-        own = jnp.where(here == 0, value[..., :share], value[..., share:])
-        other = jnp.where(here == 0, value[..., share:], value[..., :share])
-        return own + swapped(other.astype(BF16)).astype(F32)
-    return lax.psum_scatter(value, "tensor", scatter_dimension=value.ndim - 1, tiled=True)
 
 
 def tensor_columns(value):
@@ -68,7 +58,8 @@
         got = lax.ppermute(other, axis, [(i, i ^ bit) for i in range(lax.axis_size(axis))])
         value = own.astype(F32) + got.astype(F32)
         turn = len(bits) - 1 - place
-        if turn < len(beside):
+        if 0 < turn <= len(beside):
+            turn -= 1
             value, beside[turn] = lax.optimization_barrier((value, beside[turn]))
     return value.reshape(rows, value.shape[-1]), beside
 
@@ -79,27 +70,140 @@
     return lax.ppermute(value, "ctx", pairs)
 
 
-def carried(state, log_decay, rates, sign):
-    def sent(parts):
-        high = parts[1].astype(BF16)
-        low = (parts[1] - high.astype(F32)).astype(BF16)
-        both = jnp.concatenate([parts[0].astype(BF16), high[None], low[None]], 0)
-        got = moved(both, sign * (width + 1)).astype(F32)
-        return got[:N], got[N] + got[N + 1]
-
-    def apply(late_log, early):
-        return jnp.exp(late_log[None] * rates[:, None, :]) * early
-
-    width = 0
-    excl = sent((state, log_decay))
-    width = 1
-    peers = lax.axis_size("ctx")
-    while width < peers - 1:
-        incl = (state + apply(log_decay, excl[0]), log_decay + excl[1])
-        got = sent(incl)
-        excl = (excl[0] + apply(excl[1], got[0]), excl[1] + got[1])
-        width = 2 * width + 1
-    return excl[0]
+MESH = pl.DeviceIdType.MESH
+
+
+def greet(peers):
+    barrier = pltpu.get_barrier_semaphore()
+    for peer in peers:
+        pl.semaphore_signal(barrier, inc=1, device_id=peer, device_id_type=MESH)
+    pl.semaphore_wait(barrier, len(peers))
+
+
+def carry_kernel(sign, ranges, peers, end_ref, log_ref, r_ref, *refs):
+    if peers:
+        own_ref, out_ref, others_ref, sent, got, log_out, send_sem, recv_sem, own_sem, others_sem = refs
+    else:
+        out_ref, sent, got, log_out, send_sem, recv_sem = refs
+    turns, groups, _, width = sent.shape
+    seqs = log_ref.shape[0]
+    fsdp, me, tensor = lax.axis_index("fsdp"), lax.axis_index("ctx"), lax.axis_index("tensor")
+
+    def peer(by):
+        return (fsdp, lax.rem(me + by + ranges, ranges), tensor)
+
+    shifts = [sign * (1 << turn) for turn in range(turns)]
+    partners = [(fsdp, me, lax.rem(tensor + by, peers)) for by in range(1, peers)]
+    near = sorted({s % ranges for s in shifts} | {-s % ranges for s in shifts})
+    greet([peer(by) for by in near] + partners)
+    beside = [
+        pltpu.make_async_remote_copy(
+            src_ref=own_ref,
+            dst_ref=others_ref.at[k],
+            send_sem=own_sem.at[k],
+            recv_sem=others_sem.at[k],
+            device_id=partner,
+            device_id_type=MESH,
+        )
+        for k, partner in enumerate(partners)
+    ]
+    for extra in beside:
+        extra.start()
+
+    def copy(turn, group):
+        return pltpu.make_async_remote_copy(
+            src_ref=sent.at[turn, group],
+            dst_ref=got.at[turn, group],
+            send_sem=send_sem.at[turn, group],
+            recv_sem=recv_sem.at[turn, group],
+            device_id=peer(shifts[turn]),
+            device_id_type=MESH,
+        )
+
+    def decayed(log, cols, n):
+        return jnp.exp(log * r_ref[n : n + 1, cols])
+
+    def receive(turn, group):
+        copy(turn, group).wait_recv()
+        cols = slice(group * width, (group + 1) * width)
+        reach = 1 << turn
+        real = (me >= reach) if sign > 0 else (me < ranges - reach)
+
+        def part(k):
+            rows = got[turn, group, k * seqs : (k + 1) * seqs, :].astype(F32)
+            return jnp.where(real, rows, 0.0)
+
+        log = part(N) + part(N + 1)
+        if turn == 0:
+            for n in range(N):
+                out_ref[n, :, cols] = part(n)
+            log_out[:, cols] = log
+        else:
+            late = log_out[:, cols]
+            for n in range(N):
+                out_ref[n, :, cols] = out_ref[n, :, cols] + decayed(late, cols, n) * part(n)
+            log_out[:, cols] = late + log
+
+    for turn in range(turns):
+        for group in range(groups):
+            cols = slice(group * width, (group + 1) * width)
+            own_log = log_ref[:, cols]
+            if turn > 0:
+                receive(turn - 1, group)
+            for n in range(0, N, 2):
+                pair = []
+                for k in (n, n + 1):
+                    value = end_ref[k, :, cols]
+                    if turn > 0:
+                        value = value + decayed(own_log, cols, k) * out_ref[k, :, cols]
+                    pair.append(value)
+                sent[turn, group, n * seqs : (n + 2) * seqs, :] = jnp.concatenate(pair, 0).astype(
+                    BF16
+                )
+            log = own_log if turn == 0 else own_log + log_out[:, cols]
+            high = log.astype(BF16).astype(F32)
+            sent[turn, group, N * seqs :, :] = jnp.concatenate([high, log - high], 0).astype(BF16)
+            copy(turn, group).start()
+    for group in range(groups):
+        receive(turns - 1, group)
+    for turn in range(turns):
+        for group in range(groups):
+            copy(turn, group).wait_send()
+    for extra in beside:
+        extra.wait()
+
+
+def carried(end, log_decay, rates, sign, ident, shared=None):
+    _, seqs, chans = end.shape
+    ranges = lax.axis_size("ctx")
+    turns = (ranges - 1).bit_length()
+    groups = 3 if chans % (3 * LANES) == 0 else 1
+    block = (turns, groups, (N + 2) * seqs, chans // groups)
+    vmem = pl.BlockSpec(memory_space=pltpu.VMEM)
+    anywhere = pl.BlockSpec(memory_space=pl.ANY)
+    peers = 0 if shared is None else lax.axis_size("tensor")
+    state = jax.ShapeDtypeStruct((N, seqs, chans), F32)
+    scratch = [
+        pltpu.VMEM(block, BF16),
+        pltpu.VMEM(block, BF16),
+        pltpu.VMEM((seqs, chans), F32),
+        pltpu.SemaphoreType.DMA((turns, groups)),
+        pltpu.SemaphoreType.DMA((turns, groups)),
+    ]
+    if peers:
+        others = jax.ShapeDtypeStruct((peers - 1, *shared.shape), shared.dtype)
+        scratch += [pltpu.SemaphoreType.DMA((peers - 1,)), pltpu.SemaphoreType.DMA((peers - 1,))]
+    return pl.pallas_call(
+        functools.partial(carry_kernel, sign, ranges, peers),
+        in_specs=[vmem] * 3 + [anywhere] * bool(peers),
+        out_specs=[vmem, anywhere] if peers else vmem,
+        out_shape=[state, others] if peers else state,
+        scratch_shapes=scratch,
+        compiler_params=pltpu.CompilerParams(
+            collective_id=ident, has_side_effects=True, vmem_limit_bytes=32 << 20
+        ),
+        cost_estimate=pl.CostEstimate(flops=20 << 30, bytes_accessed=1 << 20, transcendentals=0),
+    )(end[:N], log_decay, rates, *([shared] if peers else []))
 
 
 def spread_matrix():
@@ -496,7 +600,7 @@
 def output_kernel(shape, peers, *refs):
     micros, group = shape
     early, late, refs = refs[:peers], refs[peers : 2 * peers], refs[2 * peers :]
-    x_ref, dres_ref, act_in_ref, gain_ref, grad_ref, act_ref, grad_tok, act_tok = refs
+    x_ref, dres_ref, act_own_ref, act_others_ref, gain_ref, grad_ref, act_ref, grad_tok, act_tok = refs
     x = x_ref[...].astype(F32)
     scale = lax.rsqrt(jnp.mean(x * x, -1, keepdims=True) + EPS)
     xhat = x * scale
@@ -510,7 +614,15 @@
     seqs = micros * group
     rows, width = x.shape
     count = rows // seqs
-    act = act_in_ref[...].astype(F32)
+    tensor = lax.axis_index("tensor")
+    pieces = []
+    for owner in range(peers):
+        piece = act_own_ref[...].astype(F32)
+        for by in range(1, peers):
+            here = lax.rem(tensor + peers - by, peers) == owner
+            piece = jnp.where(here, act_others_ref[by - 1].astype(F32), piece)
+        pieces.append(piece)
+    act = jnp.concatenate(pieces, 1)
     for k in range(width // LANES):
         grad_tok[k] = grad[:, lanes(k)]
         act_tok[k] = act[:, lanes(k)]
@@ -619,7 +731,8 @@
     def swap_owners(value):
         return lax.all_to_all(value, OWNERS, split_axis=0, concat_axis=0, tiled=True)
 
-    grad_packed = packed(grad_tok)
+    full, grad_packed = lax.optimization_barrier((full, packed(grad_tok)))
+    grad_rows_raw = swap_owners(grad_packed)
 
     w_in = full[:, :width]
     tail = full[:, width:]
@@ -687,10 +800,9 @@
         [wide_rates, (tokens, N * LANES)],
         cost=cost(length, 6),
     )
-    state_end, log_decay = end[:N], end[N]
-    state = carried(state_end, log_decay, rates, 1)
-    state, grad_packed = lax.optimization_barrier((state, grad_packed))
-    grad_rows_raw = swap_owners(grad_packed)
+    end, grad_rows_raw = lax.optimization_barrier((end, grad_rows_raw))
+    log_decay = end[N]
+    state = carried(end, log_decay, rates, 1, 0)
     pieces = 4 if length % (4 * BLK) == 0 else 1
     steps = length // pieces
     y_parts, gated_parts, mixed_parts, start_parts = [], [], [], []
@@ -699,8 +811,6 @@
             state, mixed_parts[piece - 2] = lax.optimization_barrier(
                 (state, mixed_parts[piece - 2])
             )
-        if piece == pieces - 1:
-            state, grad_rows_raw = lax.optimization_barrier((state, grad_rows_raw))
         y_part, gated_part, mixed_part, start_part, state = call(
             forward_kernel,
             [
@@ -760,14 +870,29 @@
     def product(a, b, terms):
         return jnp.einsum(terms, a, b, preferred_element_type=F32)
 
+    def shared(value, matrix, terms, axis):
+        if peers > 2:
+            total = product(value, matrix, terms)
+            share = lax.psum_scatter(total, "tensor", scatter_dimension=2, tiled=True)
+            return share.astype(BF16), value
+        low, high = jnp.split(matrix, 2, axis)
+        sent = product(value, jnp.where(here == 0, high, low), terms).astype(BF16)
+        value, sent = lax.optimization_barrier((value, sent))
+        own = product(value, jnp.where(here == 0, low, high), terms)
+        return (own + swapped(sent).astype(F32)).astype(BF16), sent
+
     hidden = product(x_rows, up, "srd,df->srf")
     act_float, gelu_pull = jax.vjp(lambda v: jax.nn.gelu(v, approximate=True), hidden)
     act = act_float.astype(BF16)
-    back_y = swap_owners(tensor_share(product(act, down, "srf,fd->srd")).astype(BF16))
+    share_y, sent_y = shared(act, down, "srf,fd->srd", 1)
+    grad_rows, _ = lax.optimization_barrier((grad_rows, sent_y))
     d_hidden = gelu_pull(product(grad_rows, down, "srd,fd->srf"))[0].astype(BF16)
-    back_x = swap_owners(tensor_share(product(d_hidden, up, "srf,df->srd")).astype(BF16))
+    back_y = swap_owners(share_y)
+    share_x, _ = shared(d_hidden, up, "srf,df->srd", 0)
+    back_x = swap_owners(share_x)
     grad_up = product(x_rows, d_hidden, "srd,srf->df")
     grad_down = product(act, grad_rows, "srf,srd->fd")
+    back_x, grad_up, grad_down = lax.optimization_barrier((back_x, grad_up, grad_down))
     expert_y = unpacked(back_y)
     expert_dx = unpacked(back_x)
     x_half = half(xhat2)
@@ -791,8 +916,6 @@
     act_half = (valid * (half(resid) + gate * expert_y)).astype(BF16)
 
     d_mixed = tensor_columns(d_resid_half.astype(BF16))
-    d_mixed, act_half = lax.optimization_barrier((d_mixed, act_half))
-    activations = tensor_columns(act_half)
     d_gated = dot(d_mixed, w_out, NT)
     d_y = d_gated * silu_z
     [start_grad] = call(
@@ -812,7 +935,7 @@
     mine_early = owned(
         jnp.concatenate([dot(d_gate_z, normed1, TN), dot(gated, d_mixed, TN)], 1)
     )
-    grad_end = carried(start_grad, log_decay, rates, -1)
+    grad_end, act_others = carried(start_grad, log_decay, rates, -1, 1, act_half)
     w_step_wide = jnp.pad(w_step, ((0, 0), (0, LANES - R)))
     d_step, du_part, d_proj_part, rate_grad, bias_sums, skip_sums = call(
         backward_kernel,
@@ -851,7 +974,7 @@
         ],
         cost=cost(length, 24),
     )
-    d_step, mine_early, activations = lax.optimization_barrier((d_step, mine_early, activations))
+    d_step, mine_early = lax.optimization_barrier((d_step, mine_early))
     d_proj = tensor_total(d_proj_part, BF16).astype(BF16)
     step_bias_grad = jnp.sum(bias_sums, 0)
     skip_grad = jnp.sum(skip_sums, 0)
@@ -959,7 +1082,13 @@
     arrays = (
         [early_rows(part) for part in early_parts]
         + [late_rows(part) for part in late_parts]
-        + [rows_of(x_tok), rows_of(d_mixed), rows_of(activations), whole(gains[:1])]
+        + [
+            rows_of(x_tok),
+            rows_of(d_mixed),
+            rows_of(act_half),
+            (act_others, pl.BlockSpec((peers - 1, block, share), lambda i: (0, i, 0))),
+            whole(gains[:1]),
+        ]
     )
     out_spec = pl.BlockSpec((micros, group, steps, width), lambda i: (0, 0, i, 0))
     input_grad, activations = pl.pallas_call(

time: 616 us -> 594 us (0.964)
  Pallas kernels: 152 us -> 196 us
  waiting for transfers between devices: 189 us -> 145 us
  starting transfers between devices: 73.2 us -> 47.9 us
    ppermute x16 -> x15, waiting for transfers between devices: 95.2 us -> 50.1 us  [swapped(): return lax.ppermute(value, 'tensor', [(0, 1), (1, 0)])]
    pallas_call x0 -> x2, Pallas kernels: none -> 42.9 us  [carried(): pl.pallas_call(functools.partial(carry_kernel, sign, ranges, peers), in_s...]
    ppermute x8 -> x2, waiting for transfers between devices: 23.6 us -> 0.79 us  [moved(): return lax.ppermute(value, 'ctx', pairs)]
    ppermute x8 -> x2, starting transfers between devices: 19.2 us -> 3.45 us  [moved(): return lax.ppermute(value, 'ctx', pairs)]
    all_to_all x5, waiting for transfers between devices: 26.8 us -> 40.1 us  [swap_owners(): lax.all_to_all(value, OWNERS, split_axis=0, concat_axis=0, tiled=True)]
    ppermute x4, waiting for transfers between devices: 9.42 us -> 18.7 us  [halved(): lax.ppermute(other, axis, [(i, i ^ bit) for i in range(lax.axis_size(axis...]
    ppermute x16 -> x15, starting transfers between devices: 20.8 us -> 12.8 us  [swapped(): return lax.ppermute(value, 'tensor', [(0, 1), (1, 0)])]
    convert_element_type x18 -> x1, other arithmetic: 9.03 us -> 1.78 us  [per_device(): (jnp.swapaxes(gate_rows, 1, 2) * grad_rows_raw.astype(F32)).astype(BF16)]
  transfers between devices with their start and end apart: 36 -> 29, of which waited for: 22 -> 22; matrix products, arithmetic and copies ran while one was open for 20% -> 21% of each run, Pallas kernels for 20% -> 24%
where the time goes in v2:
time: 594 us; the launch traced here: 585 us
  Pallas kernels  196 us (33%)
  waiting for transfers between devices  145 us (24%)
  matrix products  70.6 us (12%)
  local copies, waits for them, and re-layouts  57.1 us (10%)
  other arithmetic  52.9 us (9%)
  starting transfers between devices  47.9 us (8%)
  between operations  15.6 us (3%)
    pallas_call x7, Pallas kernels, scan_call(): pl.pallas_call(kernel, grid=(chans // width,), in_specs=[spec(shape, kind...  130 us
    ppermute x15, waiting for transfers between devices, swapped(): return lax.ppermute(value, 'tensor', [(0, 1), (1, 0)])  50.1 us
    pallas_call x2, Pallas kernels, carried(): pl.pallas_call(functools.partial(carry_kernel, sign, ranges, peers), in_s...  42.9 us
    all_to_all x5, waiting for transfers between devices, swap_owners(): lax.all_to_all(value, OWNERS, split_axis=0, concat_axis=0, tiled=True)  40.1 us
    dot_general x8, matrix products, product(): return jnp.einsum(terms, a, b, preferred_element_type=F32)  32.7 us
    dot_general x13, matrix products, dot(): return lax.dot_general(a, b, dims, preferred_element_type=F32)  31.6 us
    all_gather x1, waiting for transfers between devices, per_device(): full = lax.all_gather(first, OWNERS, axis=0, tiled=True)  28.2 us
    all_to_all x5, starting transfers between devices, swap_owners(): lax.all_to_all(value, OWNERS, split_axis=0, concat_axis=0, tiled=True)  25.5 us
  transfers between devices with their start and end apart: 29, of which 22 were waited for; matrix products, arithmetic and copies ran while one was open for 21% of the time, Pallas kernels for 24%

profile of v2, /device:TPU:0, one launch (start us, length us, event | category | flops | bytes accessed | tf_op | source)
XLA Modules:
  0.0 584.5 jit_solution(5270963306294254249)
XLA Ops:
  22.8 4.3 fusion.35
  27.1 28.2 %all-gather.3.cloned.1.call-done = bf16[768,1024]{1,0:T(8,128)(2,1)} async-done(((bf16[48,1024]{1,0:T(8,128)(2,1)}), bf16[768,1024]{1,0:T(8,128)(2,1)}) %all-gather.3.cloned.1.call-update) | async-done | bytes 1572880 | tf_op jit(solution)/shard_map/all_gather | solution.py:707
  66.5 3.7 fusion.131
  74.1 7.6 %all-to-all-start = ((bf16[16,50,768]{2,1,0:T(8,128)(2,1)}), bf16[16,50,768]{2,1,0:T(8,128)(2,1)}, u32[]{:S(2)}, u32[]{:S(2)}) async-start(bf16[16,50,768]{2,1,0:T(8,128)(2,1)} %fusion.35), calls=%async_computation | async-start | bytes 2752512 | tf_op jit(solution)/shard_map/all_to_all | solution.py:732
  83.3 5.1 add_divide_fusion
  88.3 16.5 %shard_map.238 = f32[17,8,768]{2,1,0:T(8,128)} custom-call(f32[1024,768]{1,0:T(8,128)} %get-tuple-element.209.d_ref, f32[1024,768]{1,0:T(8,128)} %get-tuple-element.203.u_ref, f32[1024,16]{1,0:T(8,128)} %get-tuple-element.223.b_ref, f32[16,768]{1,0:T(8,128)} %fusion.106.r_ref), custom_call_target="tpu_custom_call" | custom-call | flops 22649241600 | bytes 12582912 | tf_op jit(solution)/shard_map/pallas_call | solution.py:651
  104.9 6.8 %all-gather.5.cloned.1.call-done = bf16[768,1536]{1,0:T(8,128)(2,1)} async-done(((bf16[48,1536]{1,0:T(8,128)(2,1)}), bf16[768,1536]{1,0:T(8,128)(2,1)}) %all-gather.5.cloned.1.call-update) | async-done | bytes 2359312 | tf_op jit(solution)/shard_map/all_gather | solution.py:708
  111.7 3.3 fusion.133
  115.1 3.1 fusion.128.z_ref
  118.2 4.2 all-to-all-done
  122.5 22.3 %shard_map.239.h0_ref = f32[16,8,768]{2,1,0:T(8,128)S(1)} custom-call(f32[16,8,768]{2,1,0:T(8,128)S(1)} %slice.267.end_ref, f32[8,768]{1,0:T(8,128)S(1)} %slice_bitcast_fusion.7.log_ref, f32[16,768]{1,0:T(8,128)S(1)} %copy-done.2), custom_call_target="tpu_custom_call" | custom-call | flops 21474836480 | bytes 1048576 | tf_op jit(solution)/shard_map/pallas_call | solution.py:196
  145.6 8.4 %shard_map.240 = (f32[256,768]{1,0:T(8,128)}, bf16[256,768]{1,0:T(8,128)(2,1)}, bf16[256,768]{1,0:T(8,128)(2,1)}, f32[4,16,8,768]{3,2,1,0:T(8,128)}, f32[16,8,768]{2,1,0:T(8,128)}) custom-call(f32[1024,768]{1,0:T(8,128)} %get-tuple-element.209.d_ref, f32[1024,768]{1,0:T(8,128)} %get-tuple-element.203.u_ref, f32[1024,768]{1,0:T(8,128)} %fusion.128.z_ref, ...), custom_call_target="tpu_custom_call" | custom-call | flops 9437184000 | bytes 3145728 | tf_op jit(solution)/shard_map/pallas_call | solution.py:651
  154.7 8.4 %shard_map.241 = (f32[256,768]{1,0:T(8,128)}, bf16[256,768]{1,0:T(8,128)(2,1)}, bf16[256,768]{1,0:T(8,128)(2,1)}, f32[4,16,8,768]{3,2,1,0:T(8,128)}, f32[16,8,768]{2,1,0:T(8,128)}) custom-call(f32[1024,768]{1,0:T(8,128)} %get-tuple-element.209.d_ref, f32[1024,768]{1,0:T(8,128)} %get-tuple-element.203.u_ref, f32[1024,768]{1,0:T(8,128)} %fusion.128.z_ref, ...), custom_call_target="tpu_custom_call" | custom-call | flops 9437184000 | bytes 3145728 | tf_op jit(solution)/shard_map/pallas_call | solution.py:651
  167.4 8.4 %shard_map.242 = (f32[256,768]{1,0:T(8,128)}, bf16[256,768]{1,0:T(8,128)(2,1)}, bf16[256,768]{1,0:T(8,128)(2,1)}, f32[4,16,8,768]{3,2,1,0:T(8,128)}, f32[16,8,768]{2,1,0:T(8,128)}) custom-call(f32[1024,768]{1,0:T(8,128)} %get-tuple-element.209.d_ref, f32[1024,768]{1,0:T(8,128)} %get-tuple-element.203.u_ref, f32[1024,768]{1,0:T(8,128)} %fusion.128.z_ref, ...), custom_call_target="tpu_custom_call" | custom-call | flops 9437184000 | bytes 3145728 | tf_op jit(solution)/shard_map/pallas_call | solution.py:651
  177.8 8.5 %shard_map.243 = (f32[256,768]{1,0:T(8,128)}, bf16[256,768]{1,0:T(8,128)(2,1)}, bf16[256,768]{1,0:T(8,128)(2,1)}, f32[4,16,8,768]{3,2,1,0:T(8,128)}, f32[16,8,768]{2,1,0:T(8,128)}) custom-call(f32[1024,768]{1,0:T(8,128)} %get-tuple-element.209.d_ref, f32[1024,768]{1,0:T(8,128)} %get-tuple-element.203.u_ref, f32[1024,768]{1,0:T(8,128)} %fusion.128.z_ref, ...), custom_call_target="tpu_custom_call" | custom-call | flops 9437184000 | bytes 3145728 | tf_op jit(solution)/shard_map/pallas_call | solution.py:651
  188.4 10.3 %collective-permute-done.5 = bf16[256,768]{1,0:T(8,128)(2,1)} collective-permute-done((bf16[256,768]{1,0:T(8,128)(2,1)}, bf16[256,768]{1,0:T(8,128)(2,1)}, u32[]{:S(2)}, u32[]{:S(2)}) %collective-permute-start.5) | collective-permute-done | bytes 393248 | tf_op jit(solution)/shard_map/ppermute | solution.py:27
  199.9 5.4 collective-permute-done.4
  212.7 4.9 all-to-all-start.2
  219.7 15.2 %all-to-all-done.2 = bf16[16,50,384]{2,1,0:T(8,128)(2,1)} async-done(((bf16[16,50,384]{2,1,0:T(8,128)(2,1)}), bf16[16,50,384]{2,1,0:T(8,128)(2,1)}, u32[]{:S(2)}, u32[]{:S(2)}) %all-to-all-start.2) | async-done | bytes 614432 | tf_op jit(solution)/shard_map/all_to_all | solution.py:732
  238.9 4.3 all-to-all-start.1
  243.7 5.8 all-to-all-done.1
  255.2 3.2 multiply_convert_fusion
  261.0 5.9 %fusion.14 = bf16[16,50,1536]{2,1,0:T(8,128)(2,1)S(1)} fusion(f32[16,50,1536]{2,1,0:T(8,128)S(1)} %get-tuple-element.236, bf16[16,50,768]{2,1,0:T(8,128)(2,1)S(1)} %multiply_convert_fusion.3, bf16[1,1536,768]{2,1,0:T(8,128)(2,1)S(1)} %copy-done.71), kind=kOutput, calls=%fused_computation.19 | convolution fusion | flops 1912012800 | bytes 10960896 | tf_op jit(solution)/shard_map/srd,fd->srf/dot_general | solution.py:871
  274.6 11.8 %collective-permute-done.7 = bf16[16,50,384]{2,0,1:T(8,128)(2,1)} collective-permute-done((bf16[16,50,384]{2,0,1:T(8,128)(2,1)}, bf16[16,50,384]{2,0,1:T(8,128)(2,1)}, u32[]{:S(2)}, u32[]{:S(2)}) %collective-permute-start.7) | collective-permute-done | bytes 614432 | tf_op jit(solution)/shard_map/ppermute | solution.py:27
  286.4 3.5 add_convert_fusion.2
  290.0 4.4 all-to-all-start.3
  294.5 6.8 %convolution_bitcast_fusion = f32[1536,768]{1,0:T(8,128)} fusion(bf16[16,50,1536]{2,1,0:T(8,128)(2,1)} %copy-done.75, bf16[16,50,768]{2,1,0:T(8,128)(2,1)S(1)} %multiply_convert_fusion.3), kind=kOutput, calls=%fused_computation.24 | convolution fusion | flops 1887436800 | bytes 8404992 | tf_op jit(solution)/shard_map/srf,srd->fd/dot_general | solution.py:871
  301.3 3.7 add_convert_fusion.1
  305.0 6.8 %all-to-all-done.3 = bf16[16,50,384]{2,1,0:T(8,128)(2,1)} async-done(((bf16[16,50,384]{2,1,0:T(8,128)(2,1)}), bf16[16,50,384]{2,1,0:T(8,128)(2,1)}, u32[]{:S(2)}, u32[]{:S(2)}) %all-to-all-start.3) | async-done | bytes 614432 | tf_op jit(solution)/shard_map/all_to_all | solution.py:732
  311.7 4.3 all-to-all-start.4
  316.2 5.5 convolution_bitcast_fusion.1
  321.6 3.7 fusion.52
  325.4 8.1 %all-to-all-done.4 = bf16[16,50,384]{2,1,0:T(8,128)(2,1)} async-done(((bf16[16,50,384]{2,1,0:T(8,128)(2,1)}), bf16[16,50,384]{2,1,0:T(8,128)(2,1)}, u32[]{:S(2)}, u32[]{:S(2)}) %all-to-all-start.4) | async-done | bytes 614432 | tf_op jit(solution)/shard_map/all_to_all | solution.py:732
  351.8 5.5 pad_maximum_fusion.st_ref
  360.6 3.0 collective-permute-done.10
  364.9 4.4 fusion.23
  369.3 16.5 %shard_map.244.end_ref = f32[16,8,768]{2,1,0:T(8,128)} custom-call(f32[1024,768]{1,0:T(8,128)} %get-tuple-element.209.d_ref, f32[1024,768]{1,0:T(8,128)} %get-tuple-element.207.dy_ref, f32[1024,16]{1,0:T(8,128)} %get-tuple-element.222.c_ref, f32[16,768]{1,0:T(8,128)} %fusion.106.r_ref), custom_call_target="tpu_custom_call" | custom-call | flops 22649241600 | bytes 12582912 | tf_op jit(solution)/shard_map/pallas_call | solution.py:651
  385.9 3.5 convolution_convert_fusion.1
  392.5 4.3 copy.186
  396.9 20.5 %shard_map.245 = (f32[16,8,768]{2,1,0:T(8,128)S(1)}, bf16[1,1024,384]{2,1,0:T(8,128)(2,1)S(1)}) custom-call(f32[16,8,768]{2,1,0:T(8,128)S(1)} %copy-done.7, f32[8,768]{1,0:T(8,128)S(1)} %copy-done.5, f32[16,768]{1,0:T(8,128)S(1)} %copy-done.3, bf16[1024,384]{1,0:T(8,128)(2,1)S(1)} %get-tuple-element.214.refs_0_.refs_6_), custom_call_target="tpu_custom_call" | custom-call | flops 21474836480 | bytes 1048576 | tf_op jit(solution)/shard_map/pallas_call | solution.py:196
  419.1 62.9 %shard_map.246 = (bf16[1024,768]{1,0:T(8,128)(2,1)}, f32[1024,768]{1,0:T(8,128)}, bf16[1024,128]{1,0:T(8,128)(2,1)}, f32[16,8,768]{2,1,0:T(8,128)}, f32[8,768]{1,0:T(8,128)}, /*index=5*/f32[8,768]{1,0:T(8,128)}) custom-call(f32[1024,768]{1,0:T(8,128)} %get-tuple-element.209.d_ref, f32[1024,768]{1,0:T(8,128)} %get-tuple-element.203.u_ref, ...), custom_call_target="tpu_custom_call" | custom-call | flops 90596966400 | bytes 12582912 | tf_op jit(solution)/shard_map/pallas_call | solution.py:651
  484.5 6.7 %collective-permute-done.11 = bf16[1024,128]{1,0:T(8,128)(2,1)S(1)} collective-permute-done((bf16[1024,128]{1,0:T(8,128)(2,1)}, bf16[1024,128]{1,0:T(8,128)(2,1)S(1)}, u32[]{:S(2)}, u32[]{:S(2)}) %collective-permute-start.11) | collective-permute-done | bytes 262176 | tf_op jit(solution)/shard_map/ppermute | solution.py:27
  498.9 15.8 %shard_map.247 = (bf16[512,768]{1,0:T(8,128)(2,1)}, bf16[512,768]{1,0:T(8,128)(2,1)}, f32[768,768]{1,0:T(8,128)}, f32[768,128]{1,0:T(8,128)}, f32[768,48]{1,0:T(...) custom-call(f32[1024,768]{1,0:T(8,128)} %get-tuple-element.96.du_ref, bf16[1024,128]{1,0:T(8,128)(2,1)} %copy-done.45, ...), custom_call_target="tpu_custom_call" | custom-call | tf_op jit(solution)/shard_map/pallas_call | solution.py:1028
  516.8 3.5 concatenate.55
  533.0 9.8 %collective-permute-done.15 = bf16[4,48,1024]{2,1,0:T(8,128)(2,1)S(1)} collective-permute-done((bf16[4,48,1024]{2,1,0:T(8,128)(2,1)S(1)}, bf16[4,48,1024]{2,1,0:T(8,128)(2,1)S(1)}, u32[]{:S(2)}, u32[]{:S(2)}) %collective-permute-start.15) | collective-permute-done | bytes 393248 | tf_op jit(solution)/shard_map/ppermute | solution.py:58
  548.9 7.1 %collective-permute-done.17 = bf16[2,48,1024]{2,1,0:T(8,128)(2,1)S(1)} collective-permute-done((bf16[2,48,1024]{2,1,0:T(8,128)(2,1)S(1)}, bf16[2,48,1024]{2,1,0:T(8,128)(2,1)S(1)}, u32[]{:S(2)}, u32[]{:S(2)}) %collective-permute-start.17) | collective-permute-done | bytes 196640 | tf_op jit(solution)/shard_map/ppermute | solution.py:58
  556.0 5.3 collective-permute-done.18.refs_1_
  563.9 7.4 %shard_map.248 = (f32[2,4,128,768]{3,2,1,0:T(8,128)}, bf16[2,4,128,768]{3,2,1,0:T(8,128)(2,1)}) custom-call(bf16[512,768]{1,0:T(8,128)(2,1)} %get-tuple-element.108.refs_0_, bf16[512,768]{1,0:T(8,128)(2,1)} %collective-permute-done.18.refs_1_, bf16[512,768]{1,0:T(8,128)(2,1)} %get-tuple-element.117.refs_2_, ...), custom_call_target="tpu_custom_call" | custom-call | tf_op jit(solution)/shard_map/pallas_call | solution.py:1094
  (340 shorter events, 140.4 us)
Async XLA Ops:
  7.2 48.1 %all-gather.3.cloned.1.call-start = ((), (), s32[]{:S(2)}) async-start(), calls=%async_computation.6 | async-start | bytes 1671168 | tf_op jit(solution)/shard_map/all_gather | solution.py:707
  12.7 99.0 %all-gather.5.cloned.1.call-start = ((), (), s32[]{:S(2)}) async-start(), calls=%async_computation.7 | async-start | bytes 2506752 | tf_op jit(solution)/shard_map/all_gather | solution.py:708
  22.3 39.0 %copy-start.10 = (bf16[1024,768]{1,0:T(8,128)(2,1)}, bf16[1024,768]{1,0:T(8,128)(2,1)S(1)}, u32[]{:S(2)}) copy-start(bf16[1024,768]{1,0:T(8,128)(2,1)S(1)} %reshape.279.x_ref.refs_4_) | copy-start | bytes 4718596
  63.2 3.0 collective-permute-start
  71.9 10.0 %collective-permute-start.1 = (bf16[1024,80]{1,0:T(8,128)(2,1)S(1)}, bf16[1024,80]{1,0:T(8,128)(2,1)S(1)}, u32[]{:S(2)}, u32[]{:S(2)}) collective-permute-start(bf16[1024,80]{1,0:T(8,128)(2,1)S(1)} %convolution_convert_fusion.4), channel_id=1, source_target_pairs={{0,1},{1,0},{2,3},{3,2},{4,5},{5,4},{6,7},{7,6},{8,9},{9,8},{10,11... | collective-permute-start | bytes 491528 | tf_op jit(solution)/shard_map/ppermute | solution.py:27
  74.1 48.4 %all-to-all-start = ((bf16[16,50,768]{2,1,0:T(8,128)(2,1)}), bf16[16,50,768]{2,1,0:T(8,128)(2,1)}, u32[]{:S(2)}, u32[]{:S(2)}) async-start(bf16[16,50,768]{2,1,0:T(8,128)(2,1)} %fusion.35), calls=%async_computation | async-start | bytes 2752512 | tf_op jit(solution)/shard_map/all_to_all | solution.py:732
  122.5 22.3 %copy-start.4 = (f32[8,768]{1,0:T(8,128)}, f32[8,768]{1,0:T(8,128)S(1)}, u32[]{:S(2)}) copy-start(f32[8,768]{1,0:T(8,128)S(1)} %slice_bitcast_fusion.7.log_ref) | copy-start | bytes 73732
  154.0 11.4 %collective-permute-start.2 = (bf16[256,768]{1,0:T(8,128)(2,1)}, bf16[256,768]{1,0:T(8,128)(2,1)}, u32[]{:S(2)}, u32[]{:S(2)}) collective-permute-start(bf16[256,768]{1,0:T(8,128)(2,1)} %get-tuple-element.75), channel_id=1, source_target_pairs={{0,1},{1,0},{2,3},{3,2},{4,5},{5,4},{6,7},{7,6},{8,9},{9,8},{10,11... | collective-permute-start | bytes 1179656 | tf_op jit(solution)/shard_map/ppermute | solution.py:27
  163.1 12.7 %collective-permute-start.3 = (bf16[256,768]{1,0:T(8,128)(2,1)}, bf16[256,768]{1,0:T(8,128)(2,1)}, u32[]{:S(2)}, u32[]{:S(2)}) collective-permute-start(bf16[256,768]{1,0:T(8,128)(2,1)} %get-tuple-element.79), channel_id=1, source_target_pairs={{0,1},{1,0},{2,3},{3,2},{4,5},{5,4},{6,7},{7,6},{8,9},{9,8},{10,11... | collective-permute-start | bytes 1179656 | tf_op jit(solution)/shard_map/ppermute | solution.py:27
  186.3 20.1 %copy-start.11 = (bf16[1024,768]{1,0:T(8,128)(2,1)S(1)}, bf16[1024,768]{1,0:T(8,128)(2,1)}, u32[]{:S(2)}) copy-start(bf16[1024,768]{1,0:T(8,128)(2,1)} %copy-done.10) | copy-start | bytes 4718596
  186.3 12.4 %collective-permute-start.5 = (bf16[256,768]{1,0:T(8,128)(2,1)}, bf16[256,768]{1,0:T(8,128)(2,1)}, u32[]{:S(2)}, u32[]{:S(2)}) collective-permute-start(bf16[256,768]{1,0:T(8,128)(2,1)} %get-tuple-element.83), channel_id=1, source_target_pairs={{0,1},{1,0},{2,3},{3,2},{4,5},{5,4},{6,7},{7,6},{8,9},{9,8},{10,11... | collective-permute-start | bytes 1179656 | tf_op jit(solution)/shard_map/ppermute | solution.py:27
  187.0 18.3 %collective-permute-start.4 = (bf16[256,768]{1,0:T(8,128)(2,1)S(1)}, bf16[256,768]{1,0:T(8,128)(2,1)}, u32[]{:S(2)}, u32[]{:S(2)}) collective-permute-start(bf16[256,768]{1,0:T(8,128)(2,1)S(1)} %copy-done.52), channel_id=1, source_target_pairs={{0,1},{1,0},{2,3},{3,2},{4,5},{5,4},{6,7},{7,6},{8,9},{9,8},{10,11... | collective-permute-start | bytes 1179656 | tf_op jit(solution)/shard_map/ppermute | solution.py:27
  188.4 18.0 %copy-start.27 = (f32[256,768]{1,0:T(8,128)S(1)}, f32[256,768]{1,0:T(8,128)}, u32[]{:S(2)}) copy-start(f32[256,768]{1,0:T(8,128)} %convert_add_fusion.4) | copy-start | bytes 2359300
  188.4 18.0 %copy-start.28 = (f32[256,768]{1,0:T(8,128)S(1)}, f32[256,768]{1,0:T(8,128)}, u32[]{:S(2)}) copy-start(f32[256,768]{1,0:T(8,128)} %convert_add_fusion.3) | copy-start | bytes 2359300
  212.7 30.5 %copy-start.17 = (bf16[128,2,4,768]{3,2,1,0:T(4,128)(2,1)S(1)}, bf16[128,2,4,768]{3,2,1,0:T(4,128)(2,1)}, u32[]{:S(2)}) copy-start(bf16[128,2,4,768]{3,2,1,0:T(4,128)(2,1)} %copy-done.16) | copy-start | bytes 4718596
  212.7 22.2 %all-to-all-start.2 = ((bf16[16,50,384]{2,1,0:T(8,128)(2,1)}), bf16[16,50,384]{2,1,0:T(8,128)(2,1)}, u32[]{:S(2)}, u32[]{:S(2)}) async-start(bf16[16,50,384]{2,1,0:T(8,128)(2,1)} %fusion.58), calls=%async_computation.2 | async-start | bytes 1376256 | tf_op jit(solution)/shard_map/all_to_all | solution.py:732
  219.6 24.0 %copy-start.73 = (s32[2,4]{1,0:T(2,128)S(1)}, s32[2,4]{1,0:T(2,128)}, u32[]{:S(2)}) copy-start(s32[2,4]{1,0:T(2,128)} %param.17) | copy-start | bytes 100
  236.9 16.8 %collective-permute-start.6 = (bf16[16,50,384]{2,0,1:T(8,128)(2,1)}, bf16[16,50,384]{2,0,1:T(8,128)(2,1)}, u32[]{:S(2)}, u32[]{:S(2)}) collective-permute-start(bf16[16,50,384]{2,0,1:T(8,128)(2,1)} %copy.156), channel_id=1, source_target_pairs={{0,1},{1,0},{2,3},{3,2},{4,5},{5,4},{6,7},{7,6},{8,9},{9,8},{10,11... | collective-permute-start | bytes 1843208 | tf_op jit(solution)/shard_map/ppermute | solution.py:27
  238.9 10.6 %all-to-all-start.1 = ((f32[16,1,50]{2,1,0:T(1,128)}), f32[16,1,50]{2,1,0:T(1,128)S(1)}, u32[]{:S(2)}, u32[]{:S(2)}) async-start(f32[16,1,50]{2,1,0:T(1,128)} %bitcast.13), calls=%async_computation.1 | async-start | bytes 16384 | tf_op jit(solution)/shard_map/all_to_all | solution.py:732
  269.4 17.0 %collective-permute-start.7 = (bf16[16,50,384]{2,0,1:T(8,128)(2,1)}, bf16[16,50,384]{2,0,1:T(8,128)(2,1)}, u32[]{:S(2)}, u32[]{:S(2)}) collective-permute-start(bf16[16,50,384]{2,0,1:T(8,128)(2,1)} %copy.159), channel_id=1, source_target_pairs={{0,1},{1,0},{2,3},{3,2},{4,5},{5,4},{6,7},{7,6},{8,9},{9,8},{10,11... | collective-permute-start | bytes 1843208 | tf_op jit(solution)/shard_map/ppermute | solution.py:27
  270.2 16.2 %copy-start.36 = (bf16[16,50,1536]{2,1,0:T(8,128)(2,1)S(1)}, bf16[16,50,1536]{2,1,0:T(8,128)(2,1)}, u32[]{:S(2)}) copy-start(bf16[16,50,1536]{2,1,0:T(8,128)(2,1)} %copy-done.35) | copy-start | bytes 7372804
  270.2 16.2 %copy-start.70 = (bf16[1,768,1536]{2,1,0:T(8,128)(2,1)S(1)}, bf16[1,768,1536]{2,1,0:T(8,128)(2,1)}, u32[]{:S(2)}) copy-start(bf16[1,768,1536]{2,1,0:T(8,128)(2,1)} %param.28) | copy-start | bytes 7077892
  273.2 28.0 %collective-permute-start.8 = (bf16[16,50,384]{2,0,1:T(8,128)(2,1)}, bf16[16,50,384]{2,0,1:T(8,128)(2,1)}, u32[]{:S(2)}, u32[]{:S(2)}) collective-permute-start(bf16[16,50,384]{2,0,1:T(8,128)(2,1)} %copy.161), channel_id=1, source_target_pairs={{0,1},{1,0},{2,3},{3,2},{4,5},{5,4},{6,7},{7,6},{8,9},{9,8},{10,11... | collective-permute-start | bytes 1843208 | tf_op jit(solution)/shard_map/ppermute | solution.py:27
  290.0 21.8 %all-to-all-start.3 = ((bf16[16,50,384]{2,1,0:T(8,128)(2,1)}), bf16[16,50,384]{2,1,0:T(8,128)(2,1)}, u32[]{:S(2)}, u32[]{:S(2)}) async-start(bf16[16,50,384]{2,1,0:T(8,128)(2,1)} %add_convert_fusion.2), calls=%async_computation.3 | async-start | bytes 1376256 | tf_op jit(solution)/shard_map/all_to_all | solution.py:732
  301.2 14.9 %copy-start.37 = (bf16[16,50,1536]{2,1,0:T(8,128)(2,1)S(1)}, bf16[16,50,1536]{2,1,0:T(8,128)(2,1)}, u32[]{:S(2)}) copy-start(bf16[16,50,1536]{2,1,0:T(8,128)(2,1)} %copy-done.35) | copy-start | bytes 7372804
  301.2 14.9 %copy-start.39 = (bf16[16,50,384]{2,1,0:T(8,128)(2,1)S(1)}, bf16[16,50,384]{2,1,0:T(8,128)(2,1)}, u32[]{:S(2)}) copy-start(bf16[16,50,384]{2,1,0:T(8,128)(2,1)} %copy-done.38) | copy-start | bytes 1843204
  311.7 21.8 %all-to-all-start.4 = ((bf16[16,50,384]{2,1,0:T(8,128)(2,1)}), bf16[16,50,384]{2,1,0:T(8,128)(2,1)}, u32[]{:S(2)}, u32[]{:S(2)}) async-start(bf16[16,50,384]{2,1,0:T(8,128)(2,1)} %add_convert_fusion.1), calls=%async_computation.4 | async-start | bytes 1376256 | tf_op jit(solution)/shard_map/all_to_all | solution.py:732
  316.1 180.0 %reduce-scatter.4.cloned.1.call-start = ((), (), s32[]{:S(2)}) async-start(), calls=%async_computation.8 | async-start | bytes 2506752
  337.2 59.6 %copy-start = (bf16[1024,384]{1,0:T(8,128)(2,1)}, bf16[1024,384]{1,0:T(8,128)(2,1)S(1)}, u32[]{:S(2)}) copy-start(bf16[1024,384]{1,0:T(8,128)(2,1)S(1)} %get-tuple-element.214.refs_0_.refs_6_) | copy-start | bytes 2359300
  339.5 3.7 collective-permute-start.9
  344.3 19.2 %collective-permute-start.10 = (bf16[1024,384]{1,0:T(8,128)(2,1)S(1)}, bf16[1024,384]{1,0:T(8,128)(2,1)}, u32[]{:S(2)}, u32[]{:S(2)}) collective-permute-start(bf16[1024,384]{1,0:T(8,128)(2,1)S(1)} %get-tuple-element.211), channel_id=1, source_target_pairs={{0,1},{1,0},{2,3},{3,2},{4,5},{5,4},{6,7},{7,6},{8,9},{9,8},{10,11... | collective-permute-start | bytes 2359304 | tf_op jit(solution)/shard_map/ppermute | solution.py:27
  357.9 124.6 %collective-permute-start.13 = (f32[1,384]{1,0:T(1,128)}, f32[1,384]{1,0:T(1,128)}, u32[]{:S(2)}, u32[]{:S(2)}) collective-permute-start(f32[1,384]{1,0:T(1,128)} %broadcast_in_dim.54), channel_id=1, source_target_pairs={{0,1},{1,0},{2,3},{3,2},{4,5},{5,4},{6,7},{7,6},{8,9},{9,8},{10,11... | collective-permute-start | bytes 4616 | tf_op jit(solution)/shard_map/ppermute | solution.py:27
  364.8 24.5 %copy-start.30 = (bf16[1024,384]{1,0:T(8,128)(2,1)}, bf16[1024,384]{1,0:T(8,128)(2,1)S(1)}, u32[]{:S(2)}) copy-start(bf16[1024,384]{1,0:T(8,128)(2,1)S(1)} %get-tuple-element.216) | copy-start | bytes 2359300
  419.1 63.4 %copy-start.62 = (f32[384]{0:T(512)S(1)}, f32[384]{0:T(512)}, u32[]{:S(2)}) copy-start(f32[384]{0:T(512)} %copy-done.61) | copy-start | bytes 4612
  419.1 73.1 %copy-start.47 = (bf16[768,80]{1,0:T(8,128)(2,1)S(1)}, bf16[768,80]{1,0:T(8,128)(2,1)}, u32[]{:S(2)}) copy-start(bf16[768,80]{1,0:T(8,128)(2,1)} %copy-done.46) | copy-start | bytes 368644
  419.1 75.7 %copy-start.50 = (f32[768,22]{0,1:T(8,128)S(1)}, f32[768,22]{0,1:T(8,128)}, u32[]{:S(2)}) copy-start(f32[768,22]{0,1:T(8,128)} %copy-done.49) | copy-start | bytes 202756
  482.0 9.1 %collective-permute-start.11 = (bf16[1024,128]{1,0:T(8,128)(2,1)}, bf16[1024,128]{1,0:T(8,128)(2,1)S(1)}, u32[]{:S(2)}, u32[]{:S(2)}) collective-permute-start(bf16[1024,128]{1,0:T(8,128)(2,1)} %get-tuple-element.97), channel_id=1, source_target_pairs={{0,1},{1,0},{2,3},{3,2},{4,5},{5,4},{6,7},{7,6},{8,9},{9,8},{10,11... | collective-permute-start | bytes 786440 | tf_op jit(solution)/shard_map/ppermute | solution.py:27
  493.5 4.8 collective-permute-start.12
  523.6 3.4 collective-permute-start.14
  524.8 20.7 %collective-permute-start.16 = (bf16[512,768]{1,0:T(8,128)(2,1)}, bf16[512,768]{1,0:T(8,128)(2,1)}, u32[]{:S(2)}, u32[]{:S(2)}) collective-permute-start(bf16[512,768]{1,0:T(8,128)(2,1)} %get-tuple-element.117.refs_2_), channel_id=1, source_target_pairs={{0,1},{1,0},{2,3},{3,2},{4,5},{5,4},{6,7},{7,6},{8,9},{9,8},{10,11... | collective-permute-start | bytes 2359304 | tf_op jit(solution)/shard_map/ppermute | solution.py:27
  529.7 17.8 %copy-start.31 = (bf16[1024,384]{1,0:T(8,128)(2,1)S(1)}, bf16[1024,384]{1,0:T(8,128)(2,1)}, u32[]{:S(2)}) copy-start(bf16[1024,384]{1,0:T(8,128)(2,1)} %copy-done.30) | copy-start | bytes 2359300
  529.7 17.8 %copy-start.34 = (bf16[1024,384]{1,0:T(8,128)(2,1)S(1)}, bf16[1024,384]{1,0:T(8,128)(2,1)}, u32[]{:S(2)}) copy-start(bf16[1024,384]{1,0:T(8,128)(2,1)} %copy-done.32) | copy-start | bytes 2359300
  531.3 11.5 %collective-permute-start.15 = (bf16[4,48,1024]{2,1,0:T(8,128)(2,1)S(1)}, bf16[4,48,1024]{2,1,0:T(8,128)(2,1)S(1)}, u32[]{:S(2)}, u32[]{:S(2)}) collective-permute-start(bf16[4,48,1024]{2,1,0:T(8,128)(2,1)S(1)} %fusion.91), channel_id=1, source_target_pairs={{0,4},{2,6},{4,0},{6,2},{8,12},{10,14},{12,8},{14,10},{1,5},{3,7},... | collective-permute-start | bytes 1179656 | tf_op jit(solution)/shard_map/ppermute | solution.py:58
  532.6 28.8 %collective-permute-start.18 = (bf16[512,768]{1,0:T(8,128)(2,1)}, bf16[512,768]{1,0:T(8,128)(2,1)}, u32[]{:S(2)}, u32[]{:S(2)}) collective-permute-start(bf16[512,768]{1,0:T(8,128)(2,1)} %get-tuple-element.108.refs_0_), channel_id=1, source_target_pairs={{0,1},{1,0},{2,3},{3,2},{4,5},{5,4},{6,7},{7,6},{8,9},{9,8},{10,11... | collective-permute-start | bytes 2359304 | tf_op jit(solution)/shard_map/ppermute | solution.py:27
  544.3 18.7 %copy-start.29 = (f32[48,1536]{0,1:T(8,128)S(1)}, f32[48,1536]{0,1:T(8,128)}, u32[]{:S(2)}) copy-start(f32[48,1536]{0,1:T(8,128)} %convert_element_type.262) | copy-start | bytes 884740
  545.5 10.4 %collective-permute-start.17 = (bf16[2,48,1024]{2,1,0:T(8,128)(2,1)S(1)}, bf16[2,48,1024]{2,1,0:T(8,128)(2,1)S(1)}, u32[]{:S(2)}, u32[]{:S(2)}) collective-permute-start(bf16[2,48,1024]{2,1,0:T(8,128)(2,1)S(1)} %fusion.94), channel_id=1, source_target_pairs={{0,8},{2,10},{4,12},{6,14},{8,0},{10,2},{12,4},{14,6},{1,9},{3,11}... | collective-permute-start | bytes 589832 | tf_op jit(solution)/shard_map/ppermute | solution.py:58
  561.4 9.9 %collective-permute-start.19 = (bf16[1,48,1024]{2,1,0:T(8,128)(2,1)S(1)}, bf16[1,48,1024]{2,1,0:T(8,128)(2,1)S(1)}, u32[]{:S(2)}, u32[]{:S(2)}) collective-permute-start(bf16[1,48,1024]{2,1,0:T(8,128)(2,1)S(1)} %fusion.100), channel_id=1, source_target_pairs={{0,16},{16,0},{1,17},{17,1},{2,18},{18,2},{3,19},{19,3},{4,20},{20... | collective-permute-start | bytes 294920 | tf_op jit(solution)/shard_map/ppermute | solution.py:58
  573.4 3.5 collective-permute-start.20
  (66 other events, 344.3 us)
Sparse Core Ops, SparseCore 0:
  12.9 42.3 all-gather.2
  58.2 53.4 all-gather.4
  397.0 60.9 reduce-scatter.3

commit v3 on v2

--- a/solution.py
+++ b/solution.py
@@ -70,6 +70,15 @@
     return lax.ppermute(value, "ctx", pairs)
 
 
+TN = (((0,), (0,)), ((), ()))
+NT = (((1,), (1,)), ((), ()))
+NN = (((1,), (0,)), ((), ()))
+
+
+def dot(a, b, dims=NN):
+    return lax.dot_general(a, b, dims, preferred_element_type=F32)
+
+
 MESH = pl.DeviceIdType.MESH
 
 
@@ -82,7 +91,9 @@
 
 def carry_kernel(sign, ranges, peers, end_ref, log_ref, r_ref, *refs):
     if peers:
-        own_ref, out_ref, others_ref, sent, got, log_out, send_sem, recv_sem, own_sem, others_sem = refs
+        own_ref, left_refs, right_refs = refs[0], refs[1:5:2], refs[2:5:2]
+        out_ref, others_ref, products_ref = refs[5:8]
+        sent, got, log_out, send_sem, recv_sem, own_sem, others_sem = refs[8:]
     else:
         out_ref, sent, got, log_out, send_sem, recv_sem = refs
     turns, groups, _, width = sent.shape
@@ -145,6 +156,17 @@
             log_out[:, cols] = late + log
 
     for turn in range(turns):
+        if turn == 1 and peers:
+            for k, (left, right) in enumerate(zip(left_refs, right_refs)):
+                count = right.shape[1]
+
+                def product(i, _, k=k, left=left, right=right, count=count):
+                    at = pl.ds(pl.multiple_of(i * LANES, LANES), LANES)
+                    value = dot(left[:, at], right[...], TN)
+                    products_ref[at, k * count : (k + 1) * count] = value.astype(BF16)
+                    return 0
+
+                lax.fori_loop(0, left.shape[1] // LANES, product, 0)
         for group in range(groups):
             cols = slice(group * width, (group + 1) * width)
             own_log = log_ref[:, cols]
@@ -173,7 +195,7 @@
         extra.wait()
 
 
-def carried(end, log_decay, rates, sign, ident, shared=None):
+def carried(end, log_decay, rates, sign, ident, shared=None, factors=()):
     _, seqs, chans = end.shape
     ranges = lax.axis_size("ctx")
     turns = (ranges - 1).bit_length()
@@ -193,17 +215,20 @@
     if peers:
         others = jax.ShapeDtypeStruct((peers - 1, *shared.shape), shared.dtype)
         scratch += [pltpu.SemaphoreType.DMA((peers - 1,)), pltpu.SemaphoreType.DMA((peers - 1,))]
+        products = jax.ShapeDtypeStruct(
+            (factors[0].shape[1], factors[1].shape[1] + factors[3].shape[1]), BF16
+        )
     return pl.pallas_call(
         functools.partial(carry_kernel, sign, ranges, peers),
-        in_specs=[vmem] * 3 + [anywhere] * bool(peers),
-        out_specs=[vmem, anywhere] if peers else vmem,
-        out_shape=[state, others] if peers else state,
+        in_specs=[vmem] * 3 + ([anywhere] + [vmem] * len(factors) if peers else []),
+        out_specs=[vmem, anywhere, vmem] if peers else vmem,
+        out_shape=[state, others, products] if peers else state,
         scratch_shapes=scratch,
         compiler_params=pltpu.CompilerParams(
-            collective_id=ident, has_side_effects=True, vmem_limit_bytes=32 << 20
+            collective_id=ident, has_side_effects=True, vmem_limit_bytes=48 << 20
         ),
         cost_estimate=pl.CostEstimate(flops=20 << 30, bytes_accessed=1 << 20, transcendentals=0),
-    )(end[:N], log_decay, rates, *([shared] if peers else []))
+    )(end[:N], log_decay, rates, *([shared, *factors] if peers else []))
 
 
 def spread_matrix():
@@ -268,6 +293,7 @@
 
 
 def forward_kernel(
+    peers,
     d_ref,
     u_ref,
     z_ref,
@@ -277,27 +303,55 @@
     skip_ref,
     w_ref,
     h0_ref,
+    x_ref,
     y_ref,
     gated_ref,
-    mixed_ref,
     st_ref,
-    h1_ref,
+    resid_ref,
     rb,
     bb,
     cb,
+    state,
     total,
+    sent,
+    got,
+    send_sem,
+    recv_sem,
 ):
     rows, width = d_ref.shape
     seqs = rb.shape[1]
     length = rows // seqs
     parts = width // LANES
+    piece, group = pl.program_id(0), pl.program_id(1)
+    pieces, last = pl.num_programs(0), pl.num_programs(1) - 1
+    fsdp, ctx, tensor = lax.axis_index("fsdp"), lax.axis_index("ctx"), lax.axis_index("tensor")
+    partners = [(fsdp, ctx, lax.rem(tensor + by, peers)) for by in range(1, peers)]
+
+    def copy(k, which):
+        return pltpu.make_async_remote_copy(
+            src_ref=sent.at[which],
+            dst_ref=got.at[k, which],
+            send_sem=send_sem.at[k, which],
+            recv_sem=recv_sem.at[k, which],
+            device_id=partners[k],
+            device_id_type=MESH,
+        )
+
+    @pl.when((piece == 0) & (group == 0))
+    def _():
+        greet(partners)
+
     for n in range(N):
         rb[n] = jnp.broadcast_to(r_ref[n : n + 1, :], (seqs, width))
 
-    @pl.when(pl.program_id(0) == 0)
+    @pl.when(group == 0)
     def _():
         spread_into([(b_ref, bb), (c_ref, cb)], rows)
         total[...] = jnp.zeros_like(total)
+
+    @pl.when(piece == 0)
+    def _():
+        state[group] = h0_ref[...]
 
     def block(i, hs):
         for n in range(N):
@@ -330,16 +384,51 @@
         0,
         length // BLK,
         block,
-        tuple(h0_ref[n, :, lanes(k)] for n in range(N) for k in range(parts)),
+        tuple(state[group, n, :, lanes(k)] for n in range(N) for k in range(parts)),
     )
     for n in range(N):
         for k in range(parts):
-            h1_ref[n, :, lanes(k)] = hs[n * parts + k]
+            state[group, n, :, lanes(k)] = hs[n * parts + k]
     z = z_ref[...]
     gated = (y_ref[...] * (z * jax.nn.sigmoid(z))).astype(BF16)
     gated_ref[...] = gated
     total[...] += jnp.dot(gated, w_ref[...], preferred_element_type=F32)
-    mixed_ref[...] = total[...].astype(BF16)
+
+    def add(which):
+        for k in range(peers - 1):
+            copy(k, which).wait_recv()
+        at = pl.ds(pl.multiple_of(which * rows, rows), rows)
+        value = x_ref[at, :].astype(F32)
+        own = sent[which].astype(F32)
+        if peers == 2:
+            value = value + (own + got[0, which].astype(F32))
+        else:
+            for owner in range(peers):
+                term = own
+                for k in range(peers - 1):
+                    here = lax.rem(tensor + peers - k - 1, peers) == owner
+                    term = jnp.where(here, got[k, which].astype(F32), term)
+                value = value + term
+        resid_ref[at, :] = value
+
+    @pl.when(group == last)
+    def _():
+        sent[piece] = total[...].astype(BF16)
+        for k in range(peers - 1):
+            copy(k, piece).start()
+
+        @pl.when(piece > 1)
+        def _():
+            add(piece - 2)
+
+    @pl.when((group == last) & (piece == pieces - 1))
+    def _():
+        count = sent.shape[0]
+        for which in range(max(count - 2, 0), count):
+            add(which)
+        for which in range(count):
+            for k in range(peers - 1):
+                copy(k, which).wait_send()
 
 
 def start_grad_kernel(d_ref, dy_ref, c_ref, r_ref, g_ref, rb, cb):
@@ -510,15 +599,6 @@
         dproj_ref[...] = total[...].astype(BF16)
 
 
-TN = (((0,), (0,)), ((), ()))
-NT = (((1,), (1,)), ((), ()))
-NN = (((1,), (0,)), ((), ()))
-
-
-def dot(a, b, dims=NN):
-    return lax.dot_general(a, b, dims, preferred_element_type=F32)
-
-
 def normalized(x):
     return x * lax.rsqrt(jnp.mean(x * x, -1, keepdims=True) + EPS)
 
@@ -805,45 +885,66 @@
     state = carried(end, log_decay, rates, 1, 0)
     pieces = 4 if length % (4 * BLK) == 0 else 1
     steps = length // pieces
-    y_parts, gated_parts, mixed_parts, start_parts = [], [], [], []
-    for piece in range(pieces):
-        if piece > 1:
-            state, mixed_parts[piece - 2] = lax.optimization_barrier(
-                (state, mixed_parts[piece - 2])
-            )
-        y_part, gated_part, mixed_part, start_part, state = call(
-            forward_kernel,
-            [
-                both_in(delta, steps),
-                both_in(u_wide, steps),
-                (gate_z, (steps * seqs, lane_width), "tc"),
-                by_rows(b_vals, steps),
-                by_rows(c_vals, steps),
-                by_chan(rates),
-                by_chan(skip[None]),
-                (w_out, (lane_width, width), "r"),
-                by_chan(state),
-            ],
-            [
-                by_chan(out((steps * seqs, chans))),
-                by_chan(out((steps * seqs, chans), BF16)),
-                (out((steps * seqs, width), BF16), (steps * seqs, width), ""),
-                by_chan(out((steps // BLK, N, seqs, chans))),
-                by_chan(out((N, seqs, chans))),
-            ],
-            [wide_rates, (steps * seqs, N * LANES), (steps * seqs, N * LANES), (steps * seqs, width)],
-            chunk=piece,
-            cost=cost(steps, 10),
+    block = steps * seqs
+    groups = chans // lane_width
+    peers, here = lax.axis_size("tensor"), lax.axis_index("tensor")
+
+    def cut(value, *shape):
+        return value, pl.BlockSpec(shape, lambda p, j: (p, j))
+
+    def by_piece(value):
+        return value, pl.BlockSpec((block, value.shape[1]), lambda p, j: (p, 0))
+
+    def by_group(value):
+        rank = value.ndim - 1
+        return value, pl.BlockSpec(
+            (*value.shape[:-1], lane_width), lambda p, j: (0,) * rank + (j,)
         )
-        y_parts.append(y_part)
-        gated_parts.append(gated_part)
-        mixed_parts.append(tensor_total(mixed_part, BF16))
-        start_parts.append(start_part)
-    y_vals = jnp.concatenate(y_parts, 0)
-    gated = jnp.concatenate(gated_parts, 0)
-    starts = jnp.concatenate(start_parts, 0)
+
+    arrays = [
+        cut(delta, block, lane_width),
+        cut(u_wide, block, lane_width),
+        cut(gate_z, block, lane_width),
+        by_piece(b_vals),
+        by_piece(c_vals),
+        by_group(rates),
+        by_group(skip[None]),
+        (w_out, pl.BlockSpec((lane_width, width), lambda p, j: (j, 0))),
+        by_group(state),
+        (x_tok, pl.BlockSpec((tokens, width), lambda p, j: (0, 0))),
+    ]
+    results = [
+        cut(out((tokens, chans)), block, lane_width),
+        cut(out((tokens, chans), BF16), block, lane_width),
+        (
+            out((length // BLK, N, seqs, chans)),
+            pl.BlockSpec((steps // BLK, N, seqs, lane_width), lambda p, j: (p, 0, 0, j)),
+        ),
+        (out((tokens, width)), pl.BlockSpec((tokens, width), lambda p, j: (0, 0))),
+    ]
+    y_vals, gated, starts, resid = pl.pallas_call(
+        functools.partial(forward_kernel, peers),
+        grid=(pieces, groups),
+        in_specs=[spec for _, spec in arrays],
+        out_specs=[spec for _, spec in results],
+        out_shape=[value for value, _ in results],
+        scratch_shapes=[
+            pltpu.VMEM(wide_rates, F32),
+            pltpu.VMEM((block, N * LANES), F32),
+            pltpu.VMEM((block, N * LANES), F32),
+            pltpu.VMEM((groups, *state_block), F32),
+            pltpu.VMEM((block, width), F32),
+            pltpu.VMEM((pieces, block, width), BF16),
+            pltpu.VMEM((peers - 1, pieces, block, width), BF16),
+            pltpu.SemaphoreType.DMA((peers - 1, pieces)),
+            pltpu.SemaphoreType.DMA((peers - 1, pieces)),
+        ],
+        compiler_params=pltpu.CompilerParams(
+            collective_id=2, has_side_effects=True, vmem_limit_bytes=62 << 20
+        ),
+        cost_estimate=cost(length, 10),
+    )(*[value for value, _ in arrays])
     silu_z, gate_slope = silu_parts(gate_z)
-    resid = x + jnp.concatenate(mixed_parts, 0)
 
     scale2 = lax.rsqrt(jnp.mean(resid * resid, -1, keepdims=True) + EPS)
     xhat2 = resid * scale2
@@ -851,7 +952,6 @@
     probs = jax.nn.softmax(dot(normed2, w_router), -1)
     onehot = (route[:, None] == jnp.arange(experts)).astype(F32)
     gate = jnp.sum(probs * onehot, -1, keepdims=True) * kept_f[:, None]
-    peers, here = lax.axis_size("tensor"), lax.axis_index("tensor")
     share = width // peers
 
     def half(value):
@@ -870,41 +970,50 @@
     def product(a, b, terms):
         return jnp.einsum(terms, a, b, preferred_element_type=F32)
 
-    def shared(value, matrix, terms, axis):
-        if peers > 2:
-            total = product(value, matrix, terms)
-            share = lax.psum_scatter(total, "tensor", scatter_dimension=2, tiled=True)
-            return share.astype(BF16), value
+    def halves(matrix, axis):
         low, high = jnp.split(matrix, 2, axis)
-        sent = product(value, jnp.where(here == 0, high, low), terms).astype(BF16)
-        value, sent = lax.optimization_barrier((value, sent))
-        own = product(value, jnp.where(here == 0, low, high), terms)
-        return (own + swapped(sent).astype(F32)).astype(BF16), sent
+        return jnp.where(here == 0, low, high), jnp.where(here == 0, high, low)
+
+    def scattered(value):
+        return lax.psum_scatter(value, "tensor", scatter_dimension=2, tiled=True).astype(BF16)
 
     hidden = product(x_rows, up, "srd,df->srf")
     act_float, gelu_pull = jax.vjp(lambda v: jax.nn.gelu(v, approximate=True), hidden)
     act = act_float.astype(BF16)
-    share_y, sent_y = shared(act, down, "srf,fd->srd", 1)
-    grad_rows, _ = lax.optimization_barrier((grad_rows, sent_y))
-    d_hidden = gelu_pull(product(grad_rows, down, "srd,fd->srf"))[0].astype(BF16)
-    back_y = swap_owners(share_y)
-    share_x, _ = shared(d_hidden, up, "srf,df->srd", 0)
-    back_x = swap_owners(share_x)
+    d_act = product(grad_rows, down, "srd,fd->srf")
+    d_hidden = gelu_pull(d_act)[0].astype(BF16)
+    q_rows = jnp.sum(act.astype(F32) * d_act, -1)
+    if peers == 2:
+        up_own, up_other = halves(up, 0)
+        down_own, down_other = halves(down, 1)
+        x_sent = product(d_hidden, up_other, "srf,df->srd").astype(BF16)
+        x_got = swapped(x_sent)
+        act_late, _ = lax.optimization_barrier((act, x_sent))
+        x_own = product(d_hidden, up_own, "srf,df->srd")
+        y_sent = product(act_late, down_other, "srf,fd->srd").astype(BF16)
+        x_got, y_sent = lax.optimization_barrier((x_got, y_sent))
+        back_x = swap_owners((x_own + x_got.astype(F32)).astype(BF16))
+        y_got = swapped(y_sent)
+        y_own = product(act_late, down_own, "srf,fd->srd")
+        share_y = (y_own + y_got.astype(F32)).astype(BF16)
+    else:
+        back_x = swap_owners(scattered(product(d_hidden, up, "srf,df->srd")))
+        share_y = scattered(product(act, down, "srf,fd->srd"))
+    q_back = swap_owners(q_rows[:, None, :])
     grad_up = product(x_rows, d_hidden, "srd,srf->df")
     grad_down = product(act, grad_rows, "srf,srd->fd")
-    back_x, grad_up, grad_down = lax.optimization_barrier((back_x, grad_up, grad_down))
-    expert_y = unpacked(back_y)
+    back_x, grad_up, grad_down, share_y = lax.optimization_barrier(
+        (back_x, grad_up, grad_down, share_y)
+    )
     expert_dx = unpacked(back_x)
+    q_part = jnp.sum(jnp.where(pick > 0, q_back[:, 0, :, None], 0.0), (0, 1))
     x_half = half(xhat2)
     gain_half = half(gains[1])
     grad_half = half(grad_act)
     router_half = half(w_router.T)
-    sums = jnp.stack(
-        [jnp.sum(grad_half * expert_y, -1), jnp.sum(gain_half * expert_dx * x_half, -1)]
-    )
+    sums = jnp.stack([q_part, jnp.sum(gain_half * expert_dx * x_half, -1)])
     sums = tensor_total(sums, F32)
-    gate_grad = sums[0][:, None]
-    d_logits = (gate_grad * gate * (onehot - probs)).astype(BF16)
+    d_logits = (sums[0][:, None] * (onehot - probs)).astype(BF16)
     grad_router = dot(normed2, d_logits, TN)
     by_router = dot((xhat2 * gains[1]).astype(BF16), w_router)
     mean_term = (
@@ -913,9 +1022,11 @@
     d_normed2 = expert_dx + dot(d_logits, router_half)
     gain_grad2 = tensor_columns(jnp.sum(d_normed2 * x_half, 0, keepdims=True))[0]
     d_resid_half = grad_half + scale2 * (gain_half * d_normed2 - x_half * mean_term)
+
+    d_mixed = tensor_columns(d_resid_half.astype(BF16))
+    d_mixed, share_y = lax.optimization_barrier((d_mixed, share_y))
+    expert_y = unpacked(swap_owners(share_y))
     act_half = (valid * (half(resid) + gate * expert_y)).astype(BF16)
-
-    d_mixed = tensor_columns(d_resid_half.astype(BF16))
     d_gated = dot(d_mixed, w_out, NT)
     d_y = d_gated * silu_z
     [start_grad] = call(
@@ -932,10 +1043,10 @@
             value.astype(BF16), OWNERS, scatter_dimension=0, tiled=True
         ).astype(F32)
 
-    mine_early = owned(
-        jnp.concatenate([dot(d_gate_z, normed1, TN), dot(gated, d_mixed, TN)], 1)
-    )
-    grad_end, act_others = carried(start_grad, log_decay, rates, -1, 1, act_half)
+    grad_end, act_others, early = carried(
+        start_grad, log_decay, rates, -1, 1, act_half, (d_gate_z, normed1, gated, d_mixed)
+    )
+    mine_early = owned(early)
     w_step_wide = jnp.pad(w_step, ((0, 0), (0, LANES - R)))
     d_step, du_part, d_proj_part, rate_grad, bias_sums, skip_sums = call(
         backward_kernel,
@@ -974,7 +1085,6 @@
         ],
         cost=cost(length, 24),
     )
-    d_step, mine_early = lax.optimization_barrier((d_step, mine_early))
     d_proj = tensor_total(d_proj_part, BF16).astype(BF16)
     step_bias_grad = jnp.sum(bias_sums, 0)
     skip_grad = jnp.sum(skip_sums, 0)
@@ -1034,6 +1144,7 @@
         scratch_shapes=[pltpu.VMEM((block + rim, chans), F32)],
         compiler_params=pltpu.CompilerParams(vmem_limit_bytes=62 << 20),
     )(*[value for value, _ in arrays])
+    late_part, mine_early = lax.optimization_barrier((late_part, mine_early))
     grad_xproj = grad_xproj[:, :x_cols]
     conv_sums = jnp.sum(conv_sums.reshape(CONV_TAPS + 1, seqs, chans), 1)
     gain_grad1 = jnp.sum(gain_sums, 0)

time: 594 us -> 566 us (0.953)
  waiting for transfers between devices: 145 us -> 117 us
  Pallas kernels: 196 us -> 216 us
  local copies, waits for them, and re-layouts: 57.1 us -> 43.3 us
  other arithmetic: 52.9 us -> 45.5 us
    pallas_call x0 -> x1, Pallas kernels: none -> 46.9 us  [per_device(): pl.pallas_call(functools.partial(forward_kernel, peers), grid=(pieces, gr...]
    pallas_call x7 -> x3, Pallas kernels: 130 us -> 96.1 us  [scan_call(): pl.pallas_call(kernel, grid=(chans // width,), in_specs=[spec(shape, kind...]
    ppermute x15 -> x11, waiting for transfers between devices: 50.1 us -> 36.6 us  [swapped(): return lax.ppermute(value, 'tensor', [(0, 1), (1, 0)])]
    all_to_all x5 -> x6, waiting for transfers between devices: 40.1 us -> 27.5 us  [swap_owners(): lax.all_to_all(value, OWNERS, split_axis=0, concat_axis=0, tiled=True)]
    dot_general x13 -> x11, matrix products: 31.6 us -> 23.7 us  [dot(): return lax.dot_general(a, b, dims, preferred_element_type=F32)]
    pallas_call x2, Pallas kernels: 42.9 us -> 50.6 us  [carried(): pl.pallas_call(functools.partial(carry_kernel, sign, ranges, peers), in_s...]
    concatenate x2 -> x0, other arithmetic: 7.08 us -> none  [the longest x1 5.45 us: per_device(): starts = jnp.concatenate(start_parts, 0)]
    unnamed x178 -> x113, local copies, waits for them, and re-layouts: 18 us -> 11.4 us
  transfers between devices with their start and end apart: 29 -> 26, of which waited for: 22 -> 17; matrix products, arithmetic and copies ran while one was open for 21% -> 21% of each run, Pallas kernels for 24% -> 26%
where the time goes in v3:
time: 566 us; the launch traced here: 557 us
  Pallas kernels  216 us (38%)
  waiting for transfers between devices  117 us (21%)
  matrix products  66.6 us (12%)
  starting transfers between devices  52.5 us (9%)
  other arithmetic  45.5 us (8%)
  local copies, waits for them, and re-layouts  43.3 us (8%)
  between operations  15.4 us (3%)
    pallas_call x3, Pallas kernels, scan_call(): pl.pallas_call(kernel, grid=(chans // width,), in_specs=[spec(shape, kind...  96.1 us
    pallas_call x2, Pallas kernels, carried(): pl.pallas_call(functools.partial(carry_kernel, sign, ranges, peers), in_s...  50.6 us
    pallas_call x1, Pallas kernels, per_device(): pl.pallas_call(functools.partial(forward_kernel, peers), grid=(pieces, gr...  46.9 us
    dot_general x8, matrix products, product(): return jnp.einsum(terms, a, b, preferred_element_type=F32)  36.8 us
    ppermute x11, waiting for transfers between devices, swapped(): return lax.ppermute(value, 'tensor', [(0, 1), (1, 0)])  36.6 us
    all_to_all x6, starting transfers between devices, swap_owners(): lax.all_to_all(value, OWNERS, split_axis=0, concat_axis=0, tiled=True)  30.9 us
    all_to_all x6, waiting for transfers between devices, swap_owners(): lax.all_to_all(value, OWNERS, split_axis=0, concat_axis=0, tiled=True)  27.5 us
    all_gather x1, waiting for transfers between devices, per_device(): full = lax.all_gather(first, OWNERS, axis=0, tiled=True)  27 us
  transfers between devices with their start and end apart: 26, of which 17 were waited for; matrix products, arithmetic and copies ran while one was open for 21% of the time, Pallas kernels for 26%

profile of v3, /device:TPU:0, one launch (start us, length us, event | category | flops | bytes accessed | tf_op | source)
XLA Modules:
  0.0 557.2 jit_solution(7453809629932668013)
XLA Ops:
  24.2 4.1 fusion.35
  28.3 27.0 %all-gather.3.cloned.1.call-done = bf16[768,1024]{1,0:T(8,128)(2,1)} async-done(((bf16[48,1024]{1,0:T(8,128)(2,1)}), bf16[768,1024]{1,0:T(8,128)(2,1)}) %all-gather.3.cloned.1.call-update) | async-done | bytes 1572880 | tf_op jit(solution)/shard_map/all_gather | solution.py:787
  64.9 3.7 fusion.116
  72.5 6.4 %all-to-all-start = ((bf16[16,50,768]{2,1,0:T(8,128)(2,1)}), bf16[16,50,768]{2,1,0:T(8,128)(2,1)}, u32[]{:S(2)}, u32[]{:S(2)}) async-start(bf16[16,50,768]{2,1,0:T(8,128)(2,1)} %fusion.35), calls=%async_computation | async-start | bytes 2752512 | tf_op jit(solution)/shard_map/all_to_all | solution.py:812
  81.4 6.0 %add_divide_fusion = (f32[1024,768]{1,0:T(8,128)}, f32[1024,768]{1,0:T(8,128)}) fusion(f32[768]{0:T(1024)S(1)} %convert_reduce_fusion, bf16[768,1024]{1,0:T(8,128)(2,1)} %all-gather.3.cloned.1.call-done, f32[1024,80]{1,0:T(8,128)S(1)} %convert_add_fusion), kind=kOutput, calls=%fused_computation.41 | convolution fusion | flops 83361792 | bytes 6754304 | tf_op jit(solution)/shard_map/dot_general | solution.py:79
  87.5 16.5 %shard_map.238 = f32[17,8,768]{2,1,0:T(8,128)} custom-call(f32[1024,768]{1,0:T(8,128)} %get-tuple-element.176.d_ref, f32[1024,768]{1,0:T(8,128)} %get-tuple-element.169.u_ref, f32[1024,16]{1,0:T(8,128)} %get-tuple-element.186.b_ref, f32[16,768]{1,0:T(8,128)} %fusion.92.r_ref), custom_call_target="tpu_custom_call" | custom-call | flops 22649241600 | bytes 12582912 | tf_op jit(solution)/shard_map/pallas_call | solution.py:731
  104.0 5.8 %all-gather.5.cloned.1.call-done = bf16[768,1536]{1,0:T(8,128)(2,1)} async-done(((bf16[48,1536]{1,0:T(8,128)(2,1)}), bf16[768,1536]{1,0:T(8,128)(2,1)}) %all-gather.5.cloned.1.call-update) | async-done | bytes 2359312 | tf_op jit(solution)/shard_map/all_gather | solution.py:788
  109.8 3.3 fusion.118
  113.2 3.1 fusion.113.z_ref
  116.3 3.3 all-to-all-done
  119.6 22.5 %shard_map.239.h0_ref = f32[16,8,768]{2,1,0:T(8,128)S(1)} custom-call(f32[16,8,768]{2,1,0:T(8,128)S(1)} %slice.267.end_ref, f32[8,768]{1,0:T(8,128)S(1)} %slice_bitcast_fusion.9.log_ref, f32[16,768]{1,0:T(8,128)S(1)} %copy-done.5), custom_call_target="tpu_custom_call" | custom-call | flops 21474836480 | bytes 1048576 | tf_op jit(solution)/shard_map/pallas_call | solution.py:221
  142.9 46.9 %shard_map.240 = (f32[1024,768]{1,0:T(8,128)}, bf16[1024,768]{1,0:T(8,128)(2,1)}, f32[16,16,8,768]{3,2,1,0:T(8,128)}, f32[1024,768]{1,0:T(8,128)}) custom-call(f32[1024,768]{1,0:T(8,128)} %get-tuple-element.176.d_ref, f32[1024,768]{1,0:T(8,128)} %get-tuple-element.169.u_ref, f32[1024,768]{1,0:T(8,128)} %fusion.113.z_ref, ...), custom_call_target="tpu_custom_call" | custom-call | flops 37748736000 | bytes 12582912 | tf_op jit(solution)/shard_map/pallas_call | solution.py:925
  197.8 3.7 all-to-all-start.2
  201.6 3.5 convert_multiply_fusion.2
  207.2 11.7 %all-to-all-done.2 = bf16[16,50,384]{2,1,0:T(8,128)(2,1)S(1)} async-done(((bf16[16,50,384]{2,1,0:T(8,128)(2,1)}), bf16[16,50,384]{2,1,0:T(8,128)(2,1)S(1)}, u32[]{:S(2)}, u32[]{:S(2)}) %all-to-all-start.2) | async-done | bytes 614432 | tf_op jit(solution)/shard_map/all_to_all | solution.py:812
  218.9 4.4 all-to-all-start.1
  224.0 5.7 %all-to-all-done.1 = f32[16,1,50]{2,1,0:T(1,128)S(1)} async-done(((f32[16,1,50]{2,1,0:T(1,128)}), f32[16,1,50]{2,1,0:T(1,128)S(1)}, u32[]{:S(2)}, u32[]{:S(2)}) %all-to-all-start.1) | async-done | bytes 3232 | tf_op jit(solution)/shard_map/all_to_all | solution.py:812
  229.7 4.6 fusion.24
  234.3 5.5 collective-permute-done.2
  241.1 7.1 %multiply_reduce_fusion = (f32[16,50]{1,0:T(8,128)}, bf16[16,50,1536]{2,1,0:T(8,128)(2,1)S(1)}, bf16[16,50,1536]{2,1,0:T(8,128)(2,1)S(1)}) fusion(f32[16,50,1536]{2,1,0:T(8,128)S(1)} %fusion.24, bf16[1,768,1536]{2,1,0:T(8,128)(2,1)S(1)} %copy-done.48, bf16[16,50,384]{2,1,0:T(8,128)(2,1)S(1)} %get-tuple-element.184, ...), kind=kOutput, calls=%fused_computation.19 | convolution fusion | flops 1920613632 | bytes 13421696 | tf_op jit(solution)/shard_map/srd,df->srf/dot_general | solution.py:971
  250.7 5.9 %convolution_bitcast_fusion = f32[1536,768]{1,0:T(8,128)} fusion(bf16[16,50,1536]{2,1,0:T(8,128)(2,1)S(1)} %get-tuple-element.58, bf16[16,50,768]{2,1,0:T(8,128)(2,1)} %all-to-all-done, f32[16,50]{1,0:T(8,128)S(1)} %bitcast.197), kind=kOutput, calls=%fused_computation.23 | convolution fusion | flops 1889280000 | bytes 8408192 | tf_op jit(solution)/shard_map/srf,srd->fd/dot_general | solution.py:971
  256.5 5.8 %all-to-all-start.4 = ((f32[16,1,50]{2,1,0:T(1,128)}), f32[16,1,50]{2,1,0:T(1,128)S(1)}, u32[]{:S(2)}, u32[]{:S(2)}) async-start(f32[16,1,50]{2,1,0:T(1,128)} %bitcast.29), calls=%async_computation.4 | async-start | bytes 16384 | tf_op jit(solution)/shard_map/all_to_all | solution.py:812
  262.3 4.2 convolution_convert_fusion.1
  268.9 3.6 add_convert_fusion.1
  272.5 6.3 %all-to-all-start.3 = ((bf16[16,50,384]{2,1,0:T(8,128)(2,1)}), bf16[16,50,384]{2,1,0:T(8,128)(2,1)}, u32[]{:S(2)}, u32[]{:S(2)}) async-start(bf16[16,50,384]{2,1,0:T(8,128)(2,1)} %add_convert_fusion.1), calls=%async_computation.3 | async-start | bytes 1376256 | tf_op jit(solution)/shard_map/all_to_all | solution.py:812
  278.8 6.2 %convolution_bitcast_fusion.1 = f32[768,1536]{1,0:T(8,128)} fusion(bf16[16,50,1536]{2,1,0:T(8,128)(2,1)} %copy-done.27, bf16[16,50,384]{2,1,0:T(8,128)(2,1)S(1)} %copy-done.30, bf16[16,50,384]{2,1,0:T(8,128)(2,1)S(1)} %get-tuple-element.183), kind=kOutput, calls=%fused_computation.24 | convolution fusion | flops 1889894400 | bytes 8404992 | tf_op jit(solution)/shard_map/srd,srf->df/dot_general | solution.py:971
  285.8 3.5 add_convert_fusion
  289.3 6.9 %all-to-all-done.3 = bf16[16,50,384]{2,1,0:T(8,128)(2,1)} async-done(((bf16[16,50,384]{2,1,0:T(8,128)(2,1)}), bf16[16,50,384]{2,1,0:T(8,128)(2,1)}, u32[]{:S(2)}, u32[]{:S(2)}) %all-to-all-start.3) | async-done | bytes 614432 | tf_op jit(solution)/shard_map/all_to_all | solution.py:812
  296.2 2.7 fusion.40
  300.1 2.9 collective-permute-done.5
  311.6 11.7 %collective-permute-done.6 = bf16[1024,384]{1,0:T(8,128)(2,1)} collective-permute-done((bf16[1024,384]{1,0:T(8,128)(2,1)S(1)}, bf16[1024,384]{1,0:T(8,128)(2,1)}, u32[]{:S(2)}, u32[]{:S(2)}) %collective-permute-start.6) | collective-permute-done | bytes 786464 | tf_op jit(solution)/shard_map/ppermute | solution.py:27
  324.7 4.3 all-to-all-start.5
  329.3 2.8 fusion.111
  332.5 3.3 multiply_convert_fusion.1
  335.8 16.8 %shard_map.241.end_ref = f32[16,8,768]{2,1,0:T(8,128)} custom-call(f32[1024,768]{1,0:T(8,128)} %get-tuple-element.176.d_ref, f32[1024,768]{1,0:T(8,128)} %get-tuple-element.174.dy_ref, f32[1024,16]{1,0:T(8,128)} %get-tuple-element.185.c_ref, f32[16,768]{1,0:T(8,128)} %fusion.92.r_ref), custom_call_target="tpu_custom_call" | custom-call | flops 22649241600 | bytes 12582912 | tf_op jit(solution)/shard_map/pallas_call | solution.py:731
  352.7 2.7 fusion.43
  357.2 28.1 %shard_map.242 = (f32[16,8,768]{2,1,0:T(8,128)S(1)}, bf16[1,1024,384]{2,1,0:T(8,128)(2,1)S(1)}, bf16[768,1536]{1,0:T(8,128)(2,1)}) custom-call(f32[16,8,768]{2,1,0:T(8,128)S(1)} %copy-done.8, f32[8,768]{1,0:T(8,128)S(1)} %slice_bitcast_fusion.9.log_ref, f32[16,768]{1,0:T(8,128)S(1)} %copy-done.6, ...), custom_call_target="tpu_custom_call" | custom-call | flops 21474836480 | bytes 1048576 | tf_op jit(solution)/shard_map/pallas_call | solution.py:221
  387.0 62.7 %shard_map.243 = (bf16[1024,768]{1,0:T(8,128)(2,1)}, f32[1024,768]{1,0:T(8,128)}, bf16[1024,128]{1,0:T(8,128)(2,1)}, f32[16,8,768]{2,1,0:T(8,128)}, f32[8,768]{1,0:T(8,128)}, /*index=5*/f32[8,768]{1,0:T(8,128)}) custom-call(f32[1024,768]{1,0:T(8,128)} %get-tuple-element.176.d_ref, f32[1024,768]{1,0:T(8,128)} %get-tuple-element.169.u_ref, ...), custom_call_target="tpu_custom_call" | custom-call | flops 90596966400 | bytes 12582912 | tf_op jit(solution)/shard_map/pallas_call | solution.py:731
  452.3 5.5 collective-permute-done.7
  464.0 15.5 %shard_map.244 = (bf16[512,768]{1,0:T(8,128)(2,1)}, bf16[512,768]{1,0:T(8,128)(2,1)}, f32[768,768]{1,0:T(8,128)}, f32[768,128]{1,0:T(8,128)}, f32[768,48]{1,0:T(...) custom-call(f32[1024,768]{1,0:T(8,128)} %get-tuple-element.69.du_ref, bf16[1024,128]{1,0:T(8,128)(2,1)} %copy-done.32, ...), custom_call_target="tpu_custom_call" | custom-call | tf_op jit(solution)/shard_map/pallas_call | solution.py:1138
  481.5 3.5 concatenate.34
  492.0 2.7 bitcast_add_fusion
  500.0 8.9 %collective-permute-done.11 = bf16[4,48,1024]{2,1,0:T(8,128)(2,1)S(1)} collective-permute-done((bf16[4,48,1024]{2,1,0:T(8,128)(2,1)S(1)}, bf16[4,48,1024]{2,1,0:T(8,128)(2,1)S(1)}, u32[]{:S(2)}, u32[]{:S(2)}) %collective-permute-start.11) | collective-permute-done | bytes 393248 | tf_op jit(solution)/shard_map/ppermute | solution.py:58
  510.5 5.8 %collective-permute-done.12.refs_3_ = bf16[512,768]{1,0:T(8,128)(2,1)S(1)} collective-permute-done((bf16[512,768]{1,0:T(8,128)(2,1)}, bf16[512,768]{1,0:T(8,128)(2,1)S(1)}, u32[]{:S(2)}, u32[]{:S(2)}) %collective-permute-start.12) | collective-permute-done | bytes 786464 | tf_op jit(solution)/shard_map/ppermute | solution.py:27
  516.3 3.5 collective-permute-start.13
  519.8 7.7 %collective-permute-done.13 = bf16[2,48,1024]{2,1,0:T(8,128)(2,1)S(1)} collective-permute-done((bf16[2,48,1024]{2,1,0:T(8,128)(2,1)S(1)}, bf16[2,48,1024]{2,1,0:T(8,128)(2,1)S(1)}, u32[]{:S(2)}, u32[]{:S(2)}) %collective-permute-start.13) | collective-permute-done | bytes 196640 | tf_op jit(solution)/shard_map/ppermute | solution.py:58
  527.6 5.0 collective-permute-done.14.refs_1_
  535.6 7.4 %shard_map.245 = (f32[2,4,128,768]{3,2,1,0:T(8,128)}, bf16[2,4,128,768]{3,2,1,0:T(8,128)(2,1)}) custom-call(bf16[512,768]{1,0:T(8,128)(2,1)} %get-tuple-element.72.refs_0_, bf16[512,768]{1,0:T(8,128)(2,1)} %copy-done.34, bf16[512,768]{1,0:T(8,128)(2,1)} %get-tuple-element.83.refs_2_, bf16[512,768]{1,0:T(8,128)(2,1)} %copy-done.33, ...), custom_call_target="tpu_custom_call" | custom-call | tf_op jit(solution)/shard_map/pallas_call | solution.py:1205
  (257 shorter events, 100.8 us)
Async XLA Ops:
  7.2 48.1 %all-gather.3.cloned.1.call-start = ((), (), s32[]{:S(2)}) async-start(), calls=%async_computation.7 | async-start | bytes 1671168 | tf_op jit(solution)/shard_map/all_gather | solution.py:787
  12.7 97.1 %all-gather.5.cloned.1.call-start = ((), (), s32[]{:S(2)}) async-start(), calls=%async_computation.8 | async-start | bytes 2506752 | tf_op jit(solution)/shard_map/all_gather | solution.py:788
  57.1 14.8 %copy-start.37 = (f32[768,22]{0,1:T(8,128)}, f32[768,22]{0,1:T(8,128)S(1)}, u32[]{:S(2)}) copy-start(f32[768,22]{0,1:T(8,128)S(1)} %slice_convert_fusion.1) | copy-start | bytes 202756
  57.1 6.7 %copy-start.40 = (f32[4,768]{1,0:T(4,128)}, f32[4,768]{1,0:T(4,128)S(1)}, u32[]{:S(2)}) copy-start(f32[4,768]{1,0:T(4,128)S(1)} %slice_bitcast_fusion.10.taps_ref) | copy-start | bytes 36868
  60.1 53.0 %copy-start.1 = (bf16[1024,768]{1,0:T(8,128)(2,1)}, bf16[1024,768]{1,0:T(8,128)(2,1)S(1)}, u32[]{:S(2)}) copy-start(bf16[1024,768]{1,0:T(8,128)(2,1)S(1)} %fusion.17.refs_2_.normed_ref) | copy-start | bytes 4718596
  61.6 3.0 collective-permute-start
  70.3 9.7 %collective-permute-start.1 = (bf16[1024,80]{1,0:T(8,128)(2,1)S(1)}, bf16[1024,80]{1,0:T(8,128)(2,1)S(1)}, u32[]{:S(2)}, u32[]{:S(2)}) collective-permute-start(bf16[1024,80]{1,0:T(8,128)(2,1)S(1)} %convolution_convert_fusion.3), channel_id=1, source_target_pairs={{0,1},{1,0},{2,3},{3,2},{4,5},{5,4},{6,7},{7,6},{8,9},{9,8},{10,11... | collective-permute-start | bytes 491528 | tf_op jit(solution)/shard_map/ppermute | solution.py:27
  72.5 47.1 %all-to-all-start = ((bf16[16,50,768]{2,1,0:T(8,128)(2,1)}), bf16[16,50,768]{2,1,0:T(8,128)(2,1)}, u32[]{:S(2)}, u32[]{:S(2)}) async-start(bf16[16,50,768]{2,1,0:T(8,128)(2,1)} %fusion.35), calls=%async_computation | async-start | bytes 2752512 | tf_op jit(solution)/shard_map/all_to_all | solution.py:812
  80.1 7.4 %copy-start.19 = (f32[1024,80]{1,0:T(8,128)}, f32[1024,80]{1,0:T(8,128)S(1)}, u32[]{:S(2)}) copy-start(f32[1024,80]{1,0:T(8,128)S(1)} %convert_add_fusion) | copy-start | bytes 983044
  197.8 7.3 %copy-start.17 = (bf16[768,1024]{1,0:T(8,128)(2,1)S(1)}, bf16[768,1024]{1,0:T(8,128)(2,1)}, u32[]{:S(2)}) copy-start(bf16[768,1024]{1,0:T(8,128)(2,1)} %all-gather.3.cloned.1.call-done) | copy-start | bytes 4718596
  197.8 21.0 %all-to-all-start.2 = ((bf16[16,50,384]{2,1,0:T(8,128)(2,1)}), bf16[16,50,384]{2,1,0:T(8,128)(2,1)S(1)}, u32[]{:S(2)}, u32[]{:S(2)}) async-start(bf16[16,50,384]{2,1,0:T(8,128)(2,1)} %fusion.46), calls=%async_computation.2 | async-start | bytes 1376256 | tf_op jit(solution)/shard_map/all_to_all | solution.py:812
  218.9 10.8 %all-to-all-start.1 = ((f32[16,1,50]{2,1,0:T(1,128)}), f32[16,1,50]{2,1,0:T(1,128)S(1)}, u32[]{:S(2)}, u32[]{:S(2)}) async-start(f32[16,1,50]{2,1,0:T(1,128)} %bitcast.13), calls=%async_computation.1 | async-start | bytes 16384 | tf_op jit(solution)/shard_map/all_to_all | solution.py:812
  223.4 16.4 %collective-permute-start.2 = (bf16[16,50,384]{2,0,1:T(8,128)(2,1)S(1)}, bf16[16,50,384]{2,0,1:T(8,128)(2,1)}, u32[]{:S(2)}, u32[]{:S(2)}) collective-permute-start(bf16[16,50,384]{2,0,1:T(8,128)(2,1)S(1)} %copy.146), channel_id=1, source_target_pairs={{0,1},{1,0},{2,3},{3,2},{4,5},{5,4},{6,7},{7,6},{8,9},{9,8},{10,11... | collective-permute-start | bytes 1843208 | tf_op jit(solution)/shard_map/ppermute | solution.py:27
  229.7 11.5 %copy-start.48 = (bf16[1,768,1536]{2,1,0:T(8,128)(2,1)S(1)}, bf16[1,768,1536]{2,1,0:T(8,128)(2,1)}, u32[]{:S(2)}) copy-start(bf16[1,768,1536]{2,1,0:T(8,128)(2,1)} %param.28) | copy-start | bytes 7077892
  241.1 7.2 %copy-start.29 = (bf16[16,50,384]{2,1,0:T(8,128)(2,1)}, bf16[16,50,384]{2,1,0:T(8,128)(2,1)S(1)}, u32[]{:S(2)}) copy-start(bf16[16,50,384]{2,1,0:T(8,128)(2,1)S(1)} %get-tuple-element.184) | copy-start | bytes 1843204
  250.0 16.5 %collective-permute-start.3 = (bf16[16,50,384]{2,0,1:T(8,128)(2,1)S(1)}, bf16[16,50,384]{2,0,1:T(8,128)(2,1)}, u32[]{:S(2)}, u32[]{:S(2)}) collective-permute-start(bf16[16,50,384]{2,0,1:T(8,128)(2,1)S(1)} %copy.149), channel_id=1, source_target_pairs={{0,1},{1,0},{2,3},{3,2},{4,5},{5,4},{6,7},{7,6},{8,9},{9,8},{10,11... | collective-permute-start | bytes 1843208 | tf_op jit(solution)/shard_map/ppermute | solution.py:27
  256.5 16.0 %all-to-all-start.4 = ((f32[16,1,50]{2,1,0:T(1,128)}), f32[16,1,50]{2,1,0:T(1,128)S(1)}, u32[]{:S(2)}, u32[]{:S(2)}) async-start(f32[16,1,50]{2,1,0:T(1,128)} %bitcast.29), calls=%async_computation.4 | async-start | bytes 16384 | tf_op jit(solution)/shard_map/all_to_all | solution.py:812
  262.3 6.6 %copy-start.28 = (bf16[16,50,1536]{2,1,0:T(8,128)(2,1)S(1)}, bf16[16,50,1536]{2,1,0:T(8,128)(2,1)}, u32[]{:S(2)}) copy-start(bf16[16,50,1536]{2,1,0:T(8,128)(2,1)} %copy-done.27) | copy-start | bytes 7372804
  267.5 11.3 %copy-start.30 = (bf16[16,50,384]{2,1,0:T(8,128)(2,1)S(1)}, bf16[16,50,384]{2,1,0:T(8,128)(2,1)}, u32[]{:S(2)}) copy-start(bf16[16,50,384]{2,1,0:T(8,128)(2,1)} %copy-done.29) | copy-start | bytes 1843204
  267.5 18.3 %collective-permute-start.4 = (bf16[16,50,384]{2,0,1:T(8,128)(2,1)}, bf16[16,50,384]{2,0,1:T(8,128)(2,1)}, u32[]{:S(2)}, u32[]{:S(2)}) collective-permute-start(bf16[16,50,384]{2,0,1:T(8,128)(2,1)} %copy.151), channel_id=1, source_target_pairs={{0,1},{1,0},{2,3},{3,2},{4,5},{5,4},{6,7},{7,6},{8,9},{9,8},{10,11... | collective-permute-start | bytes 1843208 | tf_op jit(solution)/shard_map/ppermute | solution.py:27
  272.5 23.7 %all-to-all-start.3 = ((bf16[16,50,384]{2,1,0:T(8,128)(2,1)}), bf16[16,50,384]{2,1,0:T(8,128)(2,1)}, u32[]{:S(2)}, u32[]{:S(2)}) async-start(bf16[16,50,384]{2,1,0:T(8,128)(2,1)} %add_convert_fusion.1), calls=%async_computation.3 | async-start | bytes 1376256 | tf_op jit(solution)/shard_map/all_to_all | solution.py:812
  278.8 7.0 %copy-start.50 = (bf16[1,1536,768]{2,1,0:T(8,128)(2,1)S(1)}, bf16[1,1536,768]{2,1,0:T(8,128)(2,1)}, u32[]{:S(2)}) copy-start(bf16[1,1536,768]{2,1,0:T(8,128)(2,1)} %param.29) | copy-start | bytes 7077892
  278.8 6.9 %copy-start.53 = (bf16[16,50,1536]{2,1,0:T(8,128)(2,1)S(1)}, bf16[16,50,1536]{2,1,0:T(8,128)(2,1)}, u32[]{:S(2)}) copy-start(bf16[16,50,1536]{2,1,0:T(8,128)(2,1)} %copy-done.52) | copy-start | bytes 7372804
  299.3 3.7 collective-permute-start.5
  304.0 7.5 %copy-start.44 = (f32[384]{0:T(512)}, f32[384]{0:T(512)S(1)}, u32[]{:S(2)}) copy-start(f32[384]{0:T(512)S(1)} %get-tuple-element.177) | copy-start | bytes 4612
  304.1 19.2 %collective-permute-start.6 = (bf16[1024,384]{1,0:T(8,128)(2,1)S(1)}, bf16[1024,384]{1,0:T(8,128)(2,1)}, u32[]{:S(2)}, u32[]{:S(2)}) collective-permute-start(bf16[1024,384]{1,0:T(8,128)(2,1)S(1)} %get-tuple-element.178), channel_id=1, source_target_pairs={{0,1},{1,0},{2,3},{3,2},{4,5},{5,4},{6,7},{7,6},{8,9},{9,8},{10,11... | collective-permute-start | bytes 2359304 | tf_op jit(solution)/shard_map/ppermute | solution.py:27
  304.9 6.7 %copy-start.35 = (bf16[768,80]{1,0:T(8,128)(2,1)}, bf16[768,80]{1,0:T(8,128)(2,1)S(1)}, u32[]{:S(2)}) copy-start(bf16[768,80]{1,0:T(8,128)(2,1)S(1)} %slice.254) | copy-start | bytes 368644
  308.8 141.6 %collective-permute-start.9 = (f32[1,384]{1,0:T(1,128)}, f32[1,384]{1,0:T(1,128)}, u32[]{:S(2)}, u32[]{:S(2)}) collective-permute-start(f32[1,384]{1,0:T(1,128)} %broadcast_in_dim.72), channel_id=1, source_target_pairs={{0,1},{1,0},{2,3},{3,2},{4,5},{5,4},{6,7},{7,6},{8,9},{9,8},{10,11... | collective-permute-start | bytes 4616 | tf_op jit(solution)/shard_map/ppermute | solution.py:27
  324.7 7.5 %copy-start.21 = (bf16[1024,768]{1,0:T(8,128)(2,1)}, bf16[1024,768]{1,0:T(8,128)(2,1)S(1)}, u32[]{:S(2)}) copy-start(bf16[1024,768]{1,0:T(8,128)(2,1)S(1)} %pad_maximum_fusion.refs_4_.refs_5_) | copy-start | bytes 4718596
  324.7 28.0 %all-to-all-start.5 = ((bf16[16,50,384]{2,1,0:T(8,128)(2,1)}), bf16[16,50,384]{2,1,0:T(8,128)(2,1)}, u32[]{:S(2)}, u32[]{:S(2)}) async-start(bf16[16,50,384]{2,1,0:T(8,128)(2,1)} %add_convert_fusion), calls=%async_computation.5 | async-start | bytes 1376256 | tf_op jit(solution)/shard_map/all_to_all | solution.py:812
  329.0 165.7 %reduce-scatter.2.cloned.1.call-start = ((), (), s32[]{:S(2)}) async-start(), calls=%async_computation.9 | async-start | bytes 2506752 | tf_op jit(solution)/shard_map/reduce_scatter | solution.py:1042
  335.8 20.0 %copy-start = (bf16[1024,768]{1,0:T(8,128)(2,1)}, bf16[1024,768]{1,0:T(8,128)(2,1)S(1)}, u32[]{:S(2)}) copy-start(bf16[1024,768]{1,0:T(8,128)(2,1)S(1)} %get-tuple-element.173.refs_1_.dgate_ref) | copy-start | bytes 4718596
  355.8 29.5 %copy-start.3 = (bf16[1024,384]{1,0:T(8,128)(2,1)}, bf16[1024,384]{1,0:T(8,128)(2,1)S(1)}, u32[]{:S(2)}) copy-start(bf16[1024,384]{1,0:T(8,128)(2,1)S(1)} %multiply_convert_fusion.5.refs_0_.refs_6_) | copy-start | bytes 2359300
  387.0 63.4 %copy-start.45 = (f32[384]{0:T(512)S(1)}, f32[384]{0:T(512)}, u32[]{:S(2)}) copy-start(f32[384]{0:T(512)} %copy-done.44) | copy-start | bytes 4612
  387.0 71.9 %copy-start.36 = (bf16[768,80]{1,0:T(8,128)(2,1)S(1)}, bf16[768,80]{1,0:T(8,128)(2,1)}, u32[]{:S(2)}) copy-start(bf16[768,80]{1,0:T(8,128)(2,1)} %copy-done.35) | copy-start | bytes 368644
  387.0 74.8 %copy-start.38 = (f32[768,22]{0,1:T(8,128)S(1)}, f32[768,22]{0,1:T(8,128)}, u32[]{:S(2)}) copy-start(f32[768,22]{0,1:T(8,128)} %copy-done.37) | copy-start | bytes 202756
  449.7 12.3 %copy-start.43 = (f32[8,768]{1,0:T(8,128)S(1)}, f32[8,768]{1,0:T(8,128)}, u32[]{:S(2)}) copy-start(f32[8,768]{1,0:T(8,128)} %get-tuple-element.77) | copy-start | bytes 73732
  449.7 12.5 %copy-start.42 = (f32[8,768]{1,0:T(8,128)S(1)}, f32[8,768]{1,0:T(8,128)}, u32[]{:S(2)}) copy-start(f32[8,768]{1,0:T(8,128)} %get-tuple-element.79) | copy-start | bytes 73732
  449.7 8.1 %collective-permute-start.7 = (bf16[1024,128]{1,0:T(8,128)(2,1)}, bf16[1024,128]{1,0:T(8,128)(2,1)S(1)}, u32[]{:S(2)}, u32[]{:S(2)}) collective-permute-start(bf16[1024,128]{1,0:T(8,128)(2,1)} %get-tuple-element.70), channel_id=1, source_target_pairs={{0,1},{1,0},{2,3},{3,2},{4,5},{5,4},{6,7},{7,6},{8,9},{9,8},{10,11... | collective-permute-start | bytes 786440 | tf_op jit(solution)/shard_map/ppermute | solution.py:27
  460.2 3.2 collective-permute-start.8
  488.4 3.7 collective-permute-start.10
  495.6 20.6 %collective-permute-start.12 = (bf16[512,768]{1,0:T(8,128)(2,1)}, bf16[512,768]{1,0:T(8,128)(2,1)S(1)}, u32[]{:S(2)}, u32[]{:S(2)}) collective-permute-start(bf16[512,768]{1,0:T(8,128)(2,1)} %get-tuple-element.83.refs_2_), channel_id=1, source_target_pairs={{0,1},{1,0},{2,3},{3,2},{4,5},{5,4},{6,7},{7,6},{8,9},{9,8},{10,11... | collective-permute-start | bytes 2359304 | tf_op jit(solution)/shard_map/ppermute | solution.py:27
  497.8 11.2 %collective-permute-start.11 = (bf16[4,48,1024]{2,1,0:T(8,128)(2,1)S(1)}, bf16[4,48,1024]{2,1,0:T(8,128)(2,1)S(1)}, u32[]{:S(2)}, u32[]{:S(2)}) collective-permute-start(bf16[4,48,1024]{2,1,0:T(8,128)(2,1)S(1)} %fusion.79), channel_id=1, source_target_pairs={{0,4},{2,6},{4,0},{6,2},{8,12},{10,14},{12,8},{14,10},{1,5},{3,7},... | collective-permute-start | bytes 1179656 | tf_op jit(solution)/shard_map/ppermute | solution.py:58
  498.6 34.0 %collective-permute-start.14 = (bf16[512,768]{1,0:T(8,128)(2,1)}, bf16[512,768]{1,0:T(8,128)(2,1)S(1)}, u32[]{:S(2)}, u32[]{:S(2)}) collective-permute-start(bf16[512,768]{1,0:T(8,128)(2,1)} %get-tuple-element.72.refs_0_), channel_id=1, source_target_pairs={{0,1},{1,0},{2,3},{3,2},{4,5},{5,4},{6,7},{7,6},{8,9},{9,8},{10,11... | collective-permute-start | bytes 2359304 | tf_op jit(solution)/shard_map/ppermute | solution.py:27
  516.3 19.3 %copy-start.33 = (bf16[512,768]{1,0:T(8,128)(2,1)}, bf16[512,768]{1,0:T(8,128)(2,1)S(1)}, u32[]{:S(2)}) copy-start(bf16[512,768]{1,0:T(8,128)(2,1)S(1)} %collective-permute-done.12.refs_3_) | copy-start | bytes 2359300
  516.3 11.2 %collective-permute-start.13 = (bf16[2,48,1024]{2,1,0:T(8,128)(2,1)S(1)}, bf16[2,48,1024]{2,1,0:T(8,128)(2,1)S(1)}, u32[]{:S(2)}, u32[]{:S(2)}) collective-permute-start(bf16[2,48,1024]{2,1,0:T(8,128)(2,1)S(1)} %fusion.80), channel_id=1, source_target_pairs={{0,8},{2,10},{4,12},{6,14},{8,0},{10,2},{12,4},{14,6},{1,9},{3,11}... | collective-permute-start | bytes 589832 | tf_op jit(solution)/shard_map/ppermute | solution.py:58
  533.3 9.6 %collective-permute-start.15 = (bf16[1,48,1024]{2,1,0:T(8,128)(2,1)}, bf16[1,48,1024]{2,1,0:T(8,128)(2,1)}, u32[]{:S(2)}, u32[]{:S(2)}) collective-permute-start(bf16[1,48,1024]{2,1,0:T(8,128)(2,1)} %fusion.86), channel_id=1, source_target_pairs={{0,16},{16,0},{1,17},{17,1},{2,18},{18,2},{3,19},{19,3},{4,20},{20... | collective-permute-start | bytes 294920 | tf_op jit(solution)/shard_map/ppermute | solution.py:58
  545.3 4.3 collective-permute-start.16
  (32 other events, 93.7 us)
Sparse Core Ops, SparseCore 0:
  12.9 42.3 all-gather.2
  58.2 51.5 all-gather.4
  387.1 62.7 reduce-scatter.1

commit v4 on v3

--- a/solution.py
+++ b/solution.py
@@ -11,6 +11,7 @@
 CONV_TAPS = 4
 R = 48
 EPS = 1e-05
+VECTORS = CONV_TAPS + 2 + N + 1
 BLK = 8
 LANES = 128
 F32 = jnp.float32
@@ -603,32 +604,24 @@
     return x * lax.rsqrt(jnp.mean(x * x, -1, keepdims=True) + EPS)
 
 
-def inner_grad_kernel(
-    seqs,
-    du_ref,
-    dproj_ref,
-    conv_ref,
-    ext_ref,
-    normed_ref,
-    x_ref,
-    u_ref,
-    rank_ref,
-    dstep_ref,
-    dgate_ref,
-    w_in_ref,
-    w_gate_ref,
-    w_x_ref,
-    taps_ref,
-    after_ref,
-    late_ref,
-    early_ref,
-    gin_ref,
-    gx_ref,
-    gdt_ref,
-    chan_ref,
-    gain_ref,
-    dconv,
-):
+def inner_grad_step(seqs, refs, x, sums, dconv):
+    (
+        du_ref,
+        dproj_ref,
+        conv_ref,
+        ext_ref,
+        normed_ref,
+        u_ref,
+        rank_ref,
+        dstep_ref,
+        dgate_ref,
+        w_in_ref,
+        w_gate_ref,
+        w_x_ref,
+        taps_ref,
+        after_ref,
+    ) = refs
+    gin_ref, narrow_ref, chan_ref, gain_ref = sums
     rows, chans = du_ref.shape
     rim = (CONV_TAPS - 1) * seqs
     turn = pl.program_id(0)
@@ -636,7 +629,7 @@
 
     @pl.when(turn == 0)
     def _():
-        for ref in (gin_ref, gx_ref, gdt_ref, chan_ref, gain_ref):
+        for ref in sums:
             ref[...] = jnp.zeros_like(ref)
         dconv[rows:, :] = after_ref[...]
 
@@ -661,20 +654,212 @@
     chan_ref[CONV_TAPS * seqs :, :] += by_seq(d_conv)
     d_inner = d_inner.astype(BF16)
     part = dot(d_inner, w_in_ref[...]) + dot(dgate_ref[...], w_gate_ref[...])
-    half = pl.num_programs(0) // 2
+    gain_ref[...] += by_seq(part * normalized(x.astype(F32)))
+    gin_ref[...] += dot(d_inner, normed_ref[...], TN)
+    narrow = dot(u_ref[...], d_proj, TN) + dot(dstep_ref[...], rank_ref[...], TN)
+    narrow_ref[...] = narrow_ref[...] + narrow
+    return part
+
+
+def inner_grad_kernel(seqs, *refs):
+    refs, x_ref, late_ref, early_ref, sums, dconv = (
+        refs[:14],
+        refs[14],
+        refs[15],
+        refs[16],
+        refs[17:21],
+        refs[21],
+    )
+    part = inner_grad_step(seqs, refs, x_ref[...], sums, dconv).astype(BF16)
+    turn, half = pl.program_id(0), pl.num_programs(0) // 2
 
     @pl.when(turn < half)
     def _():
-        late_ref[...] = part.astype(BF16)
+        late_ref[...] = part
 
     @pl.when(turn >= half)
     def _():
-        early_ref[...] = part.astype(BF16)
-
-    gain_ref[...] += by_seq(part * normalized(x_ref[...].astype(F32)))
-    gin_ref[...] += dot(d_inner, normed_ref[...], TN)
-    gx_ref[...] += dot(u_ref[...], d_proj, TN)
-    gdt_ref[...] += dot(dstep_ref[...], rank_ref[...], TN)
+        early_ref[...] = part
+
+
+def finish_kernel(shape, sizes, turns, *refs):
+    micros, group = shape
+    seqs = micros * group
+    step_refs, refs = refs[:14], refs[14:]
+    x_ref, dres_ref, act_own_ref, act_got_ref, g_ref, vec_ref, routing_ref, early_ref = refs[:8]
+    grad_ref, act_ref, in_ref, out_ref, proj_ref, step_ref, channel_ref, route_ref, tail_ref = refs[
+        8:17
+    ]
+    refs = refs[7:]
+    sums, dconv, sent, got, gain_got, tail, grad_tok, act_tok = (
+        refs[10:14],
+        refs[14],
+        refs[15],
+        refs[16],
+        refs[17],
+        refs[18],
+        refs[19],
+        refs[20],
+    )
+    mine_ref = refs[21]
+    refs = refs[22:]
+    bits = [("ctx", 1 << k) for k in range(sizes[1].bit_length() - 1)]
+    bits += [("fsdp", 1 << k) for k in range(sizes[0].bit_length() - 1)]
+    stages = len(bits)
+    sends, gots = refs[:stages], refs[stages : 2 * stages]
+    part_sems, gain_sems, sum_sems = (
+        refs[2 * stages : 2 * stages + 2],
+        refs[2 * stages + 2 : 2 * stages + 4],
+        refs[2 * stages + 4 : 2 * stages + 6],
+    )
+    where = {axis: lax.axis_index(axis) for axis in ("fsdp", "ctx", "tensor")}
+    across = (where["fsdp"], where["ctx"], 1 - where["tensor"])
+    high = [lax.rem(where[axis] // bit, 2) for axis, bit in bits]
+    partners = []
+    for (axis, bit), one in zip(bits, high):
+        to = dict(where)
+        to[axis] = where[axis] + bit - 2 * bit * one
+        partners.append((to["fsdp"], to["ctx"], to["tensor"]))
+
+    def remote(src, dst, sems, at, to):
+        return pltpu.make_async_remote_copy(
+            src_ref=src,
+            dst_ref=dst,
+            send_sem=sems[0].at[at],
+            recv_sem=sems[1].at[at],
+            device_id=to,
+            device_id_type=MESH,
+        )
+
+    blocks = [pl.ds(0, 1), pl.ds(1, turns - 2), pl.ds(turns - 1, 1)]
+
+    def part_copy(which):
+        at = blocks[which]
+        return remote(sent.at[at], got.at[at], part_sems, which, across)
+
+    def sum_copy(stage, half):
+        source = sends[stage].at[half, 1 - high[stage]]
+        return remote(source, gots[stage].at[half], sum_sems, (stage, half), partners[stage])
+
+    turn = pl.program_id(0)
+
+    @pl.when(turn == 0)
+    def _():
+        greet([across] + partners)
+
+    rows = step_refs[0].shape[0]
+    first = pl.multiple_of((turns - 1 - turn) * rows, rows)
+    part = inner_grad_step(seqs, step_refs, x_ref[pl.ds(first, rows), :], sums, dconv)
+    sent[turn] = part.astype(BF16)
+
+    @pl.when(turn == 0)
+    def _():
+        part_copy(0).start()
+
+    @pl.when(turn == turns - 2)
+    def _():
+        part_copy(0).wait_send()
+        part_copy(1).start()
+
+
+    def output(which):
+        at = slice((turns - 1 - which) * rows, (turns - which) * rows)
+        x = x_ref[at, :].astype(F32)
+        width = x.shape[1]
+        scale = lax.rsqrt(jnp.mean(x * x, -1, keepdims=True) + EPS)
+        xhat = x * scale
+        scaled = g_ref[...] * (sent[which].astype(F32) + got[which].astype(F32))
+        mean = jnp.mean(scaled * xhat, -1, keepdims=True)
+        grad = dres_ref[at, :].astype(F32) + scale * (scaled - xhat * mean)
+        own, other = act_own_ref[at, :].astype(F32), act_got_ref[0, at, :].astype(F32)
+        left = where["tensor"] == 0
+        act = jnp.concatenate([jnp.where(left, own, other), jnp.where(left, other, own)], 1)
+        count = rows // seqs
+        times = slice((turns - 1 - which) * count, (turns - which) * count)
+        for k in range(width // LANES):
+            grad_tok[k] = grad[:, lanes(k)]
+            act_tok[k] = act[:, lanes(k)]
+        for m in range(micros):
+            for g in range(group):
+                every = pl.ds(m * group + g, count, stride=seqs)
+                for k in range(width // LANES):
+                    grad_ref[m, g, times, lanes(k)] = grad_tok[k, every, :]
+                    act_ref[m, g, times, lanes(k)] = act_tok[k, every, :].astype(BF16)
+
+    @pl.when(turn == turns - 1)
+    def _():
+        gin_ref, narrow_ref, chan_ref, gain_ref = sums
+        gain_copy = remote(gain_ref, gain_got, gain_sems, 0, across)
+        gain_copy.start()
+        owned = mine_ref.shape[0]
+        half_cols = mine_ref.shape[1] // 2
+        rest = gin_ref.shape[1] - half_cols
+
+        def fill(stage, half):
+            count = 1 << (stages - stage)
+            for k in range(count):
+                target = (half, k % 2, k // 2)
+                if stage > 0:
+                    before = (half, high[stage - 1], k)
+                    value = sends[stage - 1][before].astype(F32)
+                    value = value + gots[stage - 1][half, k].astype(F32)
+                    sends[stage][target] = value.astype(BF16)
+                    continue
+                at = slice(k * owned, (k + 1) * owned)
+                if half == 0:
+                    sends[0][target] = gin_ref[at, :half_cols].astype(BF16)
+                else:
+                    joined = [gin_ref[at, half_cols:], narrow_ref[at, :], tail[at, :]]
+                    sends[0][target] = jnp.concatenate(joined, 1).astype(BF16)
+            sum_copy(stage, half).start()
+
+        fill(0, 0)
+        gain_copy.wait()
+        vec = vec_ref[...]
+        row = lax.broadcasted_iota(jnp.int32, vec.shape, 0)
+        for k in range(CONV_TAPS + 1):
+            value = jnp.sum(chan_ref[k * seqs : (k + 1) * seqs, :], 0, keepdims=True)
+            vec = jnp.where(row == k, value, vec)
+        gain = jnp.sum(gain_ref[...] + gain_got[...], 0, keepdims=True)
+        vec = jnp.where(row == VECTORS, gain, vec)
+        tail[...] = vec.T + routing_ref[...]
+        fill(0, 1)
+        part_copy(0).wait_recv()
+        output(0)
+        for stage in range(1, stages):
+            for half in range(2):
+                sum_copy(stage - 1, half).wait_recv()
+                fill(stage, half)
+            if stage == 1:
+                part_copy(1).wait()
+                part_copy(2).start()
+            if stage < turns - 1:
+                output(stage)
+        for which in range(stages, turns - 1):
+            output(which)
+        part_copy(2).wait_recv()
+        output(turns - 1)
+        for half in range(2):
+            sum_copy(stages - 1, half).wait_recv()
+            value = sends[stages - 1][half, high[stages - 1], 0].astype(F32)
+            mine_ref[:, half * half_cols : (half + 1) * half_cols] = value + gots[stages - 1][
+                half, 0
+            ].astype(F32)
+        width, cols = in_ref.shape[2], proj_ref.shape[1]
+        in_ref[0] = mine_ref[:, :width]
+        in_ref[1] = early_ref[:, :width].astype(F32)
+        out_ref[...] = early_ref[:, width:].astype(F32)
+        proj_ref[...] = mine_ref[:, width : width + cols]
+        step_ref[...] = mine_ref[:, width + cols : width + cols + R]
+        at = width + LANES
+        channel_ref[...] = mine_ref[:, at : at + VECTORS - 1]
+        at += VECTORS + 1
+        route_ref[...] = mine_ref[:, at : at + route_ref.shape[1]]
+        tail_ref[...] = mine_ref[:, width + LANES :]
+        for stage in range(stages):
+            for half in range(2):
+                sum_copy(stage, half).wait_send()
+        part_copy(2).wait_send()
 
 
 def output_kernel(shape, peers, *refs):
@@ -1039,9 +1224,7 @@
     d_gate_z = (d_gated * y_vals * gate_slope).astype(BF16)
 
     def owned(value):
-        return lax.psum_scatter(
-            value.astype(BF16), OWNERS, scatter_dimension=0, tiled=True
-        ).astype(F32)
+        return lax.psum_scatter(value.astype(BF16), OWNERS, scatter_dimension=0, tiled=True)
 
     grad_end, act_others, early = carried(
         start_grad, log_decay, rates, -1, 1, act_half, (d_gate_z, normed1, gated, d_mixed)
@@ -1107,9 +1290,8 @@
         from_end(conv),
         whole(extended),
         from_end(normed1),
-        from_end(x_tok),
         from_end(u),
-        from_end(rank),
+        from_end(jnp.pad(rank, ((0, 0), (x_cols, LANES - x_cols - R)))),
         from_end(d_step),
         from_end(d_gate_z),
         whole(w_in),
@@ -1118,6 +1300,102 @@
         whole(taps),
         whole(after),
     ]
+    rows_each = narrow.shape[0]
+    decay_grad = jnp.sum(rate_grad, 1) * rates
+    fused = joined and peers == 2 and rows_each % 16 == 0 and owners >= 4 and VECTORS + 2 + experts <= LANES
+    if fused:
+        vectors = jnp.concatenate([skip_grad[None], decay_grad, step_bias_grad[None]], 0)
+        vectors = jnp.pad(vectors, ((CONV_TAPS + 1, LANES - VECTORS), (0, 0)))
+        routing_wide = jnp.pad(
+            jnp.concatenate([grad_router, gain_grad2[:, None]], 1),
+            ((0, 0), (VECTORS + 1, LANES - VECTORS - 2 - experts)),
+        )
+
+        def entire(value):
+            return value, pl.BlockSpec(value.shape, lambda i: (0,) * value.ndim)
+
+        arrays += [
+            whole(x_tok),
+            whole(d_mixed),
+            whole(act_half),
+            entire(act_others),
+            whole(gains[:1]),
+            whole(vectors),
+            whole(routing_wide),
+            whole(mine_early),
+        ]
+        cols = width + 2 * LANES
+        results = [
+            entire(out(inputs.shape)),
+            entire(out(inputs.shape, BF16)),
+            entire(out((2, rows_each, width))),
+            *[
+                whole(out((rows_each, count)))
+                for count in (width, x_cols, R, VECTORS - 1, experts, LANES)
+            ],
+        ]
+        sizes = (lax.axis_size("fsdp"), lax.axis_size("ctx"))
+        stages = (owners - 1).bit_length()
+        counts = [owners >> (stage + 1) for stage in range(stages)]
+        (
+            input_grad,
+            activations,
+            mine_in,
+            mine_out,
+            mine_x,
+            mine_dt,
+            mine_channel,
+            mine_router,
+            mine_tail,
+        ) = pl.pallas_call(
+            functools.partial(finish_kernel, (micros, group), sizes, turns),
+            grid=(turns,),
+            in_specs=[spec for _, spec in arrays],
+            out_specs=[spec for _, spec in results],
+            out_shape=[value for value, _ in results],
+            scratch_shapes=[
+                pltpu.VMEM((chans, width), F32),
+                pltpu.VMEM((chans, LANES), F32),
+                pltpu.VMEM(((CONV_TAPS + 1) * seqs, chans), F32),
+                pltpu.VMEM((seqs, width), F32),
+                pltpu.VMEM((block + rim, chans), F32),
+                pltpu.VMEM((turns, block, width), BF16),
+                pltpu.VMEM((turns, block, width), BF16),
+                pltpu.VMEM((seqs, width), F32),
+                pltpu.VMEM((chans, LANES), F32),
+                pltpu.VMEM((width // LANES, block, LANES), F32),
+                pltpu.VMEM((width // LANES, block, LANES), F32),
+                pltpu.VMEM((rows_each, cols), F32),
+                *[pltpu.VMEM((2, 2, count, rows_each, cols // 2), BF16) for count in counts],
+                *[pltpu.VMEM((2, count, rows_each, cols // 2), BF16) for count in counts],
+                pltpu.SemaphoreType.DMA((3,)),
+                pltpu.SemaphoreType.DMA((3,)),
+                pltpu.SemaphoreType.DMA((1,)),
+                pltpu.SemaphoreType.DMA((1,)),
+                pltpu.SemaphoreType.DMA((stages, 2)),
+                pltpu.SemaphoreType.DMA((stages, 2)),
+            ],
+            compiler_params=pltpu.CompilerParams(
+                collective_id=3, has_side_effects=True, vmem_limit_bytes=63 << 20
+            ),
+        )(*[value for value, _ in arrays])
+        mine_bias = mine_tail[:, VECTORS - 1]
+        gains_out = jnp.stack([mine_tail[:, VECTORS], mine_tail[:, VECTORS + 1 + experts]])
+        return (
+            activations,
+            input_grad,
+            gains_out,
+            mine_router,
+            mine_in,
+            mine_x,
+            mine_dt,
+            mine_bias,
+            mine_channel,
+            mine_out,
+            grad_up[None],
+            grad_down[None],
+        )
+    arrays.append(from_end(x_tok))
     results = [
         (
             out((tokens // 2, width), BF16),
@@ -1131,11 +1409,10 @@
         ),
         whole(out((chans, width))),
         whole(out((chans, LANES))),
-        whole(out((chans, R))),
         whole(out(((CONV_TAPS + 1) * seqs, chans))),
         whole(out((seqs, width))),
     ]
-    late_part, early_part, grad_in, grad_xproj, grad_dt, conv_sums, gain_sums = pl.pallas_call(
+    late_part, early_part, grad_in, narrow_sums, conv_sums, gain_sums = pl.pallas_call(
         functools.partial(inner_grad_kernel, seqs),
         grid=(turns,),
         in_specs=[spec for _, spec in arrays],
@@ -1145,7 +1422,7 @@
         compiler_params=pltpu.CompilerParams(vmem_limit_bytes=62 << 20),
     )(*[value for value, _ in arrays])
     late_part, mine_early = lax.optimization_barrier((late_part, mine_early))
-    grad_xproj = grad_xproj[:, :x_cols]
+    grad_xproj, grad_dt = narrow_sums[:, :x_cols], narrow_sums[:, x_cols : x_cols + R]
     conv_sums = jnp.sum(conv_sums.reshape(CONV_TAPS + 1, seqs, chans), 1)
     gain_grad1 = jnp.sum(gain_sums, 0)
 
@@ -1155,7 +1432,7 @@
             grad_dt,
             conv_sums.T,
             skip_grad[:, None],
-            (jnp.sum(rate_grad, 1) * rates).T,
+            decay_grad.T,
             step_bias_grad[:, None],
         ],
         1,
@@ -1224,12 +1501,12 @@
         input_grad,
         gains_out,
         mine_routing[:, :experts],
-        jnp.stack([mine[:, :width], mine_early[:, :width]]),
+        jnp.stack([mine[:, :width], mine_early[:, :width].astype(F32)]),
         mine_tail[:, : cuts[0]],
         mine_tail[:, cuts[0] : cuts[1]],
         mine_tail[:, cuts[2]],
         mine_tail[:, cuts[1] : cuts[2]],
-        mine_early[:, width:],
+        mine_early[:, width:].astype(F32),
         grad_up[None],
         grad_down[None],
     )

time: 566 us -> 553 us (0.977)
  Pallas kernels: 216 us -> 255 us
  waiting for transfers between devices: 117 us -> 85.1 us
  other arithmetic: 45.5 us -> 31.4 us
  starting transfers between devices: 52.5 us -> 42.4 us
    pallas_call x2 -> x1, Pallas kernels: 22.8 us -> 61.8 us  [per_device(): pl.pallas_call(functools.partial(finish_kernel, (micros, group), sizes, t...]
    ppermute x4 -> x0, waiting for transfers between devices: 18.8 us -> none  [halved(): lax.ppermute(other, axis, [(i, i ^ bit) for i in range(lax.axis_size(axis...]
    ppermute x11 -> x8, waiting for transfers between devices: 36.6 us -> 24.2 us  [swapped(): return lax.ppermute(value, 'tensor', [(0, 1), (1, 0)])]
    unnamed x113 -> x115, local copies, waits for them, and re-layouts: 11.4 us -> 19 us
    ppermute x4 -> x0, starting transfers between devices: 7.26 us -> none  [halved(): lax.ppermute(other, axis, [(i, i ^ bit) for i in range(lax.axis_size(axis...]
  transfers between devices with their start and end apart: 26 -> 19, of which waited for: 17 -> 12; matrix products, arithmetic and copies ran while one was open for 21% -> 18% of each run, Pallas kernels for 26% -> 18%
where the time goes in v4:
time: 553 us; the launch traced here: 543 us
  Pallas kernels  255 us (46%)
  waiting for transfers between devices  85.1 us (15%)
  matrix products  67.2 us (12%)
  local copies, waits for them, and re-layouts  46 us (8%)
  starting transfers between devices  42.4 us (8%)
  other arithmetic  31.4 us (6%)
  between operations  15.3 us (3%)
    pallas_call x3, Pallas kernels, scan_call(): pl.pallas_call(kernel, grid=(chans // width,), in_specs=[spec(shape, kind...  96.1 us
    pallas_call x1, Pallas kernels, per_device(): pl.pallas_call(functools.partial(finish_kernel, (micros, group), sizes, t...  61.8 us
    pallas_call x2, Pallas kernels, carried(): pl.pallas_call(functools.partial(carry_kernel, sign, ranges, peers), in_s...  50.6 us
    pallas_call x1, Pallas kernels, per_device(): pl.pallas_call(functools.partial(forward_kernel, peers), grid=(pieces, gr...  46.9 us
    dot_general x8, matrix products, product(): return jnp.einsum(terms, a, b, preferred_element_type=F32)  36.8 us
    all_to_all x6, starting transfers between devices, swap_owners(): lax.all_to_all(value, OWNERS, split_axis=0, concat_axis=0, tiled=True)  30.7 us
    all_gather x1, waiting for transfers between devices, per_device(): full = lax.all_gather(first, OWNERS, axis=0, tiled=True)  27 us
    all_to_all x6, waiting for transfers between devices, swap_owners(): lax.all_to_all(value, OWNERS, split_axis=0, concat_axis=0, tiled=True)  26.5 us
  transfers between devices with their start and end apart: 19, of which 12 were waited for; matrix products, arithmetic and copies ran while one was open for 18% of the time, Pallas kernels for 18%

profile of v4, /device:TPU:0, one launch (start us, length us, event | category | flops | bytes accessed | tf_op | source)
XLA Modules:
  0.0 542.9 jit_solution(8843056420401107368)
XLA Ops:
  14.4 2.6 copy.81
  20.4 2.6 copy.83
  24.2 4.1 fusion.35
  28.3 27.0 %all-gather.3.cloned.1.call-done = bf16[768,1024]{1,0:T(8,128)(2,1)} async-done(((bf16[48,1024]{1,0:T(8,128)(2,1)}), bf16[768,1024]{1,0:T(8,128)(2,1)}) %all-gather.3.cloned.1.call-update) | async-done | bytes 1572880 | tf_op jit(solution)/shard_map/all_gather | solution.py:972
  58.3 1.8 fusion.17.refs_2_.refs_4_
  61.6 2.2 collective-permute-start
  64.9 3.7 fusion.111
  72.4 6.4 %all-to-all-start = ((bf16[16,50,768]{2,1,0:T(8,128)(2,1)}), bf16[16,50,768]{2,1,0:T(8,128)(2,1)}, u32[]{:S(2)}, u32[]{:S(2)}) async-start(bf16[16,50,768]{2,1,0:T(8,128)(2,1)} %fusion.35), calls=%async_computation | async-start | bytes 2752512 | tf_op jit(solution)/shard_map/all_to_all | solution.py:997
  81.4 6.0 %add_divide_fusion = (f32[1024,768]{1,0:T(8,128)}, f32[1024,768]{1,0:T(8,128)}) fusion(f32[768]{0:T(1024)S(1)} %convert_reduce_fusion, bf16[768,1024]{1,0:T(8,128)(2,1)} %all-gather.3.cloned.1.call-done, f32[1024,80]{1,0:T(8,128)S(1)} %convert_add_fusion), kind=kOutput, calls=%fused_computation.39 | convolution fusion | flops 83361792 | bytes 6754304 | tf_op jit(solution)/shard_map/dot_general | solution.py:80
  87.5 16.6 %shard_map.238 = f32[17,8,768]{2,1,0:T(8,128)} custom-call(f32[1024,768]{1,0:T(8,128)} %get-tuple-element.152.d_ref, f32[1024,768]{1,0:T(8,128)} %get-tuple-element.145.u_ref, f32[1024,16]{1,0:T(8,128)} %get-tuple-element.162.b_ref, f32[16,768]{1,0:T(8,128)} %fusion.86.r_ref), custom_call_target="tpu_custom_call" | custom-call | flops 22649241600 | bytes 12582912 | tf_op jit(solution)/shard_map/pallas_call | solution.py:916
  104.0 5.8 %all-gather.5.cloned.1.call-done = bf16[768,1536]{1,0:T(8,128)(2,1)} async-done(((bf16[48,1536]{1,0:T(8,128)(2,1)}), bf16[768,1536]{1,0:T(8,128)(2,1)}) %all-gather.5.cloned.1.call-update) | async-done | bytes 2359312 | tf_op jit(solution)/shard_map/all_gather | solution.py:973
  109.8 3.4 fusion.113
  113.2 3.1 fusion.108.z_ref
  116.3 3.2 all-to-all-done
  119.6 22.5 %shard_map.239.h0_ref = f32[16,8,768]{2,1,0:T(8,128)S(1)} custom-call(f32[16,8,768]{2,1,0:T(8,128)S(1)} %slice.201.end_ref, f32[8,768]{1,0:T(8,128)S(1)} %slice_bitcast_fusion.3.log_ref, f32[16,768]{1,0:T(8,128)S(1)} %copy-done.5), custom_call_target="tpu_custom_call" | custom-call | flops 21474836480 | bytes 1048576 | tf_op jit(solution)/shard_map/pallas_call | solution.py:222
  142.8 46.9 %shard_map.240 = (f32[1024,768]{1,0:T(8,128)}, bf16[1024,768]{1,0:T(8,128)(2,1)}, f32[16,16,8,768]{3,2,1,0:T(8,128)}, f32[1024,768]{1,0:T(8,128)}) custom-call(f32[1024,768]{1,0:T(8,128)} %get-tuple-element.152.d_ref, f32[1024,768]{1,0:T(8,128)} %get-tuple-element.145.u_ref, f32[1024,768]{1,0:T(8,128)} %fusion.108.z_ref, ...), custom_call_target="tpu_custom_call" | custom-call | flops 37748736000 | bytes 12582912 | tf_op jit(solution)/shard_map/pallas_call | solution.py:1110
  189.7 2.3 multiply_reduce_fusion.1
  192.6 2.0 multiply_convert_fusion.2
  194.6 2.0 fusion.46
  196.6 3.6 all-to-all-start.2
  200.2 3.5 convert_multiply_fusion.2
  206.7 10.8 %all-to-all-done.2 = bf16[16,50,384]{2,1,0:T(8,128)(2,1)S(1)} async-done(((bf16[16,50,384]{2,1,0:T(8,128)(2,1)}), bf16[16,50,384]{2,1,0:T(8,128)(2,1)S(1)}, u32[]{:S(2)}, u32[]{:S(2)}) %all-to-all-start.2) | async-done | bytes 614432 | tf_op jit(solution)/shard_map/all_to_all | solution.py:997
  217.5 4.4 all-to-all-start.1
  222.6 5.6 %all-to-all-done.1 = f32[16,1,50]{2,1,0:T(1,128)S(1)} async-done(((f32[16,1,50]{2,1,0:T(1,128)}), f32[16,1,50]{2,1,0:T(1,128)S(1)}, u32[]{:S(2)}, u32[]{:S(2)}) %all-to-all-start.1) | async-done | bytes 3232 | tf_op jit(solution)/shard_map/all_to_all | solution.py:997
  228.3 4.6 fusion.24
  232.9 5.5 %collective-permute-done.2 = bf16[16,50,384]{2,0,1:T(8,128)(2,1)} collective-permute-done((bf16[16,50,384]{2,0,1:T(8,128)(2,1)S(1)}, bf16[16,50,384]{2,0,1:T(8,128)(2,1)}, u32[]{:S(2)}, u32[]{:S(2)}) %collective-permute-start.2) | collective-permute-done | bytes 614432 | tf_op jit(solution)/shard_map/ppermute | solution.py:28
  239.8 7.1 %multiply_reduce_fusion = (f32[16,50]{1,0:T(8,128)}, bf16[16,50,1536]{2,1,0:T(8,128)(2,1)S(1)}, bf16[16,50,1536]{2,1,0:T(8,128)(2,1)S(1)}) fusion(f32[16,50,1536]{2,1,0:T(8,128)S(1)} %fusion.24, bf16[1,768,1536]{2,1,0:T(8,128)(2,1)S(1)} %copy-done.46, bf16[16,50,384]{2,1,0:T(8,128)(2,1)S(1)} %get-tuple-element.160, ...), kind=kOutput, calls=%fused_computation.19 | convolution fusion | flops 1920613632 | bytes 13421696 | tf_op jit(solution)/shard_map/srd,df->srf/dot_general | solution.py:1156
  249.3 5.9 %convolution_bitcast_fusion = f32[1536,768]{1,0:T(8,128)} fusion(bf16[16,50,1536]{2,1,0:T(8,128)(2,1)S(1)} %get-tuple-element.52, bf16[16,50,768]{2,1,0:T(8,128)(2,1)} %all-to-all-done, f32[16,50]{1,0:T(8,128)S(1)} %bitcast.106), kind=kOutput, calls=%fused_computation.23 | convolution fusion | flops 1889280000 | bytes 8408192 | tf_op jit(solution)/shard_map/srf,srd->fd/dot_general | solution.py:1156
  255.2 5.7 %all-to-all-start.4 = ((f32[16,1,50]{2,1,0:T(1,128)}), f32[16,1,50]{2,1,0:T(1,128)S(1)}, u32[]{:S(2)}, u32[]{:S(2)}) async-start(f32[16,1,50]{2,1,0:T(1,128)} %bitcast.29), calls=%async_computation.4 | async-start | bytes 16384 | tf_op jit(solution)/shard_map/all_to_all | solution.py:997
  260.9 4.2 convolution_convert_fusion.1
  267.5 3.6 add_convert_fusion.1
  271.1 6.3 %all-to-all-start.3 = ((bf16[16,50,384]{2,1,0:T(8,128)(2,1)}), bf16[16,50,384]{2,1,0:T(8,128)(2,1)}, u32[]{:S(2)}, u32[]{:S(2)}) async-start(bf16[16,50,384]{2,1,0:T(8,128)(2,1)} %add_convert_fusion.1), calls=%async_computation.3 | async-start | bytes 1376256 | tf_op jit(solution)/shard_map/all_to_all | solution.py:997
  277.4 6.2 %convolution_bitcast_fusion.1 = f32[768,1536]{1,0:T(8,128)} fusion(bf16[16,50,1536]{2,1,0:T(8,128)(2,1)} %copy-done.25, bf16[16,50,384]{2,1,0:T(8,128)(2,1)S(1)} %copy-done.28, bf16[16,50,384]{2,1,0:T(8,128)(2,1)S(1)} %get-tuple-element.159), kind=kOutput, calls=%fused_computation.24 | convolution fusion | flops 1889894400 | bytes 8404992 | tf_op jit(solution)/shard_map/srd,srf->df/dot_general | solution.py:1156
  284.4 3.6 add_convert_fusion
  288.0 6.8 %all-to-all-done.3 = bf16[16,50,384]{2,1,0:T(8,128)(2,1)} async-done(((bf16[16,50,384]{2,1,0:T(8,128)(2,1)}), bf16[16,50,384]{2,1,0:T(8,128)(2,1)}, u32[]{:S(2)}, u32[]{:S(2)}) %all-to-all-start.3) | async-done | bytes 614432 | tf_op jit(solution)/shard_map/all_to_all | solution.py:997
  294.8 2.7 fusion.40
  299.1 2.5 collective-permute-done.5
  309.4 12.5 %collective-permute-done.9 = f32[1,384]{1,0:T(1,128)S(1)} collective-permute-done((f32[1,384]{1,0:T(1,128)S(1)}, f32[1,384]{1,0:T(1,128)S(1)}, u32[]{:S(2)}, u32[]{:S(2)}) %collective-permute-start.9) | collective-permute-done | bytes 1568 | tf_op jit(solution)/shard_map/ppermute | solution.py:28
  322.7 4.3 all-to-all-start.5
  327.4 2.8 fusion.106
  330.5 3.3 multiply_convert_fusion.1
  333.9 16.9 %shard_map.241.end_ref = f32[16,8,768]{2,1,0:T(8,128)} custom-call(f32[1024,768]{1,0:T(8,128)} %get-tuple-element.152.d_ref, f32[1024,768]{1,0:T(8,128)} %get-tuple-element.150.dy_ref, f32[1024,16]{1,0:T(8,128)} %get-tuple-element.161.c_ref, f32[16,768]{1,0:T(8,128)} %fusion.86.r_ref), custom_call_target="tpu_custom_call" | custom-call | flops 22649241600 | bytes 12582912 | tf_op jit(solution)/shard_map/pallas_call | solution.py:916
  350.7 2.7 fusion.43
  355.3 28.1 %shard_map.242 = (f32[16,8,768]{2,1,0:T(8,128)S(1)}, bf16[1,1024,384]{2,1,0:T(8,128)(2,1)S(1)}, bf16[768,1536]{1,0:T(8,128)(2,1)}) custom-call(f32[16,8,768]{2,1,0:T(8,128)S(1)} %copy-done.8, f32[8,768]{1,0:T(8,128)S(1)} %slice_bitcast_fusion.3.log_ref, f32[16,768]{1,0:T(8,128)S(1)} %copy-done.6, ...), custom_call_target="tpu_custom_call" | custom-call | flops 21474836480 | bytes 1048576 | tf_op jit(solution)/shard_map/pallas_call | solution.py:222
  385.1 62.6 %shard_map.243 = (bf16[1024,768]{1,0:T(8,128)(2,1)}, f32[1024,768]{1,0:T(8,128)}, bf16[1024,128]{1,0:T(8,128)(2,1)}, f32[16,8,768]{2,1,0:T(8,128)}, f32[8,768]{1,0:T(8,128)}, /*index=5*/f32[8,768]{1,0:T(8,128)}) custom-call(f32[1024,768]{1,0:T(8,128)} %get-tuple-element.152.d_ref, f32[1024,768]{1,0:T(8,128)} %get-tuple-element.145.u_ref, ...), custom_call_target="tpu_custom_call" | custom-call | flops 90596966400 | bytes 12582912 | tf_op jit(solution)/shard_map/pallas_call | solution.py:916
  452.2 3.7 collective-permute-done.7
  462.0 61.8 %shard_map.244 = (f32[2,4,128,768]{3,2,1,0:T(8,128)}, bf16[2,4,128,768]{3,2,1,0:T(8,128)(2,1)}, f32[2,48,768]{2,1,0:T(8,128)}, f32[48,768]{1,0:T(8,128)}, f32[48...) custom-call(f32[1024,768]{1,0:T(8,128)} %get-tuple-element.63.refs_0_, ...), custom_call_target="tpu_custom_call" | custom-call | tf_op jit(solution)/shard_map/pallas_call | solution.py:1350
  528.9 2.7 copy.107
  (224 shorter events, 69.1 us)
Async XLA Ops:
  7.2 48.1 %all-gather.3.cloned.1.call-start = ((), (), s32[]{:S(2)}) async-start(), calls=%async_computation.7 | async-start | bytes 1671168 | tf_op jit(solution)/shard_map/all_gather | solution.py:972
  12.7 97.1 %all-gather.5.cloned.1.call-start = ((), (), s32[]{:S(2)}) async-start(), calls=%async_computation.8 | async-start | bytes 2506752 | tf_op jit(solution)/shard_map/all_gather | solution.py:973
  23.5 4.9 copy-start.13
  57.1 14.7 %copy-start.33 = (f32[768,22]{0,1:T(8,128)}, f32[768,22]{0,1:T(8,128)S(1)}, u32[]{:S(2)}) copy-start(f32[768,22]{0,1:T(8,128)S(1)} %slice_convert_fusion.1) | copy-start | bytes 202756
  57.1 6.7 %copy-start.39 = (f32[4,768]{1,0:T(4,128)}, f32[4,768]{1,0:T(4,128)S(1)}, u32[]{:S(2)}) copy-start(f32[4,768]{1,0:T(4,128)S(1)} %slice_bitcast_fusion.4.refs_12_) | copy-start | bytes 36868
  60.1 53.0 %copy-start.1 = (bf16[1024,768]{1,0:T(8,128)(2,1)}, bf16[1024,768]{1,0:T(8,128)(2,1)S(1)}, u32[]{:S(2)}) copy-start(bf16[1024,768]{1,0:T(8,128)(2,1)S(1)} %fusion.17.refs_2_.refs_4_) | copy-start | bytes 4718596
  61.6 3.0 collective-permute-start
  64.9 3.7 copy-start.10
  70.2 9.7 %collective-permute-start.1 = (bf16[1024,80]{1,0:T(8,128)(2,1)S(1)}, bf16[1024,80]{1,0:T(8,128)(2,1)S(1)}, u32[]{:S(2)}, u32[]{:S(2)}) collective-permute-start(bf16[1024,80]{1,0:T(8,128)(2,1)S(1)} %convolution_convert_fusion.3), channel_id=1, source_target_pairs={{0,1},{1,0},{2,3},{3,2},{4,5},{5,4},{6,7},{7,6},{8,9},{9,8},{10,11... | collective-permute-start | bytes 491528 | tf_op jit(solution)/shard_map/ppermute | solution.py:28
  72.4 47.1 %all-to-all-start = ((bf16[16,50,768]{2,1,0:T(8,128)(2,1)}), bf16[16,50,768]{2,1,0:T(8,128)(2,1)}, u32[]{:S(2)}, u32[]{:S(2)}) async-start(bf16[16,50,768]{2,1,0:T(8,128)(2,1)} %fusion.35), calls=%async_computation | async-start | bytes 2752512 | tf_op jit(solution)/shard_map/all_to_all | solution.py:997
  80.0 7.4 %copy-start.19 = (f32[1024,80]{1,0:T(8,128)}, f32[1024,80]{1,0:T(8,128)S(1)}, u32[]{:S(2)}) copy-start(f32[1024,80]{1,0:T(8,128)S(1)} %convert_add_fusion) | copy-start | bytes 983044
  109.8 3.4 copy-start.29
  113.2 6.4 %copy-start.35 = (f32[17,8,768]{2,1,0:T(8,128)S(1)}, f32[17,8,768]{2,1,0:T(8,128)}, u32[]{:S(2)}) copy-start(f32[17,8,768]{2,1,0:T(8,128)} %shard_map.238) | copy-start | bytes 1253380
  113.2 6.4 %copy-start.5 = (f32[16,768]{1,0:T(8,128)S(1)}, f32[16,768]{1,0:T(8,128)}, u32[]{:S(2)}) copy-start(f32[16,768]{1,0:T(8,128)} %fusion.86.r_ref) | copy-start | bytes 147460
  196.6 20.9 %all-to-all-start.2 = ((bf16[16,50,384]{2,1,0:T(8,128)(2,1)}), bf16[16,50,384]{2,1,0:T(8,128)(2,1)S(1)}, u32[]{:S(2)}, u32[]{:S(2)}) async-start(bf16[16,50,384]{2,1,0:T(8,128)(2,1)} %fusion.46), calls=%async_computation.2 | async-start | bytes 1376256 | tf_op jit(solution)/shard_map/all_to_all | solution.py:997
  217.5 10.8 %all-to-all-start.1 = ((f32[16,1,50]{2,1,0:T(1,128)}), f32[16,1,50]{2,1,0:T(1,128)S(1)}, u32[]{:S(2)}, u32[]{:S(2)}) async-start(f32[16,1,50]{2,1,0:T(1,128)} %bitcast.13), calls=%async_computation.1 | async-start | bytes 16384 | tf_op jit(solution)/shard_map/all_to_all | solution.py:997
  222.0 16.4 %collective-permute-start.2 = (bf16[16,50,384]{2,0,1:T(8,128)(2,1)S(1)}, bf16[16,50,384]{2,0,1:T(8,128)(2,1)}, u32[]{:S(2)}, u32[]{:S(2)}) collective-permute-start(bf16[16,50,384]{2,0,1:T(8,128)(2,1)S(1)} %copy.86), channel_id=1, source_target_pairs={{0,1},{1,0},{2,3},{3,2},{4,5},{5,4},{6,7},{7,6},{8,9},{9,8},{10,11... | collective-permute-start | bytes 1843208 | tf_op jit(solution)/shard_map/ppermute | solution.py:28
  228.3 11.5 %copy-start.46 = (bf16[1,768,1536]{2,1,0:T(8,128)(2,1)S(1)}, bf16[1,768,1536]{2,1,0:T(8,128)(2,1)}, u32[]{:S(2)}) copy-start(bf16[1,768,1536]{2,1,0:T(8,128)(2,1)} %param.28) | copy-start | bytes 7077892
  239.7 7.2 %copy-start.27 = (bf16[16,50,384]{2,1,0:T(8,128)(2,1)}, bf16[16,50,384]{2,1,0:T(8,128)(2,1)S(1)}, u32[]{:S(2)}) copy-start(bf16[16,50,384]{2,1,0:T(8,128)(2,1)S(1)} %get-tuple-element.160) | copy-start | bytes 1843204
  248.6 16.5 %collective-permute-start.3 = (bf16[16,50,384]{2,0,1:T(8,128)(2,1)S(1)}, bf16[16,50,384]{2,0,1:T(8,128)(2,1)}, u32[]{:S(2)}, u32[]{:S(2)}) collective-permute-start(bf16[16,50,384]{2,0,1:T(8,128)(2,1)S(1)} %copy.89), channel_id=1, source_target_pairs={{0,1},{1,0},{2,3},{3,2},{4,5},{5,4},{6,7},{7,6},{8,9},{9,8},{10,11... | collective-permute-start | bytes 1843208 | tf_op jit(solution)/shard_map/ppermute | solution.py:28
  255.2 15.9 %all-to-all-start.4 = ((f32[16,1,50]{2,1,0:T(1,128)}), f32[16,1,50]{2,1,0:T(1,128)S(1)}, u32[]{:S(2)}, u32[]{:S(2)}) async-start(f32[16,1,50]{2,1,0:T(1,128)} %bitcast.29), calls=%async_computation.4 | async-start | bytes 16384 | tf_op jit(solution)/shard_map/all_to_all | solution.py:997
  260.9 6.6 %copy-start.26 = (bf16[16,50,1536]{2,1,0:T(8,128)(2,1)S(1)}, bf16[16,50,1536]{2,1,0:T(8,128)(2,1)}, u32[]{:S(2)}) copy-start(bf16[16,50,1536]{2,1,0:T(8,128)(2,1)} %copy-done.25) | copy-start | bytes 7372804
  260.9 6.6 %copy-start.47 = (bf16[1,768,1536]{2,1,0:T(8,128)(2,1)S(1)}, bf16[1,768,1536]{2,1,0:T(8,128)(2,1)}, u32[]{:S(2)}) copy-start(bf16[1,768,1536]{2,1,0:T(8,128)(2,1)} %param.28) | copy-start | bytes 7077892
  266.1 11.3 %copy-start.28 = (bf16[16,50,384]{2,1,0:T(8,128)(2,1)S(1)}, bf16[16,50,384]{2,1,0:T(8,128)(2,1)}, u32[]{:S(2)}) copy-start(bf16[16,50,384]{2,1,0:T(8,128)(2,1)} %copy-done.27) | copy-start | bytes 1843204
  266.1 18.3 %collective-permute-start.4 = (bf16[16,50,384]{2,0,1:T(8,128)(2,1)}, bf16[16,50,384]{2,0,1:T(8,128)(2,1)}, u32[]{:S(2)}, u32[]{:S(2)}) collective-permute-start(bf16[16,50,384]{2,0,1:T(8,128)(2,1)} %copy.91), channel_id=1, source_target_pairs={{0,1},{1,0},{2,3},{3,2},{4,5},{5,4},{6,7},{7,6},{8,9},{9,8},{10,11... | collective-permute-start | bytes 1843208 | tf_op jit(solution)/shard_map/ppermute | solution.py:28
  271.1 23.7 %all-to-all-start.3 = ((bf16[16,50,384]{2,1,0:T(8,128)(2,1)}), bf16[16,50,384]{2,1,0:T(8,128)(2,1)}, u32[]{:S(2)}, u32[]{:S(2)}) async-start(bf16[16,50,384]{2,1,0:T(8,128)(2,1)} %add_convert_fusion.1), calls=%async_computation.3 | async-start | bytes 1376256 | tf_op jit(solution)/shard_map/all_to_all | solution.py:997
  277.4 7.0 %copy-start.48 = (bf16[1,1536,768]{2,1,0:T(8,128)(2,1)S(1)}, bf16[1,1536,768]{2,1,0:T(8,128)(2,1)}, u32[]{:S(2)}) copy-start(bf16[1,1536,768]{2,1,0:T(8,128)(2,1)} %param.29) | copy-start | bytes 7077892
  277.4 7.0 %copy-start.51 = (bf16[16,50,1536]{2,1,0:T(8,128)(2,1)S(1)}, bf16[16,50,1536]{2,1,0:T(8,128)(2,1)}, u32[]{:S(2)}) copy-start(bf16[16,50,1536]{2,1,0:T(8,128)(2,1)} %copy-done.50) | copy-start | bytes 7372804
  297.6 4.1 copy-start.18
  297.9 3.7 collective-permute-start.5
  302.7 3.4 copy-start.20
  302.7 19.8 %collective-permute-start.6 = (bf16[1024,384]{1,0:T(8,128)(2,1)S(1)}, bf16[1024,384]{1,0:T(8,128)(2,1)S(1)}, u32[]{:S(2)}, u32[]{:S(2)}) collective-permute-start(bf16[1024,384]{1,0:T(8,128)(2,1)S(1)} %get-tuple-element.154), channel_id=1, source_target_pairs={{0,1},{1,0},{2,3},{3,2},{4,5},{5,4},{6,7},{7,6},{8,9},{9,8},{10,11... | collective-permute-start | bytes 2359304 | tf_op jit(solution)/shard_map/ppermute | solution.py:28
  303.5 5.9 %copy-start.31 = (bf16[768,80]{1,0:T(8,128)(2,1)}, bf16[768,80]{1,0:T(8,128)(2,1)S(1)}, u32[]{:S(2)}) copy-start(bf16[768,80]{1,0:T(8,128)(2,1)S(1)} %slice.188) | copy-start | bytes 368644
  307.0 14.9 %collective-permute-start.9 = (f32[1,384]{1,0:T(1,128)S(1)}, f32[1,384]{1,0:T(1,128)S(1)}, u32[]{:S(2)}, u32[]{:S(2)}) collective-permute-start(f32[1,384]{1,0:T(1,128)S(1)} %broadcast_in_dim.68), channel_id=1, source_target_pairs={{0,1},{1,0},{2,3},{3,2},{4,5},{5,4},{6,7},{7,6},{8,9},{9,8},{10,11... | collective-permute-start | bytes 4616 | tf_op jit(solution)/shard_map/ppermute | solution.py:28
  322.7 7.5 %copy-start.21 = (bf16[1024,768]{1,0:T(8,128)(2,1)}, bf16[1024,768]{1,0:T(8,128)(2,1)S(1)}, u32[]{:S(2)}) copy-start(bf16[1024,768]{1,0:T(8,128)(2,1)S(1)} %pad_maximum_fusion.refs_4_.refs_15_) | copy-start | bytes 4718596
  322.7 28.0 %all-to-all-start.5 = ((bf16[16,50,384]{2,1,0:T(8,128)(2,1)}), bf16[16,50,384]{2,1,0:T(8,128)(2,1)}, u32[]{:S(2)}, u32[]{:S(2)}) async-start(bf16[16,50,384]{2,1,0:T(8,128)(2,1)} %add_convert_fusion), calls=%async_computation.5 | async-start | bytes 1376256 | tf_op jit(solution)/shard_map/all_to_all | solution.py:997
  327.0 134.4 %reduce-scatter.2.cloned.1.call-start = ((), (), s32[]{:S(2)}) async-start(), calls=%async_computation.9 | async-start | bytes 2506752 | tf_op jit(solution)/shard_map/reduce_scatter | solution.py:1227
  333.9 20.0 %copy-start = (bf16[1024,768]{1,0:T(8,128)(2,1)}, bf16[1024,768]{1,0:T(8,128)(2,1)S(1)}, u32[]{:S(2)}) copy-start(bf16[1024,768]{1,0:T(8,128)(2,1)S(1)} %get-tuple-element.149.refs_1_.refs_8_) | copy-start | bytes 4718596
  353.9 29.5 %copy-start.3 = (bf16[1024,384]{1,0:T(8,128)(2,1)}, bf16[1024,384]{1,0:T(8,128)(2,1)S(1)}, u32[]{:S(2)}) copy-start(bf16[1024,384]{1,0:T(8,128)(2,1)S(1)} %multiply_convert_fusion.5.refs_0_.refs_16_) | copy-start | bytes 2359300
  385.1 63.4 %copy-start.37 = (f32[768,16]{0,1:T(8,128)S(1)}, f32[768,16]{0,1:T(8,128)}, u32[]{:S(2)}) copy-start(f32[768,16]{0,1:T(8,128)} %fusion.105) | copy-start | bytes 147460
  385.1 63.3 %copy-start.43 = (f32[768,1]{0,1:T(1,128)S(1)}, f32[768,1]{0,1:T(1,128)}, u32[]{:S(2)}) copy-start(f32[768,1]{0,1:T(1,128)} %maximum_bitcast_fusion) | copy-start | bytes 9220
  385.1 67.1 %copy-start.34 = (f32[768,22]{0,1:T(8,128)S(1)}, f32[768,22]{0,1:T(8,128)}, u32[]{:S(2)}) copy-start(f32[768,22]{0,1:T(8,128)} %copy-done.33) | copy-start | bytes 202756
  447.8 9.2 %copy-start.32 = (bf16[768,80]{1,0:T(8,128)(2,1)S(1)}, bf16[768,80]{1,0:T(8,128)(2,1)}, u32[]{:S(2)}) copy-start(bf16[768,80]{1,0:T(8,128)(2,1)} %copy-done.31) | copy-start | bytes 368644
  447.8 8.1 %collective-permute-start.7 = (bf16[1024,128]{1,0:T(8,128)(2,1)}, bf16[1024,128]{1,0:T(8,128)(2,1)S(1)}, u32[]{:S(2)}, u32[]{:S(2)}) collective-permute-start(bf16[1024,128]{1,0:T(8,128)(2,1)} %get-tuple-element.64), channel_id=1, source_target_pairs={{0,1},{1,0},{2,3},{3,2},{4,5},{5,4},{6,7},{7,6},{8,9},{9,8},{10,11... | collective-permute-start | bytes 786440 | tf_op jit(solution)/shard_map/ppermute | solution.py:28
  457.0 4.4 copy-start.30
  458.2 3.2 collective-permute-start.8
  523.9 7.7 %copy-start.24 = (f32[2,4,128,768]{3,2,1,0:T(8,128)S(1)}, f32[2,4,128,768]{3,2,1,0:T(8,128)}, u32[]{:S(2)}) copy-start(f32[2,4,128,768]{3,2,1,0:T(8,128)} %get-tuple-element.187) | copy-start | bytes 9437188
  531.6 3.6 copy-start.38
  (23 other events, 45.8 us)
Sparse Core Ops, SparseCore 0:
  12.9 42.3 all-gather.2
  58.2 51.5 all-gather.4
  385.2 62.6 reduce-scatter.1

commit v5 on v4

--- a/solution.py
+++ b/solution.py
@@ -156,18 +156,21 @@
                 out_ref[n, :, cols] = out_ref[n, :, cols] + decayed(late, cols, n) * part(n)
             log_out[:, cols] = late + log
 
+    def multiply(k):
+        left, right = left_refs[k], right_refs[k]
+        count = right.shape[1]
+
+        def product(i, _):
+            at = pl.ds(pl.multiple_of(i * LANES, LANES), LANES)
+            value = dot(left[:, at], right[...], TN)
+            products_ref[at, k * count : (k + 1) * count] = value.astype(BF16)
+            return 0
+
+        lax.fori_loop(0, left.shape[1] // LANES, product, 0)
+
     for turn in range(turns):
-        if turn == 1 and peers:
-            for k, (left, right) in enumerate(zip(left_refs, right_refs)):
-                count = right.shape[1]
-
-                def product(i, _, k=k, left=left, right=right, count=count):
-                    at = pl.ds(pl.multiple_of(i * LANES, LANES), LANES)
-                    value = dot(left[:, at], right[...], TN)
-                    products_ref[at, k * count : (k + 1) * count] = value.astype(BF16)
-                    return 0
-
-                lax.fori_loop(0, left.shape[1] // LANES, product, 0)
+        if turn == turns - 1 and peers:
+            multiply(0)
         for group in range(groups):
             cols = slice(group * width, (group + 1) * width)
             own_log = log_ref[:, cols]
@@ -187,6 +190,8 @@
             high = log.astype(BF16).astype(F32)
             sent[turn, group, N * seqs :, :] = jnp.concatenate([high, log - high], 0).astype(BF16)
             copy(turn, group).start()
+    if peers:
+        multiply(1)
     for group in range(groups):
         receive(turns - 1, group)
     for turn in range(turns):
@@ -576,7 +581,7 @@
                 )
             return tuple(new)
 
-        gs = lax.fori_loop(0, BLK, back, gs, unroll=2)
+        gs = lax.fori_loop(0, BLK, back, gs, unroll=4)
         at = pl.ds(pl.multiple_of(i * BLK * seqs, BLK * seqs), BLK * seqs)
         d_step = (dsb[...] * sig_ref[at, :]).astype(BF16)
         dstep_ref[at, :] = d_step
@@ -1094,7 +1099,7 @@
         by_piece(c_vals),
         by_group(rates),
         by_group(skip[None]),
-        (w_out, pl.BlockSpec((lane_width, width), lambda p, j: (j, 0))),
+        (later_full, pl.BlockSpec((lane_width, width), lambda p, j: (j, 1))),
         by_group(state),
         (x_tok, pl.BlockSpec((tokens, width), lambda p, j: (0, 0))),
     ]
@@ -1294,8 +1299,8 @@
         from_end(jnp.pad(rank, ((0, 0), (x_cols, LANES - x_cols - R)))),
         from_end(d_step),
         from_end(d_gate_z),
-        whole(w_in),
-        whole(w_gate),
+        (full, pl.BlockSpec((chans, width), lambda i: (0, 0))),
+        (later_full, pl.BlockSpec((chans, width), lambda i: (0, 0))),
         whole(w_x_wide),
         whole(taps),
         whole(after),

time: 553 us -> 550 us (level)
    unnamed x115 -> x111, local copies, waits for them, and re-layouts: 19 us -> 18.7 us
where the time goes in v5:
time: 550 us; the launch traced here: 540 us
  Pallas kernels  252 us (46%)
  waiting for transfers between devices  86.3 us (16%)
  matrix products  68.4 us (12%)
  local copies, waits for them, and re-layouts  43.8 us (8%)
  starting transfers between devices  42.8 us (8%)
  other arithmetic  31.4 us (6%)
  between operations  15.3 us (3%)
    pallas_call x3, Pallas kernels, scan_call(): pl.pallas_call(kernel, grid=(chans // width,), in_specs=[spec(shape, kind...  95 us
    pallas_call x1, Pallas kernels, per_device(): pl.pallas_call(functools.partial(finish_kernel, (micros, group), sizes, t...  61.6 us
    pallas_call x2, Pallas kernels, carried(): pl.pallas_call(functools.partial(carry_kernel, sign, ranges, peers), in_s...  48.3 us
    pallas_call x1, Pallas kernels, per_device(): pl.pallas_call(functools.partial(forward_kernel, peers), grid=(pieces, gr...  47 us
    dot_general x8, matrix products, product(): return jnp.einsum(terms, a, b, preferred_element_type=F32)  36.8 us
    all_to_all x6, starting transfers between devices, swap_owners(): lax.all_to_all(value, OWNERS, split_axis=0, concat_axis=0, tiled=True)  30.7 us
    all_to_all x6, waiting for transfers between devices, swap_owners(): lax.all_to_all(value, OWNERS, split_axis=0, concat_axis=0, tiled=True)  28.7 us
    all_gather x1, waiting for transfers between devices, per_device(): full = lax.all_gather(first, OWNERS, axis=0, tiled=True)  27 us
  transfers between devices with their start and end apart: 19, of which 12 were waited for; matrix products, arithmetic and copies ran while one was open for 18% of the time, Pallas kernels for 18%

profile of v5, /device:TPU:0, one launch (start us, length us, event | category | flops | bytes accessed | tf_op | source)
XLA Modules:
  0.0 539.9 jit_solution(5363988708946943753)
XLA Ops:
  14.4 2.6 copy.81
  20.4 2.6 copy.83
  24.2 4.1 fusion.35
  28.3 27.0 %all-gather.3.cloned.1.call-done.refs_9_ = bf16[768,1024]{1,0:T(8,128)(2,1)} async-done(((bf16[48,1024]{1,0:T(8,128)(2,1)}), bf16[768,1024]{1,0:T(8,128)(2,1)}) %all-gather.3.cloned.1.call-update) | async-done | bytes 1572880 | tf_op jit(solution)/shard_map/all_gather | solution.py:977
  55.3 1.7 copy.82
  58.3 1.8 fusion.17.refs_2_.refs_4_
  61.6 2.2 collective-permute-start
  64.9 3.7 fusion.111
  72.5 6.4 %all-to-all-start = ((bf16[16,50,768]{2,1,0:T(8,128)(2,1)}), bf16[16,50,768]{2,1,0:T(8,128)(2,1)}, u32[]{:S(2)}, u32[]{:S(2)}) async-start(bf16[16,50,768]{2,1,0:T(8,128)(2,1)} %fusion.35), calls=%async_computation | async-start | bytes 2752512 | tf_op jit(solution)/shard_map/all_to_all | solution.py:1002
  81.4 6.0 %add_divide_fusion = (f32[1024,768]{1,0:T(8,128)}, f32[1024,768]{1,0:T(8,128)}) fusion(f32[768]{0:T(1024)S(1)} %convert_reduce_fusion, bf16[768,1024]{1,0:T(8,128)(2,1)} %all-gather.3.cloned.1.call-done.refs_9_, f32[1024,80]{1,0:T(8,128)S(1)} %convert_add_fusion), kind=kOutput, calls=%fused_computation.39 | convolution fusion | flops 83361792 | bytes 6754304 | tf_op jit(solution)/shard_map/dot_general | solution.py:80
  87.4 16.6 %shard_map.238 = f32[17,8,768]{2,1,0:T(8,128)} custom-call(f32[1024,768]{1,0:T(8,128)} %get-tuple-element.152.d_ref, f32[1024,768]{1,0:T(8,128)} %get-tuple-element.145.u_ref, f32[1024,16]{1,0:T(8,128)} %get-tuple-element.160.b_ref, f32[16,768]{1,0:T(8,128)} %fusion.91.r_ref), custom_call_target="tpu_custom_call" | custom-call | flops 22649241600 | bytes 12582912 | tf_op jit(solution)/shard_map/pallas_call | solution.py:921
  104.0 5.8 %all-gather.5.cloned.1.call-done.w_ref.refs_10_ = bf16[768,1536]{1,0:T(8,128)(2,1)} async-done(((bf16[48,1536]{1,0:T(8,128)(2,1)}), bf16[768,1536]{1,0:T(8,128)(2,1)}) %all-gather.5.cloned.1.call-update) | async-done | bytes 2359312 | tf_op jit(solution)/shard_map/all_gather | solution.py:978
  109.8 4.4 fusion.51.z_ref
  114.2 5.3 all-to-all-done
  119.6 22.5 %shard_map.239.h0_ref = f32[16,8,768]{2,1,0:T(8,128)S(1)} custom-call(f32[16,8,768]{2,1,0:T(8,128)S(1)} %slice.200.end_ref, f32[8,768]{1,0:T(8,128)S(1)} %slice_bitcast_fusion.3.log_ref, f32[16,768]{1,0:T(8,128)S(1)} %copy-done.5), custom_call_target="tpu_custom_call" | custom-call | flops 21474836480 | bytes 1048576 | tf_op jit(solution)/shard_map/pallas_call | solution.py:227
  142.9 47.0 %shard_map.240 = (f32[1024,768]{1,0:T(8,128)}, bf16[1024,768]{1,0:T(8,128)(2,1)}, f32[16,16,8,768]{3,2,1,0:T(8,128)}, f32[1024,768]{1,0:T(8,128)}) custom-call(f32[1024,768]{1,0:T(8,128)} %get-tuple-element.152.d_ref, f32[1024,768]{1,0:T(8,128)} %get-tuple-element.145.u_ref, f32[1024,768]{1,0:T(8,128)} %fusion.51.z_ref, ...), custom_call_target="tpu_custom_call" | custom-call | flops 37748736000 | bytes 12582912 | tf_op jit(solution)/shard_map/pallas_call | solution.py:1115
  189.9 2.3 multiply_reduce_fusion.1
  192.7 2.1 multiply_convert_fusion.2
  194.8 2.0 fusion.46
  196.8 3.6 all-to-all-start.2
  200.4 3.4 convert_multiply_fusion.2
  206.8 10.9 %all-to-all-done.2 = bf16[16,50,384]{2,1,0:T(8,128)(2,1)S(1)} async-done(((bf16[16,50,384]{2,1,0:T(8,128)(2,1)}), bf16[16,50,384]{2,1,0:T(8,128)(2,1)S(1)}, u32[]{:S(2)}, u32[]{:S(2)}) %all-to-all-start.2) | async-done | bytes 614432 | tf_op jit(solution)/shard_map/all_to_all | solution.py:1002
  217.7 4.4 all-to-all-start.1
  222.9 5.6 %all-to-all-done.1 = f32[16,1,50]{2,1,0:T(1,128)S(1)} async-done(((f32[16,1,50]{2,1,0:T(1,128)}), f32[16,1,50]{2,1,0:T(1,128)S(1)}, u32[]{:S(2)}, u32[]{:S(2)}) %all-to-all-start.1) | async-done | bytes 3232 | tf_op jit(solution)/shard_map/all_to_all | solution.py:1002
  228.5 4.6 fusion.24
  233.1 5.5 %collective-permute-done.2 = bf16[16,50,384]{2,0,1:T(8,128)(2,1)} collective-permute-done((bf16[16,50,384]{2,0,1:T(8,128)(2,1)S(1)}, bf16[16,50,384]{2,0,1:T(8,128)(2,1)}, u32[]{:S(2)}, u32[]{:S(2)}) %collective-permute-start.2) | collective-permute-done | bytes 614432 | tf_op jit(solution)/shard_map/ppermute | solution.py:28
  240.0 7.1 %multiply_reduce_fusion = (f32[16,50]{1,0:T(8,128)}, bf16[16,50,1536]{2,1,0:T(8,128)(2,1)S(1)}, bf16[16,50,1536]{2,1,0:T(8,128)(2,1)S(1)}) fusion(f32[16,50,1536]{2,1,0:T(8,128)S(1)} %fusion.24, bf16[1,768,1536]{2,1,0:T(8,128)(2,1)S(1)} %copy-done.44, bf16[16,50,384]{2,1,0:T(8,128)(2,1)S(1)} %get-tuple-element.158, ...), kind=kOutput, calls=%fused_computation.19 | convolution fusion | flops 1920613632 | bytes 13421696 | tf_op jit(solution)/shard_map/srd,df->srf/dot_general | solution.py:1161
  249.5 5.9 %convolution_bitcast_fusion = f32[1536,768]{1,0:T(8,128)} fusion(bf16[16,50,1536]{2,1,0:T(8,128)(2,1)S(1)} %get-tuple-element.52, bf16[16,50,768]{2,1,0:T(8,128)(2,1)} %all-to-all-done, f32[16,50]{1,0:T(8,128)S(1)} %bitcast.106), kind=kOutput, calls=%fused_computation.23 | convolution fusion | flops 1889280000 | bytes 8408192 | tf_op jit(solution)/shard_map/srf,srd->fd/dot_general | solution.py:1161
  255.4 5.8 %all-to-all-start.4 = ((f32[16,1,50]{2,1,0:T(1,128)}), f32[16,1,50]{2,1,0:T(1,128)S(1)}, u32[]{:S(2)}, u32[]{:S(2)}) async-start(f32[16,1,50]{2,1,0:T(1,128)} %bitcast.29), calls=%async_computation.4 | async-start | bytes 16384 | tf_op jit(solution)/shard_map/all_to_all | solution.py:1002
  261.1 4.2 convolution_convert_fusion.1
  267.7 3.6 add_convert_fusion.1
  271.3 6.3 %all-to-all-start.3 = ((bf16[16,50,384]{2,1,0:T(8,128)(2,1)}), bf16[16,50,384]{2,1,0:T(8,128)(2,1)}, u32[]{:S(2)}, u32[]{:S(2)}) async-start(bf16[16,50,384]{2,1,0:T(8,128)(2,1)} %add_convert_fusion.1), calls=%async_computation.3 | async-start | bytes 1376256 | tf_op jit(solution)/shard_map/all_to_all | solution.py:1002
  277.6 6.2 %convolution_bitcast_fusion.1 = f32[768,1536]{1,0:T(8,128)} fusion(bf16[16,50,1536]{2,1,0:T(8,128)(2,1)} %copy-done.24, bf16[16,50,384]{2,1,0:T(8,128)(2,1)S(1)} %copy-done.27, bf16[16,50,384]{2,1,0:T(8,128)(2,1)S(1)} %get-tuple-element.157), kind=kOutput, calls=%fused_computation.24 | convolution fusion | flops 1889894400 | bytes 8404992 | tf_op jit(solution)/shard_map/srd,srf->df/dot_general | solution.py:1161
  284.6 3.6 add_convert_fusion
  288.1 6.8 %all-to-all-done.3 = bf16[16,50,384]{2,1,0:T(8,128)(2,1)} async-done(((bf16[16,50,384]{2,1,0:T(8,128)(2,1)}), bf16[16,50,384]{2,1,0:T(8,128)(2,1)}, u32[]{:S(2)}, u32[]{:S(2)}) %all-to-all-start.3) | async-done | bytes 614432 | tf_op jit(solution)/shard_map/all_to_all | solution.py:1002
  295.0 2.7 fusion.40
  299.8 2.0 collective-permute-done.5
  310.2 11.8 %collective-permute-done.9 = f32[1,384]{1,0:T(1,128)S(1)} collective-permute-done((f32[1,384]{1,0:T(1,128)S(1)}, f32[1,384]{1,0:T(1,128)S(1)}, u32[]{:S(2)}, u32[]{:S(2)}) %collective-permute-start.9) | collective-permute-done | bytes 1568 | tf_op jit(solution)/shard_map/ppermute | solution.py:28
  322.9 4.3 all-to-all-start.5
  327.5 2.8 fusion.49
  330.7 3.3 multiply_convert_fusion.1
  334.1 16.8 %shard_map.241.end_ref = f32[16,8,768]{2,1,0:T(8,128)} custom-call(f32[1024,768]{1,0:T(8,128)} %get-tuple-element.152.d_ref, f32[1024,768]{1,0:T(8,128)} %get-tuple-element.150.dy_ref, f32[1024,16]{1,0:T(8,128)} %get-tuple-element.159.c_ref, f32[16,768]{1,0:T(8,128)} %fusion.91.r_ref), custom_call_target="tpu_custom_call" | custom-call | flops 22649241600 | bytes 12582912 | tf_op jit(solution)/shard_map/pallas_call | solution.py:921
  350.9 2.7 fusion.43
  355.4 25.8 %shard_map.242 = (f32[16,8,768]{2,1,0:T(8,128)S(1)}, bf16[1,1024,384]{2,1,0:T(8,128)(2,1)S(1)}, bf16[768,1536]{1,0:T(8,128)(2,1)}) custom-call(f32[16,8,768]{2,1,0:T(8,128)S(1)} %copy-done.8, f32[8,768]{1,0:T(8,128)S(1)} %slice_bitcast_fusion.3.log_ref, f32[16,768]{1,0:T(8,128)S(1)} %copy-done.6, ...), custom_call_target="tpu_custom_call" | custom-call | flops 21474836480 | bytes 1048576 | tf_op jit(solution)/shard_map/pallas_call | solution.py:227
  383.0 61.6 %shard_map.243 = (bf16[1024,768]{1,0:T(8,128)(2,1)}, f32[1024,768]{1,0:T(8,128)}, bf16[1024,128]{1,0:T(8,128)(2,1)}, f32[16,8,768]{2,1,0:T(8,128)}, f32[8,768]{1,0:T(8,128)}, /*index=5*/f32[8,768]{1,0:T(8,128)}) custom-call(f32[1024,768]{1,0:T(8,128)} %get-tuple-element.152.d_ref, f32[1024,768]{1,0:T(8,128)} %get-tuple-element.145.u_ref, ...), custom_call_target="tpu_custom_call" | custom-call | flops 90596966400 | bytes 12582912 | tf_op jit(solution)/shard_map/pallas_call | solution.py:921
  449.4 3.8 collective-permute-done.7
  459.3 61.6 %shard_map.244 = (f32[2,4,128,768]{3,2,1,0:T(8,128)}, bf16[2,4,128,768]{3,2,1,0:T(8,128)(2,1)}, f32[2,48,768]{2,1,0:T(8,128)}, f32[48,768]{1,0:T(8,128)}, f32[48...) custom-call(f32[1024,768]{1,0:T(8,128)} %get-tuple-element.63.refs_0_, ...), custom_call_target="tpu_custom_call" | custom-call | tf_op jit(solution)/shard_map/pallas_call | solution.py:1355
  525.9 2.7 copy.107
  (218 shorter events, 68.9 us)
Async XLA Ops:
  7.2 48.1 %all-gather.3.cloned.1.call-start = ((), (), s32[]{:S(2)}) async-start(), calls=%async_computation.7 | async-start | bytes 1671168 | tf_op jit(solution)/shard_map/all_gather | solution.py:977
  12.7 97.1 %all-gather.5.cloned.1.call-start = ((), (), s32[]{:S(2)}) async-start(), calls=%async_computation.8 | async-start | bytes 2506752 | tf_op jit(solution)/shard_map/all_gather | solution.py:978
  23.5 4.9 copy-start.13
  57.0 3.1 copy-start.16
  57.1 14.8 %copy-start.31 = (f32[768,22]{0,1:T(8,128)}, f32[768,22]{0,1:T(8,128)S(1)}, u32[]{:S(2)}) copy-start(f32[768,22]{0,1:T(8,128)S(1)} %slice_convert_fusion.1) | copy-start | bytes 202756
  57.1 6.7 %copy-start.37 = (f32[4,768]{1,0:T(4,128)}, f32[4,768]{1,0:T(4,128)S(1)}, u32[]{:S(2)}) copy-start(f32[4,768]{1,0:T(4,128)S(1)} %slice_bitcast_fusion.4.refs_12_) | copy-start | bytes 36868
  60.1 49.7 %copy-start.1 = (bf16[1024,768]{1,0:T(8,128)(2,1)}, bf16[1024,768]{1,0:T(8,128)(2,1)S(1)}, u32[]{:S(2)}) copy-start(bf16[1024,768]{1,0:T(8,128)(2,1)S(1)} %fusion.17.refs_2_.refs_4_) | copy-start | bytes 4718596
  61.6 3.0 collective-permute-start
  64.8 3.7 copy-start.10
  70.3 9.7 %collective-permute-start.1 = (bf16[1024,80]{1,0:T(8,128)(2,1)S(1)}, bf16[1024,80]{1,0:T(8,128)(2,1)S(1)}, u32[]{:S(2)}, u32[]{:S(2)}) collective-permute-start(bf16[1024,80]{1,0:T(8,128)(2,1)S(1)} %convolution_convert_fusion.3), channel_id=1, source_target_pairs={{0,1},{1,0},{2,3},{3,2},{4,5},{5,4},{6,7},{7,6},{8,9},{9,8},{10,11... | collective-permute-start | bytes 491528 | tf_op jit(solution)/shard_map/ppermute | solution.py:28
  72.5 47.1 %all-to-all-start = ((bf16[16,50,768]{2,1,0:T(8,128)(2,1)}), bf16[16,50,768]{2,1,0:T(8,128)(2,1)}, u32[]{:S(2)}, u32[]{:S(2)}) async-start(bf16[16,50,768]{2,1,0:T(8,128)(2,1)} %fusion.35), calls=%async_computation | async-start | bytes 2752512 | tf_op jit(solution)/shard_map/all_to_all | solution.py:1002
  80.1 7.3 %copy-start.18 = (f32[1024,80]{1,0:T(8,128)}, f32[1024,80]{1,0:T(8,128)S(1)}, u32[]{:S(2)}) copy-start(f32[1024,80]{1,0:T(8,128)S(1)} %convert_add_fusion) | copy-start | bytes 983044
  104.0 15.6 %copy-start.33 = (f32[17,8,768]{2,1,0:T(8,128)S(1)}, f32[17,8,768]{2,1,0:T(8,128)}, u32[]{:S(2)}) copy-start(f32[17,8,768]{2,1,0:T(8,128)} %shard_map.238) | copy-start | bytes 1253380
  104.0 15.6 %copy-start.5 = (f32[16,768]{1,0:T(8,128)S(1)}, f32[16,768]{1,0:T(8,128)}, u32[]{:S(2)}) copy-start(f32[16,768]{1,0:T(8,128)} %fusion.91.r_ref) | copy-start | bytes 147460
  196.8 20.9 %all-to-all-start.2 = ((bf16[16,50,384]{2,1,0:T(8,128)(2,1)}), bf16[16,50,384]{2,1,0:T(8,128)(2,1)S(1)}, u32[]{:S(2)}, u32[]{:S(2)}) async-start(bf16[16,50,384]{2,1,0:T(8,128)(2,1)} %fusion.46), calls=%async_computation.2 | async-start | bytes 1376256 | tf_op jit(solution)/shard_map/all_to_all | solution.py:1002
  217.7 10.8 %all-to-all-start.1 = ((f32[16,1,50]{2,1,0:T(1,128)}), f32[16,1,50]{2,1,0:T(1,128)S(1)}, u32[]{:S(2)}, u32[]{:S(2)}) async-start(f32[16,1,50]{2,1,0:T(1,128)} %bitcast.13), calls=%async_computation.1 | async-start | bytes 16384 | tf_op jit(solution)/shard_map/all_to_all | solution.py:1002
  222.2 16.4 %collective-permute-start.2 = (bf16[16,50,384]{2,0,1:T(8,128)(2,1)S(1)}, bf16[16,50,384]{2,0,1:T(8,128)(2,1)}, u32[]{:S(2)}, u32[]{:S(2)}) collective-permute-start(bf16[16,50,384]{2,0,1:T(8,128)(2,1)S(1)} %copy.86), channel_id=1, source_target_pairs={{0,1},{1,0},{2,3},{3,2},{4,5},{5,4},{6,7},{7,6},{8,9},{9,8},{10,11... | collective-permute-start | bytes 1843208 | tf_op jit(solution)/shard_map/ppermute | solution.py:28
  228.5 11.5 %copy-start.44 = (bf16[1,768,1536]{2,1,0:T(8,128)(2,1)S(1)}, bf16[1,768,1536]{2,1,0:T(8,128)(2,1)}, u32[]{:S(2)}) copy-start(bf16[1,768,1536]{2,1,0:T(8,128)(2,1)} %param.28) | copy-start | bytes 7077892
  240.0 7.2 %copy-start.26 = (bf16[16,50,384]{2,1,0:T(8,128)(2,1)}, bf16[16,50,384]{2,1,0:T(8,128)(2,1)S(1)}, u32[]{:S(2)}) copy-start(bf16[16,50,384]{2,1,0:T(8,128)(2,1)S(1)} %get-tuple-element.158) | copy-start | bytes 1843204
  248.9 16.5 %collective-permute-start.3 = (bf16[16,50,384]{2,0,1:T(8,128)(2,1)S(1)}, bf16[16,50,384]{2,0,1:T(8,128)(2,1)}, u32[]{:S(2)}, u32[]{:S(2)}) collective-permute-start(bf16[16,50,384]{2,0,1:T(8,128)(2,1)S(1)} %copy.89), channel_id=1, source_target_pairs={{0,1},{1,0},{2,3},{3,2},{4,5},{5,4},{6,7},{7,6},{8,9},{9,8},{10,11... | collective-permute-start | bytes 1843208 | tf_op jit(solution)/shard_map/ppermute | solution.py:28
  255.4 15.9 %all-to-all-start.4 = ((f32[16,1,50]{2,1,0:T(1,128)}), f32[16,1,50]{2,1,0:T(1,128)S(1)}, u32[]{:S(2)}, u32[]{:S(2)}) async-start(f32[16,1,50]{2,1,0:T(1,128)} %bitcast.29), calls=%async_computation.4 | async-start | bytes 16384 | tf_op jit(solution)/shard_map/all_to_all | solution.py:1002
  261.1 6.6 %copy-start.25 = (bf16[16,50,1536]{2,1,0:T(8,128)(2,1)S(1)}, bf16[16,50,1536]{2,1,0:T(8,128)(2,1)}, u32[]{:S(2)}) copy-start(bf16[16,50,1536]{2,1,0:T(8,128)(2,1)} %copy-done.24) | copy-start | bytes 7372804
  261.1 6.6 %copy-start.45 = (bf16[1,768,1536]{2,1,0:T(8,128)(2,1)S(1)}, bf16[1,768,1536]{2,1,0:T(8,128)(2,1)}, u32[]{:S(2)}) copy-start(bf16[1,768,1536]{2,1,0:T(8,128)(2,1)} %param.28) | copy-start | bytes 7077892
  266.3 11.3 %copy-start.27 = (bf16[16,50,384]{2,1,0:T(8,128)(2,1)S(1)}, bf16[16,50,384]{2,1,0:T(8,128)(2,1)}, u32[]{:S(2)}) copy-start(bf16[16,50,384]{2,1,0:T(8,128)(2,1)} %copy-done.26) | copy-start | bytes 1843204
  266.3 18.2 %collective-permute-start.4 = (bf16[16,50,384]{2,0,1:T(8,128)(2,1)}, bf16[16,50,384]{2,0,1:T(8,128)(2,1)}, u32[]{:S(2)}, u32[]{:S(2)}) collective-permute-start(bf16[16,50,384]{2,0,1:T(8,128)(2,1)} %copy.91), channel_id=1, source_target_pairs={{0,1},{1,0},{2,3},{3,2},{4,5},{5,4},{6,7},{7,6},{8,9},{9,8},{10,11... | collective-permute-start | bytes 1843208 | tf_op jit(solution)/shard_map/ppermute | solution.py:28
  271.3 23.7 %all-to-all-start.3 = ((bf16[16,50,384]{2,1,0:T(8,128)(2,1)}), bf16[16,50,384]{2,1,0:T(8,128)(2,1)}, u32[]{:S(2)}, u32[]{:S(2)}) async-start(bf16[16,50,384]{2,1,0:T(8,128)(2,1)} %add_convert_fusion.1), calls=%async_computation.3 | async-start | bytes 1376256 | tf_op jit(solution)/shard_map/all_to_all | solution.py:1002
  277.6 7.0 %copy-start.46 = (bf16[1,1536,768]{2,1,0:T(8,128)(2,1)S(1)}, bf16[1,1536,768]{2,1,0:T(8,128)(2,1)}, u32[]{:S(2)}) copy-start(bf16[1,1536,768]{2,1,0:T(8,128)(2,1)} %param.29) | copy-start | bytes 7077892
  277.6 6.9 %copy-start.49 = (bf16[16,50,1536]{2,1,0:T(8,128)(2,1)S(1)}, bf16[16,50,1536]{2,1,0:T(8,128)(2,1)}, u32[]{:S(2)}) copy-start(bf16[16,50,1536]{2,1,0:T(8,128)(2,1)} %copy-done.48) | copy-start | bytes 7372804
  297.8 4.1 copy-start.17
  298.1 3.7 collective-permute-start.5
  301.9 5.0 copy-start.19
  302.9 19.8 %collective-permute-start.6 = (bf16[1024,384]{1,0:T(8,128)(2,1)S(1)}, bf16[1024,384]{1,0:T(8,128)(2,1)S(1)}, u32[]{:S(2)}, u32[]{:S(2)}) collective-permute-start(bf16[1024,384]{1,0:T(8,128)(2,1)S(1)} %get-tuple-element.154), channel_id=1, source_target_pairs={{0,1},{1,0},{2,3},{3,2},{4,5},{5,4},{6,7},{7,6},{8,9},{9,8},{10,11... | collective-permute-start | bytes 2359304 | tf_op jit(solution)/shard_map/ppermute | solution.py:28
  307.8 14.2 %collective-permute-start.9 = (f32[1,384]{1,0:T(1,128)S(1)}, f32[1,384]{1,0:T(1,128)S(1)}, u32[]{:S(2)}, u32[]{:S(2)}) collective-permute-start(f32[1,384]{1,0:T(1,128)S(1)} %broadcast_in_dim.68), channel_id=1, source_target_pairs={{0,1},{1,0},{2,3},{3,2},{4,5},{5,4},{6,7},{7,6},{8,9},{9,8},{10,11... | collective-permute-start | bytes 4616 | tf_op jit(solution)/shard_map/ppermute | solution.py:28
  322.9 7.5 %copy-start.20 = (bf16[1024,768]{1,0:T(8,128)(2,1)}, bf16[1024,768]{1,0:T(8,128)(2,1)S(1)}, u32[]{:S(2)}) copy-start(bf16[1024,768]{1,0:T(8,128)(2,1)S(1)} %pad_maximum_fusion.refs_4_.refs_15_) | copy-start | bytes 4718596
  322.9 28.0 %all-to-all-start.5 = ((bf16[16,50,384]{2,1,0:T(8,128)(2,1)}), bf16[16,50,384]{2,1,0:T(8,128)(2,1)}, u32[]{:S(2)}, u32[]{:S(2)}) async-start(bf16[16,50,384]{2,1,0:T(8,128)(2,1)} %add_convert_fusion), calls=%async_computation.5 | async-start | bytes 1376256 | tf_op jit(solution)/shard_map/all_to_all | solution.py:1002
  327.2 131.4 %reduce-scatter.2.cloned.1.call-start = ((), (), s32[]{:S(2)}) async-start(), calls=%async_computation.9 | async-start | bytes 2506752 | tf_op jit(solution)/shard_map/reduce_scatter | solution.py:1232
  327.5 3.2 copy-start.22
  334.1 20.0 %copy-start = (bf16[1024,768]{1,0:T(8,128)(2,1)}, bf16[1024,768]{1,0:T(8,128)(2,1)S(1)}, u32[]{:S(2)}) copy-start(bf16[1024,768]{1,0:T(8,128)(2,1)S(1)} %get-tuple-element.149.refs_1_.refs_8_) | copy-start | bytes 4718596
  354.1 27.2 %copy-start.3 = (bf16[1024,384]{1,0:T(8,128)(2,1)}, bf16[1024,384]{1,0:T(8,128)(2,1)S(1)}, u32[]{:S(2)}) copy-start(bf16[1024,384]{1,0:T(8,128)(2,1)S(1)} %multiply_convert_fusion.5.refs_0_.refs_16_) | copy-start | bytes 2359300
  383.0 62.6 %copy-start.35 = (f32[768,16]{0,1:T(8,128)S(1)}, f32[768,16]{0,1:T(8,128)}, u32[]{:S(2)}) copy-start(f32[768,16]{0,1:T(8,128)} %fusion.110) | copy-start | bytes 147460
  383.0 62.6 %copy-start.41 = (f32[768,1]{0,1:T(1,128)S(1)}, f32[768,1]{0,1:T(1,128)}, u32[]{:S(2)}) copy-start(f32[768,1]{0,1:T(1,128)} %maximum_bitcast_fusion) | copy-start | bytes 9220
  383.0 66.4 %copy-start.32 = (f32[768,22]{0,1:T(8,128)S(1)}, f32[768,22]{0,1:T(8,128)}, u32[]{:S(2)}) copy-start(f32[768,22]{0,1:T(8,128)} %copy-done.31) | copy-start | bytes 202756
  444.6 9.7 %copy-start.30 = (bf16[768,80]{1,0:T(8,128)(2,1)S(1)}, bf16[768,80]{1,0:T(8,128)(2,1)}, u32[]{:S(2)}) copy-start(bf16[768,80]{1,0:T(8,128)(2,1)} %copy-done.29) | copy-start | bytes 368644
  444.6 8.6 %collective-permute-start.7 = (bf16[1024,128]{1,0:T(8,128)(2,1)}, bf16[1024,128]{1,0:T(8,128)(2,1)S(1)}, u32[]{:S(2)}, u32[]{:S(2)}) collective-permute-start(bf16[1024,128]{1,0:T(8,128)(2,1)} %get-tuple-element.64), channel_id=1, source_target_pairs={{0,1},{1,0},{2,3},{3,2},{4,5},{5,4},{6,7},{7,6},{8,9},{9,8},{10,11... | collective-permute-start | bytes 786440 | tf_op jit(solution)/shard_map/ppermute | solution.py:28
  454.2 4.4 copy-start.28
  455.5 3.2 collective-permute-start.8
  520.9 7.7 %copy-start.23 = (f32[2,4,128,768]{3,2,1,0:T(8,128)S(1)}, f32[2,4,128,768]{3,2,1,0:T(8,128)}, u32[]{:S(2)}) copy-start(f32[2,4,128,768]{3,2,1,0:T(8,128)} %get-tuple-element.185) | copy-start | bytes 9437188
  528.6 3.6 copy-start.36
  (21 other events, 38.8 us)
Sparse Core Ops, SparseCore 0:
  12.9 42.3 all-gather.2
  58.2 51.5 all-gather.4
  383.1 62.9 reduce-scatter.1

commit v6 on v5

--- a/solution.py
+++ b/solution.py
@@ -290,7 +290,7 @@
 
     zero = jnp.zeros((seqs, LANES), F32)
     hs, total = lax.fori_loop(
-        0, length, body, ((zero,) * (N * parts), jnp.zeros((seqs, width), F32)), unroll=4
+        0, length, body, ((zero,) * (N * parts), jnp.zeros((seqs, width), F32)), unroll=8
     )
     for n in range(N):
         for k in range(parts):
@@ -384,7 +384,7 @@
                 y_ref[row, lanes(k)] = ys[k]
             return tuple(new)
 
-        return lax.fori_loop(0, BLK, body, hs, unroll=4)
+        return lax.fori_loop(0, BLK, body, hs, unroll=8)
 
     hs = lax.fori_loop(
         0,
@@ -463,7 +463,7 @@
         return tuple(new)
 
     zero = jnp.zeros((seqs, LANES), F32)
-    gs = lax.fori_loop(0, length, body, (zero,) * (N * parts), unroll=4)
+    gs = lax.fori_loop(0, length, body, (zero,) * (N * parts), unroll=8)
     for n in range(N):
         for k in range(parts):
             g_ref[n, :, lanes(k)] = gs[n * parts + k]

time: 550 us -> 550 us (level)
  transfers between devices with their start and end apart: 19 -> 19, of which waited for: 12 -> 12; matrix products, arithmetic and copies ran while one was open for 18% -> 18% of each run, Pallas kernels for 18% -> 17%
where the time goes in v6:
time: 550 us; the launch traced here: 539 us
  Pallas kernels  251 us (46%)
  waiting for transfers between devices  86.7 us (16%)
  matrix products  68.4 us (12%)
  local copies, waits for them, and re-layouts  43.8 us (8%)
  starting transfers between devices  42.8 us (8%)
  other arithmetic  31.4 us (6%)
  between operations  15.3 us (3%)
    pallas_call x3, Pallas kernels, scan_call(): pl.pallas_call(kernel, grid=(chans // width,), in_specs=[spec(shape, kind...  94.1 us
    pallas_call x1, Pallas kernels, per_device(): pl.pallas_call(functools.partial(finish_kernel, (micros, group), sizes, t...  61.6 us
    pallas_call x2, Pallas kernels, carried(): pl.pallas_call(functools.partial(carry_kernel, sign, ranges, peers), in_s...  48.3 us
    pallas_call x1, Pallas kernels, per_device(): pl.pallas_call(functools.partial(forward_kernel, peers), grid=(pieces, gr...  46.6 us
    dot_general x8, matrix products, product(): return jnp.einsum(terms, a, b, preferred_element_type=F32)  36.8 us
    all_to_all x6, starting transfers between devices, swap_owners(): lax.all_to_all(value, OWNERS, split_axis=0, concat_axis=0, tiled=True)  30.7 us
    all_to_all x6, waiting for transfers between devices, swap_owners(): lax.all_to_all(value, OWNERS, split_axis=0, concat_axis=0, tiled=True)  28.7 us
    all_gather x1, waiting for transfers between devices, per_device(): full = lax.all_gather(first, OWNERS, axis=0, tiled=True)  27 us
  transfers between devices with their start and end apart: 19, of which 12 were waited for; matrix products, arithmetic and copies ran while one was open for 18% of the time, Pallas kernels for 17%

profile of v6, /device:TPU:0, one launch (start us, length us, event | category | flops | bytes accessed | tf_op | source)
XLA Modules:
  0.0 539.1 jit_solution(3094517033555365345)
XLA Ops:
  14.4 2.6 copy.81
  20.4 2.6 copy.83
  24.2 4.1 fusion.35
  28.3 27.0 %all-gather.3.cloned.1.call-done.refs_9_ = bf16[768,1024]{1,0:T(8,128)(2,1)} async-done(((bf16[48,1024]{1,0:T(8,128)(2,1)}), bf16[768,1024]{1,0:T(8,128)(2,1)}) %all-gather.3.cloned.1.call-update) | async-done | bytes 1572880 | tf_op jit(solution)/shard_map/all_gather | solution.py:977
  55.3 1.7 copy.82
  58.3 1.8 fusion.17.refs_2_.refs_4_
  61.6 2.2 collective-permute-start
  64.9 3.7 fusion.111
  72.5 6.4 %all-to-all-start = ((bf16[16,50,768]{2,1,0:T(8,128)(2,1)}), bf16[16,50,768]{2,1,0:T(8,128)(2,1)}, u32[]{:S(2)}, u32[]{:S(2)}) async-start(bf16[16,50,768]{2,1,0:T(8,128)(2,1)} %fusion.35), calls=%async_computation | async-start | bytes 2752512 | tf_op jit(solution)/shard_map/all_to_all | solution.py:1002
  81.4 6.0 %add_divide_fusion = (f32[1024,768]{1,0:T(8,128)}, f32[1024,768]{1,0:T(8,128)}) fusion(f32[768]{0:T(1024)S(1)} %convert_reduce_fusion, bf16[768,1024]{1,0:T(8,128)(2,1)} %all-gather.3.cloned.1.call-done.refs_9_, f32[1024,80]{1,0:T(8,128)S(1)} %convert_add_fusion), kind=kOutput, calls=%fused_computation.39 | convolution fusion | flops 83361792 | bytes 6754304 | tf_op jit(solution)/shard_map/dot_general | solution.py:80
  87.4 16.2 %shard_map.238 = f32[17,8,768]{2,1,0:T(8,128)} custom-call(f32[1024,768]{1,0:T(8,128)} %get-tuple-element.152.d_ref, f32[1024,768]{1,0:T(8,128)} %get-tuple-element.145.u_ref, f32[1024,16]{1,0:T(8,128)} %get-tuple-element.160.b_ref, f32[16,768]{1,0:T(8,128)} %fusion.91.r_ref), custom_call_target="tpu_custom_call" | custom-call | flops 22649241600 | bytes 12582912 | tf_op jit(solution)/shard_map/pallas_call | solution.py:921
  103.6 6.2 %all-gather.5.cloned.1.call-done.w_ref.refs_10_ = bf16[768,1536]{1,0:T(8,128)(2,1)} async-done(((bf16[48,1536]{1,0:T(8,128)(2,1)}), bf16[768,1536]{1,0:T(8,128)(2,1)}) %all-gather.5.cloned.1.call-update) | async-done | bytes 2359312 | tf_op jit(solution)/shard_map/all_gather | solution.py:978
  109.8 4.4 fusion.51.z_ref
  114.2 5.3 all-to-all-done
  119.6 22.5 %shard_map.239.h0_ref = f32[16,8,768]{2,1,0:T(8,128)S(1)} custom-call(f32[16,8,768]{2,1,0:T(8,128)S(1)} %slice.200.end_ref, f32[8,768]{1,0:T(8,128)S(1)} %slice_bitcast_fusion.3.log_ref, f32[16,768]{1,0:T(8,128)S(1)} %copy-done.5), custom_call_target="tpu_custom_call" | custom-call | flops 21474836480 | bytes 1048576 | tf_op jit(solution)/shard_map/pallas_call | solution.py:227
  142.9 46.6 %shard_map.240 = (f32[1024,768]{1,0:T(8,128)}, bf16[1024,768]{1,0:T(8,128)(2,1)}, f32[16,16,8,768]{3,2,1,0:T(8,128)}, f32[1024,768]{1,0:T(8,128)}) custom-call(f32[1024,768]{1,0:T(8,128)} %get-tuple-element.152.d_ref, f32[1024,768]{1,0:T(8,128)} %get-tuple-element.145.u_ref, f32[1024,768]{1,0:T(8,128)} %fusion.51.z_ref, ...), custom_call_target="tpu_custom_call" | custom-call | flops 37748736000 | bytes 12582912 | tf_op jit(solution)/shard_map/pallas_call | solution.py:1115
  189.5 2.3 multiply_reduce_fusion.1
  192.3 2.1 multiply_convert_fusion.2
  194.4 2.0 fusion.46
  196.4 3.6 all-to-all-start.2
  200.0 3.4 convert_multiply_fusion.2
  206.4 10.9 %all-to-all-done.2 = bf16[16,50,384]{2,1,0:T(8,128)(2,1)S(1)} async-done(((bf16[16,50,384]{2,1,0:T(8,128)(2,1)}), bf16[16,50,384]{2,1,0:T(8,128)(2,1)S(1)}, u32[]{:S(2)}, u32[]{:S(2)}) %all-to-all-start.2) | async-done | bytes 614432 | tf_op jit(solution)/shard_map/all_to_all | solution.py:1002
  217.3 4.4 all-to-all-start.1
  222.5 5.6 %all-to-all-done.1 = f32[16,1,50]{2,1,0:T(1,128)S(1)} async-done(((f32[16,1,50]{2,1,0:T(1,128)}), f32[16,1,50]{2,1,0:T(1,128)S(1)}, u32[]{:S(2)}, u32[]{:S(2)}) %all-to-all-start.1) | async-done | bytes 3232 | tf_op jit(solution)/shard_map/all_to_all | solution.py:1002
  228.1 4.6 fusion.24
  232.7 5.5 %collective-permute-done.2 = bf16[16,50,384]{2,0,1:T(8,128)(2,1)} collective-permute-done((bf16[16,50,384]{2,0,1:T(8,128)(2,1)S(1)}, bf16[16,50,384]{2,0,1:T(8,128)(2,1)}, u32[]{:S(2)}, u32[]{:S(2)}) %collective-permute-start.2) | collective-permute-done | bytes 614432 | tf_op jit(solution)/shard_map/ppermute | solution.py:28
  239.6 7.1 %multiply_reduce_fusion = (f32[16,50]{1,0:T(8,128)}, bf16[16,50,1536]{2,1,0:T(8,128)(2,1)S(1)}, bf16[16,50,1536]{2,1,0:T(8,128)(2,1)S(1)}) fusion(f32[16,50,1536]{2,1,0:T(8,128)S(1)} %fusion.24, bf16[1,768,1536]{2,1,0:T(8,128)(2,1)S(1)} %copy-done.44, bf16[16,50,384]{2,1,0:T(8,128)(2,1)S(1)} %get-tuple-element.158, ...), kind=kOutput, calls=%fused_computation.19 | convolution fusion | flops 1920613632 | bytes 13421696 | tf_op jit(solution)/shard_map/srd,df->srf/dot_general | solution.py:1161
  249.1 5.9 %convolution_bitcast_fusion = f32[1536,768]{1,0:T(8,128)} fusion(bf16[16,50,1536]{2,1,0:T(8,128)(2,1)S(1)} %get-tuple-element.52, bf16[16,50,768]{2,1,0:T(8,128)(2,1)} %all-to-all-done, f32[16,50]{1,0:T(8,128)S(1)} %bitcast.106), kind=kOutput, calls=%fused_computation.23 | convolution fusion | flops 1889280000 | bytes 8408192 | tf_op jit(solution)/shard_map/srf,srd->fd/dot_general | solution.py:1161
  255.0 5.7 %all-to-all-start.4 = ((f32[16,1,50]{2,1,0:T(1,128)}), f32[16,1,50]{2,1,0:T(1,128)S(1)}, u32[]{:S(2)}, u32[]{:S(2)}) async-start(f32[16,1,50]{2,1,0:T(1,128)} %bitcast.29), calls=%async_computation.4 | async-start | bytes 16384 | tf_op jit(solution)/shard_map/all_to_all | solution.py:1002
  260.8 4.2 convolution_convert_fusion.1
  267.4 3.6 add_convert_fusion.1
  270.9 6.3 %all-to-all-start.3 = ((bf16[16,50,384]{2,1,0:T(8,128)(2,1)}), bf16[16,50,384]{2,1,0:T(8,128)(2,1)}, u32[]{:S(2)}, u32[]{:S(2)}) async-start(bf16[16,50,384]{2,1,0:T(8,128)(2,1)} %add_convert_fusion.1), calls=%async_computation.3 | async-start | bytes 1376256 | tf_op jit(solution)/shard_map/all_to_all | solution.py:1002
  277.2 6.2 %convolution_bitcast_fusion.1 = f32[768,1536]{1,0:T(8,128)} fusion(bf16[16,50,1536]{2,1,0:T(8,128)(2,1)} %copy-done.24, bf16[16,50,384]{2,1,0:T(8,128)(2,1)S(1)} %copy-done.27, bf16[16,50,384]{2,1,0:T(8,128)(2,1)S(1)} %get-tuple-element.157), kind=kOutput, calls=%fused_computation.24 | convolution fusion | flops 1889894400 | bytes 8404992 | tf_op jit(solution)/shard_map/srd,srf->df/dot_general | solution.py:1161
  284.2 3.6 add_convert_fusion
  287.8 6.8 %all-to-all-done.3 = bf16[16,50,384]{2,1,0:T(8,128)(2,1)} async-done(((bf16[16,50,384]{2,1,0:T(8,128)(2,1)}), bf16[16,50,384]{2,1,0:T(8,128)(2,1)}, u32[]{:S(2)}, u32[]{:S(2)}) %all-to-all-start.3) | async-done | bytes 614432 | tf_op jit(solution)/shard_map/all_to_all | solution.py:1002
  294.6 2.7 fusion.40
  299.4 2.0 collective-permute-done.5
  309.9 11.8 %collective-permute-done.9 = f32[1,384]{1,0:T(1,128)S(1)} collective-permute-done((f32[1,384]{1,0:T(1,128)S(1)}, f32[1,384]{1,0:T(1,128)S(1)}, u32[]{:S(2)}, u32[]{:S(2)}) %collective-permute-start.9) | collective-permute-done | bytes 1568 | tf_op jit(solution)/shard_map/ppermute | solution.py:28
  322.5 4.3 all-to-all-start.5
  327.2 2.8 fusion.49
  330.3 3.3 multiply_convert_fusion.1
  333.7 16.4 %shard_map.241.end_ref = f32[16,8,768]{2,1,0:T(8,128)} custom-call(f32[1024,768]{1,0:T(8,128)} %get-tuple-element.152.d_ref, f32[1024,768]{1,0:T(8,128)} %get-tuple-element.150.dy_ref, f32[1024,16]{1,0:T(8,128)} %get-tuple-element.159.c_ref, f32[16,768]{1,0:T(8,128)} %fusion.91.r_ref), custom_call_target="tpu_custom_call" | custom-call | flops 22649241600 | bytes 12582912 | tf_op jit(solution)/shard_map/pallas_call | solution.py:921
  350.1 2.7 fusion.43
  354.6 25.8 %shard_map.242 = (f32[16,8,768]{2,1,0:T(8,128)S(1)}, bf16[1,1024,384]{2,1,0:T(8,128)(2,1)S(1)}, bf16[768,1536]{1,0:T(8,128)(2,1)}) custom-call(f32[16,8,768]{2,1,0:T(8,128)S(1)} %copy-done.8, f32[8,768]{1,0:T(8,128)S(1)} %slice_bitcast_fusion.3.log_ref, f32[16,768]{1,0:T(8,128)S(1)} %copy-done.6, ...), custom_call_target="tpu_custom_call" | custom-call | flops 21474836480 | bytes 1048576 | tf_op jit(solution)/shard_map/pallas_call | solution.py:227
  382.2 61.6 %shard_map.243 = (bf16[1024,768]{1,0:T(8,128)(2,1)}, f32[1024,768]{1,0:T(8,128)}, bf16[1024,128]{1,0:T(8,128)(2,1)}, f32[16,8,768]{2,1,0:T(8,128)}, f32[8,768]{1,0:T(8,128)}, /*index=5*/f32[8,768]{1,0:T(8,128)}) custom-call(f32[1024,768]{1,0:T(8,128)} %get-tuple-element.152.d_ref, f32[1024,768]{1,0:T(8,128)} %get-tuple-element.145.u_ref, ...), custom_call_target="tpu_custom_call" | custom-call | flops 90596966400 | bytes 12582912 | tf_op jit(solution)/shard_map/pallas_call | solution.py:921
  448.5 3.8 collective-permute-done.7
  458.5 61.6 %shard_map.244 = (f32[2,4,128,768]{3,2,1,0:T(8,128)}, bf16[2,4,128,768]{3,2,1,0:T(8,128)(2,1)}, f32[2,48,768]{2,1,0:T(8,128)}, f32[48,768]{1,0:T(8,128)}, f32[48...) custom-call(f32[1024,768]{1,0:T(8,128)} %get-tuple-element.63.refs_0_, ...), custom_call_target="tpu_custom_call" | custom-call | tf_op jit(solution)/shard_map/pallas_call | solution.py:1355
  525.1 2.7 copy.107
  (218 shorter events, 68.9 us)
Async XLA Ops:
  7.2 48.1 %all-gather.3.cloned.1.call-start = ((), (), s32[]{:S(2)}) async-start(), calls=%async_computation.7 | async-start | bytes 1671168 | tf_op jit(solution)/shard_map/all_gather | solution.py:977
  12.7 97.1 %all-gather.5.cloned.1.call-start = ((), (), s32[]{:S(2)}) async-start(), calls=%async_computation.8 | async-start | bytes 2506752 | tf_op jit(solution)/shard_map/all_gather | solution.py:978
  23.5 4.9 copy-start.13
  57.0 3.1 copy-start.16
  57.1 14.8 %copy-start.31 = (f32[768,22]{0,1:T(8,128)}, f32[768,22]{0,1:T(8,128)S(1)}, u32[]{:S(2)}) copy-start(f32[768,22]{0,1:T(8,128)S(1)} %slice_convert_fusion.1) | copy-start | bytes 202756
  57.1 6.7 %copy-start.37 = (f32[4,768]{1,0:T(4,128)}, f32[4,768]{1,0:T(4,128)S(1)}, u32[]{:S(2)}) copy-start(f32[4,768]{1,0:T(4,128)S(1)} %slice_bitcast_fusion.4.refs_12_) | copy-start | bytes 36868
  60.1 49.7 %copy-start.1 = (bf16[1024,768]{1,0:T(8,128)(2,1)}, bf16[1024,768]{1,0:T(8,128)(2,1)S(1)}, u32[]{:S(2)}) copy-start(bf16[1024,768]{1,0:T(8,128)(2,1)S(1)} %fusion.17.refs_2_.refs_4_) | copy-start | bytes 4718596
  61.6 3.0 collective-permute-start
  64.8 3.7 copy-start.10
  70.3 9.7 %collective-permute-start.1 = (bf16[1024,80]{1,0:T(8,128)(2,1)S(1)}, bf16[1024,80]{1,0:T(8,128)(2,1)S(1)}, u32[]{:S(2)}, u32[]{:S(2)}) collective-permute-start(bf16[1024,80]{1,0:T(8,128)(2,1)S(1)} %convolution_convert_fusion.3), channel_id=1, source_target_pairs={{0,1},{1,0},{2,3},{3,2},{4,5},{5,4},{6,7},{7,6},{8,9},{9,8},{10,11... | collective-permute-start | bytes 491528 | tf_op jit(solution)/shard_map/ppermute | solution.py:28
  72.5 47.1 %all-to-all-start = ((bf16[16,50,768]{2,1,0:T(8,128)(2,1)}), bf16[16,50,768]{2,1,0:T(8,128)(2,1)}, u32[]{:S(2)}, u32[]{:S(2)}) async-start(bf16[16,50,768]{2,1,0:T(8,128)(2,1)} %fusion.35), calls=%async_computation | async-start | bytes 2752512 | tf_op jit(solution)/shard_map/all_to_all | solution.py:1002
  80.1 7.3 %copy-start.18 = (f32[1024,80]{1,0:T(8,128)}, f32[1024,80]{1,0:T(8,128)S(1)}, u32[]{:S(2)}) copy-start(f32[1024,80]{1,0:T(8,128)S(1)} %convert_add_fusion) | copy-start | bytes 983044
  103.6 16.0 %copy-start.33 = (f32[17,8,768]{2,1,0:T(8,128)S(1)}, f32[17,8,768]{2,1,0:T(8,128)}, u32[]{:S(2)}) copy-start(f32[17,8,768]{2,1,0:T(8,128)} %shard_map.238) | copy-start | bytes 1253380
  103.6 16.0 %copy-start.5 = (f32[16,768]{1,0:T(8,128)S(1)}, f32[16,768]{1,0:T(8,128)}, u32[]{:S(2)}) copy-start(f32[16,768]{1,0:T(8,128)} %fusion.91.r_ref) | copy-start | bytes 147460
  196.4 20.9 %all-to-all-start.2 = ((bf16[16,50,384]{2,1,0:T(8,128)(2,1)}), bf16[16,50,384]{2,1,0:T(8,128)(2,1)S(1)}, u32[]{:S(2)}, u32[]{:S(2)}) async-start(bf16[16,50,384]{2,1,0:T(8,128)(2,1)} %fusion.46), calls=%async_computation.2 | async-start | bytes 1376256 | tf_op jit(solution)/shard_map/all_to_all | solution.py:1002
  217.3 10.8 %all-to-all-start.1 = ((f32[16,1,50]{2,1,0:T(1,128)}), f32[16,1,50]{2,1,0:T(1,128)S(1)}, u32[]{:S(2)}, u32[]{:S(2)}) async-start(f32[16,1,50]{2,1,0:T(1,128)} %bitcast.13), calls=%async_computation.1 | async-start | bytes 16384 | tf_op jit(solution)/shard_map/all_to_all | solution.py:1002
  221.9 16.4 %collective-permute-start.2 = (bf16[16,50,384]{2,0,1:T(8,128)(2,1)S(1)}, bf16[16,50,384]{2,0,1:T(8,128)(2,1)}, u32[]{:S(2)}, u32[]{:S(2)}) collective-permute-start(bf16[16,50,384]{2,0,1:T(8,128)(2,1)S(1)} %copy.86), channel_id=1, source_target_pairs={{0,1},{1,0},{2,3},{3,2},{4,5},{5,4},{6,7},{7,6},{8,9},{9,8},{10,11... | collective-permute-start | bytes 1843208 | tf_op jit(solution)/shard_map/ppermute | solution.py:28
  228.1 11.5 %copy-start.44 = (bf16[1,768,1536]{2,1,0:T(8,128)(2,1)S(1)}, bf16[1,768,1536]{2,1,0:T(8,128)(2,1)}, u32[]{:S(2)}) copy-start(bf16[1,768,1536]{2,1,0:T(8,128)(2,1)} %param.28) | copy-start | bytes 7077892
  239.6 7.2 %copy-start.26 = (bf16[16,50,384]{2,1,0:T(8,128)(2,1)}, bf16[16,50,384]{2,1,0:T(8,128)(2,1)S(1)}, u32[]{:S(2)}) copy-start(bf16[16,50,384]{2,1,0:T(8,128)(2,1)S(1)} %get-tuple-element.158) | copy-start | bytes 1843204
  248.5 16.5 %collective-permute-start.3 = (bf16[16,50,384]{2,0,1:T(8,128)(2,1)S(1)}, bf16[16,50,384]{2,0,1:T(8,128)(2,1)}, u32[]{:S(2)}, u32[]{:S(2)}) collective-permute-start(bf16[16,50,384]{2,0,1:T(8,128)(2,1)S(1)} %copy.89), channel_id=1, source_target_pairs={{0,1},{1,0},{2,3},{3,2},{4,5},{5,4},{6,7},{7,6},{8,9},{9,8},{10,11... | collective-permute-start | bytes 1843208 | tf_op jit(solution)/shard_map/ppermute | solution.py:28
  255.0 15.9 %all-to-all-start.4 = ((f32[16,1,50]{2,1,0:T(1,128)}), f32[16,1,50]{2,1,0:T(1,128)S(1)}, u32[]{:S(2)}, u32[]{:S(2)}) async-start(f32[16,1,50]{2,1,0:T(1,128)} %bitcast.29), calls=%async_computation.4 | async-start | bytes 16384 | tf_op jit(solution)/shard_map/all_to_all | solution.py:1002
  260.7 6.6 %copy-start.25 = (bf16[16,50,1536]{2,1,0:T(8,128)(2,1)S(1)}, bf16[16,50,1536]{2,1,0:T(8,128)(2,1)}, u32[]{:S(2)}) copy-start(bf16[16,50,1536]{2,1,0:T(8,128)(2,1)} %copy-done.24) | copy-start | bytes 7372804
  260.7 6.6 %copy-start.45 = (bf16[1,768,1536]{2,1,0:T(8,128)(2,1)S(1)}, bf16[1,768,1536]{2,1,0:T(8,128)(2,1)}, u32[]{:S(2)}) copy-start(bf16[1,768,1536]{2,1,0:T(8,128)(2,1)} %param.28) | copy-start | bytes 7077892
  265.9 11.3 %copy-start.27 = (bf16[16,50,384]{2,1,0:T(8,128)(2,1)S(1)}, bf16[16,50,384]{2,1,0:T(8,128)(2,1)}, u32[]{:S(2)}) copy-start(bf16[16,50,384]{2,1,0:T(8,128)(2,1)} %copy-done.26) | copy-start | bytes 1843204
  265.9 18.3 %collective-permute-start.4 = (bf16[16,50,384]{2,0,1:T(8,128)(2,1)}, bf16[16,50,384]{2,0,1:T(8,128)(2,1)}, u32[]{:S(2)}, u32[]{:S(2)}) collective-permute-start(bf16[16,50,384]{2,0,1:T(8,128)(2,1)} %copy.91), channel_id=1, source_target_pairs={{0,1},{1,0},{2,3},{3,2},{4,5},{5,4},{6,7},{7,6},{8,9},{9,8},{10,11... | collective-permute-start | bytes 1843208 | tf_op jit(solution)/shard_map/ppermute | solution.py:28
  270.9 23.7 %all-to-all-start.3 = ((bf16[16,50,384]{2,1,0:T(8,128)(2,1)}), bf16[16,50,384]{2,1,0:T(8,128)(2,1)}, u32[]{:S(2)}, u32[]{:S(2)}) async-start(bf16[16,50,384]{2,1,0:T(8,128)(2,1)} %add_convert_fusion.1), calls=%async_computation.3 | async-start | bytes 1376256 | tf_op jit(solution)/shard_map/all_to_all | solution.py:1002
  277.2 7.0 %copy-start.46 = (bf16[1,1536,768]{2,1,0:T(8,128)(2,1)S(1)}, bf16[1,1536,768]{2,1,0:T(8,128)(2,1)}, u32[]{:S(2)}) copy-start(bf16[1,1536,768]{2,1,0:T(8,128)(2,1)} %param.29) | copy-start | bytes 7077892
  277.2 6.9 %copy-start.49 = (bf16[16,50,1536]{2,1,0:T(8,128)(2,1)S(1)}, bf16[16,50,1536]{2,1,0:T(8,128)(2,1)}, u32[]{:S(2)}) copy-start(bf16[16,50,1536]{2,1,0:T(8,128)(2,1)} %copy-done.48) | copy-start | bytes 7372804
  297.4 4.1 copy-start.17
  297.7 3.7 collective-permute-start.5
  301.5 5.0 copy-start.19
  302.5 19.8 %collective-permute-start.6 = (bf16[1024,384]{1,0:T(8,128)(2,1)S(1)}, bf16[1024,384]{1,0:T(8,128)(2,1)S(1)}, u32[]{:S(2)}, u32[]{:S(2)}) collective-permute-start(bf16[1024,384]{1,0:T(8,128)(2,1)S(1)} %get-tuple-element.154), channel_id=1, source_target_pairs={{0,1},{1,0},{2,3},{3,2},{4,5},{5,4},{6,7},{7,6},{8,9},{9,8},{10,11... | collective-permute-start | bytes 2359304 | tf_op jit(solution)/shard_map/ppermute | solution.py:28
  307.5 14.2 %collective-permute-start.9 = (f32[1,384]{1,0:T(1,128)S(1)}, f32[1,384]{1,0:T(1,128)S(1)}, u32[]{:S(2)}, u32[]{:S(2)}) collective-permute-start(f32[1,384]{1,0:T(1,128)S(1)} %broadcast_in_dim.68), channel_id=1, source_target_pairs={{0,1},{1,0},{2,3},{3,2},{4,5},{5,4},{6,7},{7,6},{8,9},{9,8},{10,11... | collective-permute-start | bytes 4616 | tf_op jit(solution)/shard_map/ppermute | solution.py:28
  322.5 7.5 %copy-start.20 = (bf16[1024,768]{1,0:T(8,128)(2,1)}, bf16[1024,768]{1,0:T(8,128)(2,1)S(1)}, u32[]{:S(2)}) copy-start(bf16[1024,768]{1,0:T(8,128)(2,1)S(1)} %pad_maximum_fusion.refs_4_.refs_15_) | copy-start | bytes 4718596
  322.5 27.5 %all-to-all-start.5 = ((bf16[16,50,384]{2,1,0:T(8,128)(2,1)}), bf16[16,50,384]{2,1,0:T(8,128)(2,1)}, u32[]{:S(2)}, u32[]{:S(2)}) async-start(bf16[16,50,384]{2,1,0:T(8,128)(2,1)} %add_convert_fusion), calls=%async_computation.5 | async-start | bytes 1376256 | tf_op jit(solution)/shard_map/all_to_all | solution.py:1002
  326.8 131.0 %reduce-scatter.2.cloned.1.call-start = ((), (), s32[]{:S(2)}) async-start(), calls=%async_computation.9 | async-start | bytes 2506752 | tf_op jit(solution)/shard_map/reduce_scatter | solution.py:1232
  327.1 3.2 copy-start.22
  333.7 19.6 %copy-start = (bf16[1024,768]{1,0:T(8,128)(2,1)}, bf16[1024,768]{1,0:T(8,128)(2,1)S(1)}, u32[]{:S(2)}) copy-start(bf16[1024,768]{1,0:T(8,128)(2,1)S(1)} %get-tuple-element.149.refs_1_.refs_8_) | copy-start | bytes 4718596
  353.2 27.2 %copy-start.3 = (bf16[1024,384]{1,0:T(8,128)(2,1)}, bf16[1024,384]{1,0:T(8,128)(2,1)S(1)}, u32[]{:S(2)}) copy-start(bf16[1024,384]{1,0:T(8,128)(2,1)S(1)} %multiply_convert_fusion.5.refs_0_.refs_16_) | copy-start | bytes 2359300
  382.1 62.6 %copy-start.35 = (f32[768,16]{0,1:T(8,128)S(1)}, f32[768,16]{0,1:T(8,128)}, u32[]{:S(2)}) copy-start(f32[768,16]{0,1:T(8,128)} %fusion.110) | copy-start | bytes 147460
  382.1 62.6 %copy-start.41 = (f32[768,1]{0,1:T(1,128)S(1)}, f32[768,1]{0,1:T(1,128)}, u32[]{:S(2)}) copy-start(f32[768,1]{0,1:T(1,128)} %maximum_bitcast_fusion) | copy-start | bytes 9220
  382.2 66.3 %copy-start.32 = (f32[768,22]{0,1:T(8,128)S(1)}, f32[768,22]{0,1:T(8,128)}, u32[]{:S(2)}) copy-start(f32[768,22]{0,1:T(8,128)} %copy-done.31) | copy-start | bytes 202756
  443.7 9.7 %copy-start.30 = (bf16[768,80]{1,0:T(8,128)(2,1)S(1)}, bf16[768,80]{1,0:T(8,128)(2,1)}, u32[]{:S(2)}) copy-start(bf16[768,80]{1,0:T(8,128)(2,1)} %copy-done.29) | copy-start | bytes 368644
  443.8 8.6 %collective-permute-start.7 = (bf16[1024,128]{1,0:T(8,128)(2,1)}, bf16[1024,128]{1,0:T(8,128)(2,1)S(1)}, u32[]{:S(2)}, u32[]{:S(2)}) collective-permute-start(bf16[1024,128]{1,0:T(8,128)(2,1)} %get-tuple-element.64), channel_id=1, source_target_pairs={{0,1},{1,0},{2,3},{3,2},{4,5},{5,4},{6,7},{7,6},{8,9},{9,8},{10,11... | collective-permute-start | bytes 786440 | tf_op jit(solution)/shard_map/ppermute | solution.py:28
  453.4 4.4 copy-start.28
  454.7 3.2 collective-permute-start.8
  520.1 7.7 %copy-start.23 = (f32[2,4,128,768]{3,2,1,0:T(8,128)S(1)}, f32[2,4,128,768]{3,2,1,0:T(8,128)}, u32[]{:S(2)}) copy-start(f32[2,4,128,768]{3,2,1,0:T(8,128)} %get-tuple-element.185) | copy-start | bytes 9437188
  527.8 3.6 copy-start.36
  (21 other events, 38.8 us)
Sparse Core Ops, SparseCore 0:
  12.9 42.3 all-gather.2
  58.2 51.5 all-gather.4
  382.3 62.9 reduce-scatter.1
